TPU v7x, 256 devices: a whole 4x4x8 slice. The times are simulated.
256 devices in a mesh: seq: 8 (over x, core), fsdp: 32 (over y, z).
Axes of the slice: x: 4, y: 4, z: 8, core: 2. Of those that a mesh axis runs over, the one named last changes fastest.
Arguments:
- queries: bfloat16 [32, 1024, 32, 128], P('fsdp', 'seq'), may hold values from -6 to 6
- keys: bfloat16 [32, 1024, 4, 128], P('fsdp', 'seq'), may hold values from -6 to 6
- values: bfloat16 [32, 1024, 4, 128], P('fsdp', 'seq'), may hold values from -6 to 6
- attn_out: bfloat16 [32, 1024, 32, 128], P('fsdp', 'seq'), may hold values from -6 to 6
- out_grad: bfloat16 [32, 1024, 5120], P('fsdp', 'seq'), may hold values from -6 to 6
- out_weight: bfloat16 [4096, 5120], P(('seq', 'fsdp')), may hold values from -0.09375 to 0.09375
- lengths: int32 [32, 3], P('fsdp'), may hold values from 1 to 512, 1024 in all within a row
Outputs:
- grad_queries: bfloat16 [32, 1024, 32, 128], P('fsdp', 'seq')
- grad_keys: bfloat16 [32, 1024, 4, 128], P('fsdp', 'seq')
- grad_values: bfloat16 [32, 1024, 4, 128], P('fsdp', 'seq')
- grad_out_weight: float32 [4096, 5120], P(('seq', 'fsdp'))
Inputs may be any that keep to these rules, and one draw needn't show every extreme that they name: The 3 lengths of a pack sum to 1024; the longest has exactly 512 tokens.
All inputs are finite; a program needn't handle non-finite values.
Results may differ from a plain program's by a relative error of at most 0.02.
Values may be sent and summed in bfloat16 or wider, within the bound.
No kernel may reach another device: no remote copies, remote signals or barrier semaphores. Data moves between devices by JAX's collectives and lax.ppermute only.
A program may use at most 128 MiB of HBM per device.

v0:
```python
import functools
import math

import jax
import jax.numpy as jnp
from jax import lax
from jax.experimental import pallas as pl
from jax.experimental.pallas import tpu as pltpu
from jax.sharding import Mesh
from jax.sharding import PartitionSpec as P

TOK = 128
QB = 256
WIDTHS = (1280, 1280)
PIECES = 2
F32 = jnp.float32
BF16 = jnp.bfloat16
VMEM = 56 * 1024 * 1024


def params():
    return pltpu.CompilerParams(vmem_limit_bytes=VMEM)


def shift(value, axis, by):
    size = lax.axis_size(axis)
    return lax.ppermute(value, axis, [(i, (i + by) % size) for i in range(size)])


def after(value, *others):
    return lax.optimization_barrier((value, *others))[0]


def swap(value):
    return lax.ppermute(value, "core", [(0, 1), (1, 0)])


def weight_kernel(factor, info, own, prev, succ, far0, far1, o_own, o_sib, *outs):
    *terms, rows = outs
    here = info[0]

    def put(chip, rc, value):
        rows[pl.ds(pl.multiple_of(rc * 512 + chip * TOK, TOK), TOK), :] = value

    for rc in range(2):
        part = slice(rc * TOK, (rc + 1) * TOK)
        put(here, rc, own[part, :])
        put(lax.rem(here + 3, 4), rc, prev[part, :])
        put(lax.rem(here + 1, 4), rc, succ[part, :])
    put(lax.rem(here + 2, 4), 0, far0[...])
    put(lax.rem(here + 2, 4), 1, far1[...])
    y = info[1]
    low = rows[:512, :]
    high = rows[512:, :]
    for kk in range(2):
        for part in range(2):
            cols = slice(kk * 512 + part * 256, kk * 512 + part * 256 + 256)
            dims = (((0,), (0,)), ((), ()))
            term = lax.dot_general(o_own[:, cols], low, dims, preferred_element_type=F32)
            term += lax.dot_general(o_sib[:, cols], high, dims, preferred_element_type=F32)
            term = (term * factor).astype(BF16)
            for at in range(16):
                f = part * 16 + at
                ry = lax.rem(f // 8 - y + 4, 4)
                terms[0][f % 8, ry, kk] = term[at * 16 : at * 16 + 16, :]


def weight_piece(info, parts, o_own, o_sib, factor):
    width = parts[0].shape[1]
    whole = pl.BlockSpec(memory_space=pltpu.VMEM)
    return pl.pallas_call(
        functools.partial(weight_kernel, factor),
        out_shape=(
            jax.ShapeDtypeStruct((8, 4, 2, 16, width), BF16),
            jax.ShapeDtypeStruct((1024, width), BF16),
        ),
        in_specs=[pl.BlockSpec(memory_space=pltpu.SMEM)] + [whole] * 7,
        out_specs=(whole, whole),
        compiler_params=params(),
        cost_estimate=pl.CostEstimate(
            flops=2 * 1024 * 1024 * width, bytes_accessed=12 * 1024 * 1024, transcendentals=0
        ),
    )(info, *parts, o_own, o_sib)


def project_kernel(info, *refs):
    first, last, near, prev, succ, far0, far1, out, weight = refs
    rows = (first, last)
    y, core = info[1], info[3]

    def put(from_y, at, value):
        row = lax.rem(from_y, 4) * 128 + at
        count = value.shape[0] * 16
        weight[pl.ds(pl.multiple_of(row, 64), count), :] = value.reshape(count, 2560)

    put(y, 0, near[...])
    put(y + 3, 0, prev[...])
    put(y + 1, 0, succ[...])
    put(y + 2, 0, far0[...])
    put(y + 2, 64, far1[...])
    for part in range(2):
        block = slice(part * 256, part * 256 + 256)
        total = None
        begin = 0
        for piece in rows:
            width = piece.shape[1]
            term = lax.dot_general(
                piece[...],
                weight[block, begin : begin + width],
                (((1,), (1,)), ((), ())),
                preferred_element_type=F32,
            )
            total = term if total is None else total + term
            begin += width
        total = total.astype(out.dtype)
        for rc in range(2):
            for chip in range(4):
                at = rc * 512 + chip * TOK
                spot = chip * 256 + (core if rc == 0 else 1 - core) * TOK
                out[pl.ds(pl.multiple_of(spot, TOK), TOK), block] = total[at : at + TOK, :]


def project(info, pieces, parts, rc, dtype):
    far = pl.BlockSpec((None, 4, 16, 2560), lambda n, info: (rc, 0, 0, 0))
    grid_spec = pltpu.PrefetchScalarGridSpec(
        num_scalar_prefetch=1,
        grid=(1,),
        in_specs=[pl.BlockSpec(p.shape, lambda n, info: (0, 0)) for p in pieces]
        + [pl.BlockSpec((8, 16, 2560), lambda n, info: (0, 0, 0))] * 3
        + [far, far],
        out_specs=pl.BlockSpec((1024, 512), lambda n, info: (0, 0)),
        scratch_shapes=[pltpu.VMEM((512, 2560), BF16)],
    )
    return pl.pallas_call(
        project_kernel,
        out_shape=jax.ShapeDtypeStruct((1024, 512), dtype),
        grid_spec=grid_spec,
        compiler_params=params(),
        cost_estimate=pl.CostEstimate(
            flops=2 * 1024 * 512 * 2560, bytes_accessed=10 * 1024 * 1024, transcendentals=0
        ),
    )(info, *pieces, *parts)


def attention_kernel(info, query, key, value, mine, theirs, o_own, o_sib, out, key_acc, value_acc):
    head = pl.program_id(0)
    core = info[3]
    ends = (info[4], info[4] + info[5], info[4] + info[5] + info[6])
    scale = 128 ** (-0.5)

    @pl.when(head == 0)
    def _():
        key_acc[...] = jnp.zeros_like(key_acc)
        value_acc[...] = jnp.zeros_like(value_acc)

    for block in range(4):
        at = block * QB
        begin = max(0, at - 512)
        span = at + QB - begin
        rows = slice(at, at + QB)
        cols = slice(begin, at + QB)
        q = query[rows, :]
        k = key[cols, :]
        v = value[cols, :]
        grad = (mine[rows, :].astype(F32) + theirs[rows, :].astype(F32)).astype(BF16)
        near = o_own[block * TOK : block * TOK + TOK, :].astype(F32)
        other = o_sib[block * TOK : block * TOK + TOK, :].astype(F32)
        saved = jnp.concatenate(
            [jnp.where(core == 0, near, other), jnp.where(core == 0, other, near)], axis=0
        )
        delta = jnp.sum((grad.astype(F32) * saved).T, axis=0, keepdims=True)
        i = at + lax.broadcasted_iota(jnp.int32, (1, QB), 1)
        start = jnp.zeros_like(i)
        for end in ends:
            start = jnp.where(i >= end, end, start)
        j = begin + lax.broadcasted_iota(jnp.int32, (span, QB), 0)
        scores = lax.dot_general(k, q, (((1,), (1,)), ((), ())), preferred_element_type=F32)
        scores = scores * (scale * math.log2(math.e))
        scores = jnp.where((j <= i) & (j >= start), scores, -1e30)
        top = jnp.max(scores, axis=0, keepdims=True)
        raised = jnp.exp2(scores - top)
        soft = raised * (1.0 / jnp.sum(raised, axis=0, keepdims=True))
        value_acc[cols, :] += jnp.dot(soft.astype(BF16), grad, preferred_element_type=F32)
        grad_soft = lax.dot_general(v, grad, (((1,), (1,)), ((), ())), preferred_element_type=F32)
        grad_scores = (soft * (grad_soft - delta) * scale).astype(BF16)
        key_acc[cols, :] += jnp.dot(grad_scores, q, preferred_element_type=F32)
        grad_query = lax.dot_general(
            grad_scores, k, (((0,), (0,)), ((), ())), preferred_element_type=F32
        )
        out[rows, pl.ds(pl.multiple_of(head * 128, 128), 128)] = grad_query.astype(BF16)

    @pl.when(head == 3)
    def _():
        out[:, 512:640] = key_acc[...].astype(BF16)
        out[:, 640:768] = value_acc[...].astype(BF16)


def attention(info, packed, mine, theirs, o_own, o_sib):
    grid_spec = pltpu.PrefetchScalarGridSpec(
        num_scalar_prefetch=1,
        grid=(4,),
        in_specs=[
            pl.BlockSpec((1024, 128), lambda h, info: (0, h)),
            pl.BlockSpec((1024, 128), lambda h, info: (0, 4)),
            pl.BlockSpec((1024, 128), lambda h, info: (0, 5)),
            pl.BlockSpec((1024, 128), lambda h, info: (0, h)),
            pl.BlockSpec((1024, 128), lambda h, info: (0, h)),
            pl.BlockSpec((512, 128), lambda h, info: (0, info[3] * 4 + h)),
            pl.BlockSpec((512, 128), lambda h, info: (0, info[3] * 4 + h)),
        ],
        out_specs=pl.BlockSpec((1024, 768), lambda h, info: (0, 0)),
        scratch_shapes=[pltpu.VMEM((1024, 128), F32), pltpu.VMEM((1024, 128), F32)],
    )
    return pl.pallas_call(
        attention_kernel,
        out_shape=jax.ShapeDtypeStruct((1024, 768), BF16),
        grid_spec=grid_spec,
        compiler_params=params(),
        cost_estimate=pl.CostEstimate(
            flops=4 * 10 * 256 * 256 * 128 * 10,
            bytes_accessed=8 * 1024 * 1024,
            transcendentals=4 * 10 * 256 * 256,
        ),
    )(info, packed, packed, packed, mine, theirs, o_own, o_sib)


def add(*terms):
    total = terms[0].astype(F32)
    for term in terms[1:]:
        total = total + term.astype(F32)
    return total


def per_device(queries, keys, values, attn_out, out_grad, out_weight, lengths):
    x, core, y, z = (lax.axis_index(name) for name in ("x", "core", "y", "z"))
    info = jnp.stack([x, y, z, core]).astype(jnp.int32)
    info = jnp.concatenate([info, lengths[0]])
    factor = 32768 ** (-0.5)

    def halves(value):
        left, right = value[:, :2560], value[:, 2560:]
        return jnp.where(core == 0, left, right), jnp.where(core == 0, right, left)

    weight_mine, weight_theirs = halves(out_weight)
    weight_pair = jnp.stack([weight_mine, swap(weight_theirs)])
    gathered = lax.all_gather(weight_pair, "z", axis=0, tiled=False)

    o_split = jnp.transpose(attn_out.reshape(TOK, 4, 1024), (1, 0, 2))
    o_own = lax.all_to_all(o_split, "x", split_axis=0, concat_axis=0, tiled=True)
    o_own = o_own.reshape(512, 1024)
    o_sib = swap(o_own)

    grad_mine, grad_theirs = halves(out_grad[0])
    grad_chip = jnp.concatenate([grad_mine, swap(grad_theirs)], axis=0)
    packed = jnp.concatenate(
        [
            queries.reshape(TOK, 8, 512),
            jnp.repeat(keys[0], 2, axis=1),
            jnp.repeat(values[0], 2, axis=1),
        ],
        axis=2,
    )
    packed = jnp.transpose(packed, (1, 0, 2))

    first_own, last_own = grad_chip[:, : WIDTHS[0]], grad_chip[:, WIDTHS[0] :]

    def weigh(parts):
        return weight_piece(info, parts, o_own, o_sib, factor)

    first_own = after(first_own, weight_pair)
    prev, succ = shift(first_own, "x", 1), shift(first_own, "x", -1)
    near0, near1 = gathered[:, 0], gathered[:, 1]
    prev1, succ1 = shift(near1, "y", 1), shift(near1, "y", -1)
    prev, succ, packed, near0 = lax.optimization_barrier((prev, succ, packed, near0))
    far0, far1 = shift(prev[:TOK], "x", 1), shift(succ[TOK:], "x", -1)
    far0, far1, prev1, succ1, last_own, near0 = lax.optimization_barrier(
        (far0, far1, prev1, succ1, last_own, near0)
    )
    first_term, first_rows = weigh((first_own, prev, succ, far0, far1))
    prev, succ = shift(last_own, "x", 1), shift(last_own, "x", -1)
    prev0, succ0 = shift(near0, "y", 1), shift(near0, "y", -1)
    prev, succ, packed, first_term, prev0, succ0 = lax.optimization_barrier(
        (prev, succ, packed, first_term, prev0, succ0)
    )
    packed = lax.all_to_all(packed, ("x", "core"), split_axis=0, concat_axis=0, tiled=True)
    packed = packed.reshape(1024, 768)
    far0, far1 = shift(prev[:TOK], "x", 1), shift(succ[TOK:], "x", -1)
    weight_far0 = shift(jnp.stack([prev0[:4], prev1[:4]]), "y", 1)
    weight_far1 = shift(jnp.stack([succ0[4:], succ1[4:]]), "y", -1)
    last_term, last_rows = weigh((last_own, prev, succ, far0, far1))
    pieces = (first_rows, last_rows)

    summed = [
        lax.psum_scatter(term, "z", scatter_dimension=0, tiled=True)[0]
        for term in (first_term, last_term)
    ]

    sibling_part = project(info, pieces, (near1, prev1, succ1, weight_far0, weight_far1), 1, BF16)
    theirs = swap(sibling_part)
    mine = project(info, pieces, (near0, prev0, succ0, weight_far0, weight_far1), 0, F32)
    grads = attention(info, packed, mine, theirs, o_own, o_sib)

    summed = after(jnp.concatenate(summed, axis=-1), grads)
    summed = add(summed[0], *(shift(summed[r], "y", r) for r in (1, 2, 3)))
    keep = jnp.where(core == 0, summed[0], summed[1])
    give = jnp.where(core == 0, summed[1], summed[0])
    come = swap(give)
    grad_out_weight = jnp.concatenate(
        [jnp.where(core == 0, keep, come), jnp.where(core == 0, come, keep)], axis=-1
    ).astype(F32)

    back = lax.all_to_all(
        grads.reshape(8, TOK, 768), ("x", "core"), split_axis=0, concat_axis=0, tiled=True
    )
    grad_queries = jnp.transpose(back[:, :, :512], (1, 0, 2)).reshape(1, TOK, 32, 128)

    def pair_sum(part):
        part = part.astype(F32).reshape(4, 2, TOK, 128).sum(axis=1).astype(BF16)
        return jnp.transpose(part, (1, 0, 2))[None]

    return (
        grad_queries,
        pair_sum(back[:, :, 512:640]),
        pair_sum(back[:, :, 640:768]),
        grad_out_weight,
    )


def solution(mesh):
    mesh = Mesh(mesh.devices.reshape(4, 2, 4, 8), ("x", "core", "y", "z"))
    pack, token = ("y", "z"), ("x", "core")
    placed = (
        P(pack, token, None, None),
        P(pack, token, None, None),
        P(pack, token, None, None),
        P(pack, token, None, None),
        P(pack, token, None),
        P(token + pack, None),
        P(pack, None),
    )
    return jax.shard_map(
        per_device,
        mesh=mesh,
        in_specs=placed,
        out_specs=(
            P(pack, token, None, None),
            P(pack, token, None, None),
            P(pack, token, None, None),
            P(token + pack, None),
        ),
        check_vma=False,
    )
```

profile of v0, /device:TPU:1, one launch (start us, length us, event | category | flops | bytes accessed | tf_op | source)
XLA Modules:
  0.0 227.3 jit_solution(17190050765586731888)
XLA Ops:
  7.2 0.9 select_bitcast_fusion.1
  8.2 3.3 %collective-permute-start.1 = (bf16[16,2560]{1,0:T(8,128)(2,1)S(1)}, bf16[16,2560]{1,0:T(8,128)(2,1)S(1)}, u32[]{:S(2)}, u32[]{:S(2)}) collective-permute-start(bf16[16,2560]{1,0:T(8,128)(2,1)S(1)} %get-tuple-element.66), channel_id=1, source_target_pairs={{0,32},{32,0},{1,33},{33,1},{2,34},{34,2},{3,35},{35,3},{4,36},{36... | collective-permute-start | bytes 245768 | tf_op jit(solution)/shard_map/ppermute | solution.py:35
  11.5 0.9 collective-permute-done.1
  13.1 2.2 broadcast_select_fusion
  16.0 1.3 copy.35
  17.3 4.2 %all-to-all-start = ((bf16[4,128,1024]{2,1,0:T(8,128)(2,1)}), bf16[4,128,1024]{2,1,0:T(8,128)(2,1)}, u32[]{:S(2)}, u32[]{:S(2)}) async-start(bf16[4,128,1024]{2,1,0:T(8,128)(2,1)} %bitcast.69), calls=%async_computation | async-start | bytes 2097152 | tf_op jit(solution)/shard_map/all_to_all | solution.py:249
  21.6 1.1 pad_maximum_fusion
  22.8 2.6 %collective-permute-start.3 = (bf16[256,1280]{1,0:T(8,128)(2,1)}, bf16[256,1280]{1,0:T(8,128)(2,1)}, u32[]{:S(2)}, u32[]{:S(2)}) collective-permute-start(bf16[256,1280]{1,0:T(8,128)(2,1)} %get-tuple-element.26.own), channel_id=1, source_target_pairs={{0,192},{64,0},{128,64},{192,128},{1,193},{65,1},{129,65},{193,129... | collective-permute-start | bytes 1966088 | tf_op jit(solution)/shard_map/ppermute | solution.py:27
  25.3 24.4 %all-gather.3.cloned.1.call-done = bf16[16,16,2560]{2,1,0:T(8,128)(2,1)} async-done(((bf16[2,16,2560]{2,1,0:T(8,128)(2,1)}), bf16[16,16,2560]{2,1,0:T(8,128)(2,1)}) %all-gather.3.cloned.1.call-update) | async-done | bytes 1310736 | tf_op jit(solution)/shard_map/all_gather | solution.py:246
  49.8 1.5 slice_bitcast_fusion.1
  51.3 2.5 %collective-permute-start.7 = (bf16[8,16,2560]{2,1,0:T(8,128)(2,1)S(1)}, bf16[8,16,2560]{2,1,0:T(8,128)(2,1)}, u32[]{:S(2)}, u32[]{:S(2)}) collective-permute-start(bf16[8,16,2560]{2,1,0:T(8,128)(2,1)S(1)} %get-tuple-element.56.refs_2_), channel_id=1, source_target_pairs={{0,24},{8,0},{16,8},{24,16},{1,25},{9,1},{17,9},{25,17},{2,26},{10... | collective-permute-start | bytes 1966088 | tf_op jit(solution)/shard_map/ppermute | solution.py:27
  53.8 4.6 %collective-permute-start.10 = (bf16[512,1024]{1,0:T(8,128)(2,1)}, bf16[512,1024]{1,0:T(8,128)(2,1)}, u32[]{:S(2)}, u32[]{:S(2)}) collective-permute-start(bf16[512,1024]{1,0:T(8,128)(2,1)} %bitcast.17.o_own), channel_id=1, source_target_pairs={{0,32},{32,0},{1,33},{33,1},{2,34},{34,2},{3,35},{35,3},{4,36},{36... | collective-permute-start | bytes 3145736 | tf_op jit(solution)/shard_map/ppermute | solution.py:35
  60.8 1.3 maximum_bitcast_fusion
  62.1 1.0 slice.83
  63.1 1.0 slice.84
  64.1 2.5 %collective-permute-start.5 = (bf16[128,1280]{1,0:T(8,128)(2,1)S(1)}, bf16[128,1280]{1,0:T(8,128)(2,1)S(1)}, u32[]{:S(2)}, u32[]{:S(2)}) collective-permute-start(bf16[128,1280]{1,0:T(8,128)(2,1)S(1)} %slice.84), channel_id=1, source_target_pairs={{0,192},{64,0},{128,64},{192,128},{1,193},{65,1},{129,65},{193,129... | collective-permute-start | bytes 983048 | tf_op jit(solution)/shard_map/ppermute | solution.py:27
  66.5 7.1 %collective-permute-done.5.far1 = bf16[128,1280]{1,0:T(8,128)(2,1)S(1)} collective-permute-done((bf16[128,1280]{1,0:T(8,128)(2,1)S(1)}, bf16[128,1280]{1,0:T(8,128)(2,1)S(1)}, u32[]{:S(2)}, u32[]{:S(2)}) %collective-permute-start.5) | collective-permute-done | bytes 327712 | tf_op jit(solution)/shard_map/ppermute | solution.py:27
  73.7 3.1 %collective-permute-done.4.far0 = bf16[128,1280]{1,0:T(8,128)(2,1)S(1)} collective-permute-done((bf16[128,1280]{1,0:T(8,128)(2,1)S(1)}, bf16[128,1280]{1,0:T(8,128)(2,1)S(1)}, u32[]{:S(2)}, u32[]{:S(2)}) %collective-permute-start.4) | collective-permute-done | bytes 327712 | tf_op jit(solution)/shard_map/ppermute | solution.py:27
  77.2 1.1 collective-permute-start.8
  78.3 3.0 %collective-permute-start.12 = (bf16[8,16,2560]{2,1,0:T(8,128)(2,1)S(1)}, bf16[8,16,2560]{2,1,0:T(8,128)(2,1)S(1)}, u32[]{:S(2)}, u32[]{:S(2)}) collective-permute-start(bf16[8,16,2560]{2,1,0:T(8,128)(2,1)S(1)} %get-tuple-element.35.refs_2_), channel_id=1, source_target_pairs={{0,24},{8,0},{16,8},{24,16},{1,25},{9,1},{17,9},{25,17},{2,26},{10... | collective-permute-start | bytes 1966088 | tf_op jit(solution)/shard_map/ppermute | solution.py:27
  81.9 7.0 %shard_map.102 = (bf16[8,4,2,16,1280]{4,3,2,1,0:T(8,128)(2,1)}, bf16[1024,1280]{1,0:T(8,128)(2,1)}) custom-call(s32[7]{0:T(128)} %concatenate.15.info, bf16[256,1280]{1,0:T(8,128)(2,1)} %get-tuple-element.26.own, bf16[256,1280]{1,0:T(8,128)(2,1)} %collective-permute-done.2.prev, bf16[256,1280]{1,0:T(8,128)(2,1)} %collective-permute-done.3.succ, ...), custom_call_target="tpu_custom_call" | custom-call | flops 2684354560 | bytes 12582912 | tf_op jit(solution)/shard_map/pallas_call | solution.py:71
  88.8 3.2 %collective-permute-done.9.succ = bf16[256,1280]{1,0:T(8,128)(2,1)} collective-permute-done((bf16[256,1280]{1,0:T(8,128)(2,1)S(1)}, bf16[256,1280]{1,0:T(8,128)(2,1)}, u32[]{:S(2)}, u32[]{:S(2)}) %collective-permute-start.9) | collective-permute-done | bytes 655392 | tf_op jit(solution)/shard_map/ppermute | solution.py:27
  92.1 1.6 collective-permute-done.8.prev
  93.7 3.1 %collective-permute-done.11.refs_3_ = bf16[8,16,2560]{2,1,0:T(8,128)(2,1)S(1)} collective-permute-done((bf16[8,16,2560]{2,1,0:T(8,128)(2,1)S(1)}, bf16[8,16,2560]{2,1,0:T(8,128)(2,1)S(1)}, u32[]{:S(2)}, u32[]{:S(2)}) %collective-permute-start.11) | collective-permute-done | bytes 655392 | tf_op jit(solution)/shard_map/ppermute | solution.py:27
  96.9 1.2 slice.87
  98.0 1.0 slice.88
  99.0 1.9 collective-permute-start.14
  101.0 4.5 %collective-permute-done.14.far1 = bf16[128,1280]{1,0:T(8,128)(2,1)S(1)} collective-permute-done((bf16[128,1280]{1,0:T(8,128)(2,1)S(1)}, bf16[128,1280]{1,0:T(8,128)(2,1)S(1)}, u32[]{:S(2)}, u32[]{:S(2)}) %collective-permute-start.14) | collective-permute-done | bytes 327712 | tf_op jit(solution)/shard_map/ppermute | solution.py:27
  105.5 3.1 %collective-permute-done.13.far0 = bf16[128,1280]{1,0:T(8,128)(2,1)S(1)} collective-permute-done((bf16[128,1280]{1,0:T(8,128)(2,1)S(1)}, bf16[128,1280]{1,0:T(8,128)(2,1)S(1)}, u32[]{:S(2)}, u32[]{:S(2)}) %collective-permute-start.13) | collective-permute-done | bytes 327712 | tf_op jit(solution)/shard_map/ppermute | solution.py:27
  109.3 7.0 %shard_map.103 = (bf16[8,4,2,16,1280]{4,3,2,1,0:T(8,128)(2,1)}, bf16[1024,1280]{1,0:T(8,128)(2,1)}) custom-call(s32[7]{0:T(128)} %concatenate.15.info, bf16[256,1280]{1,0:T(8,128)(2,1)} %get-tuple-element.30.own, bf16[256,1280]{1,0:T(8,128)(2,1)} %collective-permute-done.8.prev, bf16[256,1280]{1,0:T(8,128)(2,1)} %collective-permute-done.9.succ, ...), custom_call_target="tpu_custom_call" | custom-call | flops 2684354560 | bytes 12582912 | tf_op jit(solution)/shard_map/pallas_call | solution.py:71
  116.3 1.0 slice_bitcast_fusion.5
  117.3 1.0 slice_bitcast_fusion.3
  120.1 7.8 %all-to-all-start.1 = ((bf16[8,128,768]{2,1,0:T(8,128)(2,1)}), bf16[8,128,768]{2,1,0:T(8,128)(2,1)S(1)}, u32[]{:S(2)}, u32[]{:S(2)}) async-start(bf16[8,128,768]{2,1,0:T(8,128)(2,1)} %maximum_bitcast_fusion), calls=%async_computation.1 | async-start | bytes 3145728 | tf_op jit(solution)/shard_map/all_to_all | solution.py:285
  128.0 3.1 %collective-permute-done.16.refs_6_ = bf16[2,4,16,2560]{3,2,1,0:T(8,128)(2,1)} collective-permute-done((bf16[2,4,16,2560]{3,2,1,0:T(8,128)(2,1)S(1)}, bf16[2,4,16,2560]{3,2,1,0:T(8,128)(2,1)}, u32[]{:S(2)}, u32[]{:S(2)}) %collective-permute-start.16) | collective-permute-done | bytes 655392 | tf_op jit(solution)/shard_map/ppermute | solution.py:27
  131.1 1.9 collective-permute-done.15.refs_5_
  133.8 7.8 %shard_map.105 = bf16[1024,512]{1,0:T(8,128)(2,1)} custom-call(s32[7]{0:T(128)} %concatenate.15.info, bf16[1024,1280]{1,0:T(8,128)(2,1)} %get-tuple-element.37.refs_0_, bf16[1024,1280]{1,0:T(8,128)(2,1)} %get-tuple-element.40.refs_1_, bf16[8,16,2560]{2,1,0:T(8,128)(2,1)} %copy-done.6, bf16[8,16,2560]{2,1,0:T(8,128)(2,1)} %collective-permute-done.6.refs_3_, ...), custom_call_target="tpu_custom_call" | custom-call | flops 2684354560 | bytes 10485760 | tf_op jit(solution)/shard_map/pallas_call | solution.py:134
  141.6 4.7 %collective-permute-start.17 = (bf16[1024,512]{1,0:T(8,128)(2,1)}, bf16[1024,512]{1,0:T(8,128)(2,1)S(1)}, u32[]{:S(2)}, u32[]{:S(2)}) collective-permute-start(bf16[1024,512]{1,0:T(8,128)(2,1)} %shard_map.105), channel_id=1, source_target_pairs={{0,32},{32,0},{1,33},{33,1},{2,34},{34,2},{3,35},{35,3},{4,36},{36... | collective-permute-start | bytes 3145736 | tf_op jit(solution)/shard_map/ppermute | solution.py:35
  146.3 8.3 %shard_map.104.mine = f32[1024,512]{1,0:T(8,128)} custom-call(s32[7]{0:T(128)} %concatenate.15.info, bf16[1024,1280]{1,0:T(8,128)(2,1)} %get-tuple-element.37.refs_0_, bf16[1024,1280]{1,0:T(8,128)(2,1)} %get-tuple-element.40.refs_1_, bf16[8,16,2560]{2,1,0:T(8,128)(2,1)} %copy-done, bf16[8,16,2560]{2,1,0:T(8,128)(2,1)} %copy-done.3, ...), custom_call_target="tpu_custom_call" | custom-call | flops 2684354560 | bytes 10485760 | tf_op jit(solution)/shard_map/pallas_call | solution.py:134
  154.6 1.2 copy-done.1
  156.1 18.0 %shard_map.106 = bf16[1024,768]{1,0:T(8,128)(2,1)} custom-call(s32[7]{0:T(128)} %concatenate.15.info, bf16[1024,768]{1,0:T(8,128)(2,1)} %bitcast.71, bf16[1024,768]{1,0:T(8,128)(2,1)} %bitcast.72, bf16[1024,768]{1,0:T(8,128)(2,1)} %bitcast.73, f32[1024,512]{1,0:T(8,128)} %shard_map.104.mine, bf16[1024,512]{1,0:T(8,128)(2,1)} %copy-done.13, ...), custom_call_target="tpu_custom_call" | custom-call | flops 3355443200 | bytes 8388608 | tf_op jit(solution)/shard_map/pallas_call | solution.py:214
  174.1 6.1 %reduce-scatter.5.cloned.1.call-done = bf16[1,4,2,16,1280]{4,3,2,1,0:T(8,128)(2,1)} async-done(((bf16[8,4,2,16,1280]{4,3,2,1,0:T(8,128)(2,1)}), bf16[1,4,2,16,1280]{4,3,2,1,0:T(8,128)(2,1)}) %reduce-scatter.5.cloned.1.call-update) | async-done | bytes 327696 | tf_op jit(solution)/shard_map/reduce_scatter | solution.py:294
  180.2 1.1 pad_maximum_fusion.3
  181.4 1.6 collective-permute-start.18
  182.9 1.2 collective-permute-start.20
  184.1 1.5 collective-permute-start.19
  185.6 9.9 %all-to-all-start.2 = ((bf16[8,128,768]{2,1,0:T(8,128)(2,1)}), bf16[8,128,768]{2,1,0:T(8,128)(2,1)S(1)}, u32[]{:S(2)}, u32[]{:S(2)}) async-start(bf16[8,128,768]{2,1,0:T(8,128)(2,1)} %bitcast.70), calls=%async_computation.2 | async-start | bytes 3145728 | tf_op jit(solution)/shard_map/all_to_all | solution.py:312
  196.4 19.8 %all-to-all-done.2 = bf16[8,128,768]{2,1,0:T(8,128)(2,1)S(1)} async-done(((bf16[8,128,768]{2,1,0:T(8,128)(2,1)}), bf16[8,128,768]{2,1,0:T(8,128)(2,1)S(1)}, u32[]{:S(2)}, u32[]{:S(2)}) %all-to-all-start.2) | async-done | bytes 1572896 | tf_op jit(solution)/shard_map/all_to_all | solution.py:312
  216.9 1.4 reshape.57
  (89 shorter events, 12.5 us)
Async XLA Ops:
  7.2 42.6 %all-gather.3.cloned.1.call-start = ((), (), s32[]{:S(2)}) async-start(), calls=%async_computation.7 | async-start | bytes 1474560 | tf_op jit(solution)/shard_map/all_gather | solution.py:246
  8.2 7.6 %copy-start.4 = (bf16[1,128,32,128]{3,2,1,0:T(8,128)(2,1)S(1)}, bf16[1,128,32,128]{3,2,1,0:T(8,128)(2,1)}, u32[]{:S(2)}) copy-start(bf16[1,128,32,128]{3,2,1,0:T(8,128)(2,1)} %param.10) | copy-start | bytes 3145732
  8.2 4.3 %collective-permute-start.1 = (bf16[16,2560]{1,0:T(8,128)(2,1)S(1)}, bf16[16,2560]{1,0:T(8,128)(2,1)S(1)}, u32[]{:S(2)}, u32[]{:S(2)}) collective-permute-start(bf16[16,2560]{1,0:T(8,128)(2,1)S(1)} %get-tuple-element.66), channel_id=1, source_target_pairs={{0,32},{32,0},{1,33},{33,1},{2,34},{34,2},{3,35},{35,3},{4,36},{36... | collective-permute-start | bytes 245768 | tf_op jit(solution)/shard_map/ppermute | solution.py:35
  15.4 6.2 %collective-permute-start = (bf16[128,2560]{1,0:T(8,128)(2,1)}, bf16[128,2560]{1,0:T(8,128)(2,1)S(1)}, u32[]{:S(2)}, u32[]{:S(2)}) collective-permute-start(bf16[128,2560]{1,0:T(8,128)(2,1)} %get-tuple-element.58), channel_id=1, source_target_pairs={{0,32},{32,0},{1,33},{33,1},{2,34},{34,2},{3,35},{35,3},{4,36},{36... | collective-permute-start | bytes 1966088 | tf_op jit(solution)/shard_map/ppermute | solution.py:35
  17.3 36.5 %all-to-all-start = ((bf16[4,128,1024]{2,1,0:T(8,128)(2,1)}), bf16[4,128,1024]{2,1,0:T(8,128)(2,1)}, u32[]{:S(2)}, u32[]{:S(2)}) async-start(bf16[4,128,1024]{2,1,0:T(8,128)(2,1)} %bitcast.69), calls=%async_computation | async-start | bytes 2097152 | tf_op jit(solution)/shard_map/all_to_all | solution.py:249
  21.5 152.6 %reduce-scatter.3.cloned.1.call-start = ((), (), s32[]{:S(2)}) async-start(), calls=%async_computation.5 | async-start | bytes 2949120 | tf_op jit(solution)/shard_map/reduce_scatter | solution.py:294
  22.8 35.6 %copy-start.10 = (bf16[1,128,4,128]{3,2,1,0:T(4,128)(2,1)S(1)}, bf16[1,128,4,128]{3,2,1,0:T(4,128)(2,1)}, u32[]{:S(2)}) copy-start(bf16[1,128,4,128]{3,2,1,0:T(4,128)(2,1)} %param.8) | copy-start | bytes 393220
  22.8 36.3 %copy-start.11 = (bf16[1,128,4,128]{3,2,1,0:T(4,128)(2,1)S(1)}, bf16[1,128,4,128]{3,2,1,0:T(4,128)(2,1)}, u32[]{:S(2)}) copy-start(bf16[1,128,4,128]{3,2,1,0:T(4,128)(2,1)} %param.9) | copy-start | bytes 393220
  22.8 39.3 %collective-permute-start.3 = (bf16[256,1280]{1,0:T(8,128)(2,1)}, bf16[256,1280]{1,0:T(8,128)(2,1)}, u32[]{:S(2)}, u32[]{:S(2)}) collective-permute-start(bf16[256,1280]{1,0:T(8,128)(2,1)} %get-tuple-element.26.own), channel_id=1, source_target_pairs={{0,192},{64,0},{128,64},{192,128},{1,193},{65,1},{129,65},{193,129... | collective-permute-start | bytes 1966088 | tf_op jit(solution)/shard_map/ppermute | solution.py:27
  25.3 36.7 %collective-permute-start.2 = (bf16[256,1280]{1,0:T(8,128)(2,1)}, bf16[256,1280]{1,0:T(8,128)(2,1)}, u32[]{:S(2)}, u32[]{:S(2)}) collective-permute-start(bf16[256,1280]{1,0:T(8,128)(2,1)} %get-tuple-element.26.own), channel_id=1, source_target_pairs={{0,64},{64,128},{128,192},{192,0},{1,65},{65,129},{129,193},{193,1... | collective-permute-start | bytes 1966088 | tf_op jit(solution)/shard_map/ppermute | solution.py:27
  49.8 9.3 %copy-start.5 = (bf16[1,128,32,128]{3,2,1,0:T(8,128)(2,1)S(1)}, bf16[1,128,32,128]{3,2,1,0:T(8,128)(2,1)}, u32[]{:S(2)}) copy-start(bf16[1,128,32,128]{3,2,1,0:T(8,128)(2,1)} %param.7) | copy-start | bytes 3145732
  51.2 8.9 %copy-start.6 = (bf16[8,16,2560]{2,1,0:T(8,128)(2,1)}, bf16[8,16,2560]{2,1,0:T(8,128)(2,1)S(1)}, u32[]{:S(2)}) copy-start(bf16[8,16,2560]{2,1,0:T(8,128)(2,1)S(1)} %get-tuple-element.56.refs_2_) | copy-start | bytes 1966084
  51.2 30.1 %copy-start = (bf16[8,16,2560]{2,1,0:T(8,128)(2,1)}, bf16[8,16,2560]{2,1,0:T(8,128)(2,1)S(1)}, u32[]{:S(2)}) copy-start(bf16[8,16,2560]{2,1,0:T(8,128)(2,1)S(1)} %get-tuple-element.35.refs_2_) | copy-start | bytes 1966084
  51.3 25.5 %collective-permute-start.7 = (bf16[8,16,2560]{2,1,0:T(8,128)(2,1)S(1)}, bf16[8,16,2560]{2,1,0:T(8,128)(2,1)}, u32[]{:S(2)}, u32[]{:S(2)}) collective-permute-start(bf16[8,16,2560]{2,1,0:T(8,128)(2,1)S(1)} %get-tuple-element.56.refs_2_), channel_id=1, source_target_pairs={{0,24},{8,0},{16,8},{24,16},{1,25},{9,1},{17,9},{25,17},{2,26},{10... | collective-permute-start | bytes 1966088 | tf_op jit(solution)/shard_map/ppermute | solution.py:27
  53.8 23.0 %collective-permute-start.6 = (bf16[8,16,2560]{2,1,0:T(8,128)(2,1)S(1)}, bf16[8,16,2560]{2,1,0:T(8,128)(2,1)}, u32[]{:S(2)}, u32[]{:S(2)}) collective-permute-start(bf16[8,16,2560]{2,1,0:T(8,128)(2,1)S(1)} %get-tuple-element.56.refs_2_), channel_id=1, source_target_pairs={{0,8},{8,16},{16,24},{24,0},{1,9},{9,17},{17,25},{25,1},{2,10},{10... | collective-permute-start | bytes 1966088 | tf_op jit(solution)/shard_map/ppermute | solution.py:27
  53.8 28.1 %collective-permute-start.10 = (bf16[512,1024]{1,0:T(8,128)(2,1)}, bf16[512,1024]{1,0:T(8,128)(2,1)}, u32[]{:S(2)}, u32[]{:S(2)}) collective-permute-start(bf16[512,1024]{1,0:T(8,128)(2,1)} %bitcast.17.o_own), channel_id=1, source_target_pairs={{0,32},{32,0},{1,33},{33,1},{2,34},{34,2},{3,35},{35,3},{4,36},{36... | collective-permute-start | bytes 3145736 | tf_op jit(solution)/shard_map/ppermute | solution.py:35
  59.8 0.9 copy-start.9
  60.7 16.0 %copy-start.7 = (bf16[256,1280]{1,0:T(8,128)(2,1)S(1)}, bf16[256,1280]{1,0:T(8,128)(2,1)}, u32[]{:S(2)}) copy-start(bf16[256,1280]{1,0:T(8,128)(2,1)} %get-tuple-element.30.own) | copy-start | bytes 1966084
  60.8 20.6 %copy-start.12 = (s32[1,3]{1,0:T(1,128)S(1)}, s32[1,3]{1,0:T(1,128)}, u32[]{:S(2)}) copy-start(s32[1,3]{1,0:T(1,128)} %param.13) | copy-start | bytes 40
  64.1 9.6 %collective-permute-start.5 = (bf16[128,1280]{1,0:T(8,128)(2,1)S(1)}, bf16[128,1280]{1,0:T(8,128)(2,1)S(1)}, u32[]{:S(2)}, u32[]{:S(2)}) collective-permute-start(bf16[128,1280]{1,0:T(8,128)(2,1)S(1)} %slice.84), channel_id=1, source_target_pairs={{0,192},{64,0},{128,64},{192,128},{1,193},{65,1},{129,65},{193,129... | collective-permute-start | bytes 983048 | tf_op jit(solution)/shard_map/ppermute | solution.py:27
  66.5 10.2 %collective-permute-start.4 = (bf16[128,1280]{1,0:T(8,128)(2,1)S(1)}, bf16[128,1280]{1,0:T(8,128)(2,1)S(1)}, u32[]{:S(2)}, u32[]{:S(2)}) collective-permute-start(bf16[128,1280]{1,0:T(8,128)(2,1)S(1)} %slice.83), channel_id=1, source_target_pairs={{0,64},{64,128},{128,192},{192,0},{1,65},{65,129},{129,193},{193,1... | collective-permute-start | bytes 983048 | tf_op jit(solution)/shard_map/ppermute | solution.py:27
  73.7 3.5 %copy-start.14 = (bf16[128,1280]{1,0:T(8,128)(2,1)}, bf16[128,1280]{1,0:T(8,128)(2,1)S(1)}, u32[]{:S(2)}) copy-start(bf16[128,1280]{1,0:T(8,128)(2,1)S(1)} %collective-permute-done.5.far1) | copy-start | bytes 983044
  76.8 1.6 copy-start.15
  76.8 15.3 %collective-permute-start.9 = (bf16[256,1280]{1,0:T(8,128)(2,1)S(1)}, bf16[256,1280]{1,0:T(8,128)(2,1)}, u32[]{:S(2)}, u32[]{:S(2)}) collective-permute-start(bf16[256,1280]{1,0:T(8,128)(2,1)S(1)} %copy-done.7), channel_id=1, source_target_pairs={{0,192},{64,0},{128,64},{192,128},{1,193},{65,1},{129,65},{193,129... | collective-permute-start | bytes 1966088 | tf_op jit(solution)/shard_map/ppermute | solution.py:27
  77.2 16.5 %collective-permute-start.8 = (bf16[256,1280]{1,0:T(8,128)(2,1)S(1)}, bf16[256,1280]{1,0:T(8,128)(2,1)}, u32[]{:S(2)}, u32[]{:S(2)}) collective-permute-start(bf16[256,1280]{1,0:T(8,128)(2,1)S(1)} %copy-done.7), channel_id=1, source_target_pairs={{0,64},{64,128},{128,192},{192,0},{1,65},{65,129},{129,193},{193,1... | collective-permute-start | bytes 1966088 | tf_op jit(solution)/shard_map/ppermute | solution.py:27
  78.3 15.3 %collective-permute-start.12 = (bf16[8,16,2560]{2,1,0:T(8,128)(2,1)S(1)}, bf16[8,16,2560]{2,1,0:T(8,128)(2,1)S(1)}, u32[]{:S(2)}, u32[]{:S(2)}) collective-permute-start(bf16[8,16,2560]{2,1,0:T(8,128)(2,1)S(1)} %get-tuple-element.35.refs_2_), channel_id=1, source_target_pairs={{0,24},{8,0},{16,8},{24,16},{1,25},{9,1},{17,9},{25,17},{2,26},{10... | collective-permute-start | bytes 1966088 | tf_op jit(solution)/shard_map/ppermute | solution.py:27
  81.3 15.5 %collective-permute-start.11 = (bf16[8,16,2560]{2,1,0:T(8,128)(2,1)S(1)}, bf16[8,16,2560]{2,1,0:T(8,128)(2,1)S(1)}, u32[]{:S(2)}, u32[]{:S(2)}) collective-permute-start(bf16[8,16,2560]{2,1,0:T(8,128)(2,1)S(1)} %get-tuple-element.35.refs_2_), channel_id=1, source_target_pairs={{0,8},{8,16},{16,24},{24,0},{1,9},{9,17},{17,25},{25,1},{2,10},{10... | collective-permute-start | bytes 1966088 | tf_op jit(solution)/shard_map/ppermute | solution.py:27
  93.7 24.7 %copy-start.2 = (bf16[8,16,2560]{2,1,0:T(8,128)(2,1)}, bf16[8,16,2560]{2,1,0:T(8,128)(2,1)S(1)}, u32[]{:S(2)}) copy-start(bf16[8,16,2560]{2,1,0:T(8,128)(2,1)S(1)} %collective-permute-done.12.refs_4_) | copy-start | bytes 1966084
  96.8 22.3 %copy-start.3 = (bf16[8,16,2560]{2,1,0:T(8,128)(2,1)}, bf16[8,16,2560]{2,1,0:T(8,128)(2,1)S(1)}, u32[]{:S(2)}) copy-start(bf16[8,16,2560]{2,1,0:T(8,128)(2,1)S(1)} %collective-permute-done.11.refs_3_) | copy-start | bytes 1966084
  96.8 83.4 %reduce-scatter.5.cloned.1.call-start = ((), (), s32[]{:S(2)}) async-start(), calls=%async_computation.6 | async-start | bytes 2949120 | tf_op jit(solution)/shard_map/reduce_scatter | solution.py:294
  99.0 6.4 %collective-permute-start.14 = (bf16[128,1280]{1,0:T(8,128)(2,1)S(1)}, bf16[128,1280]{1,0:T(8,128)(2,1)S(1)}, u32[]{:S(2)}, u32[]{:S(2)}) collective-permute-start(bf16[128,1280]{1,0:T(8,128)(2,1)S(1)} %slice.88), channel_id=1, source_target_pairs={{0,192},{64,0},{128,64},{192,128},{1,193},{65,1},{129,65},{193,129... | collective-permute-start | bytes 983048 | tf_op jit(solution)/shard_map/ppermute | solution.py:27
  101.0 7.6 %collective-permute-start.13 = (bf16[128,1280]{1,0:T(8,128)(2,1)S(1)}, bf16[128,1280]{1,0:T(8,128)(2,1)S(1)}, u32[]{:S(2)}, u32[]{:S(2)}) collective-permute-start(bf16[128,1280]{1,0:T(8,128)(2,1)S(1)} %slice.87), channel_id=1, source_target_pairs={{0,64},{64,128},{128,192},{192,0},{1,65},{65,129},{129,193},{193,1... | collective-permute-start | bytes 983048 | tf_op jit(solution)/shard_map/ppermute | solution.py:27
  105.5 3.1 %copy-start.16 = (bf16[128,1280]{1,0:T(8,128)(2,1)}, bf16[128,1280]{1,0:T(8,128)(2,1)S(1)}, u32[]{:S(2)}) copy-start(bf16[128,1280]{1,0:T(8,128)(2,1)S(1)} %collective-permute-done.14.far1) | copy-start | bytes 983044
  108.6 0.7 copy-start.17
  118.4 12.6 %collective-permute-start.16 = (bf16[2,4,16,2560]{3,2,1,0:T(8,128)(2,1)S(1)}, bf16[2,4,16,2560]{3,2,1,0:T(8,128)(2,1)}, u32[]{:S(2)}, u32[]{:S(2)}) collective-permute-start(bf16[2,4,16,2560]{3,2,1,0:T(8,128)(2,1)S(1)} %pad_maximum_fusion.2), channel_id=1, source_target_pairs={{0,24},{8,0},{16,8},{24,16},{1,25},{9,1},{17,9},{25,17},{2,26},{10... | collective-permute-start | bytes 1966088 | tf_op jit(solution)/shard_map/ppermute | solution.py:27
  119.2 13.7 %collective-permute-start.15 = (bf16[2,4,16,2560]{3,2,1,0:T(8,128)(2,1)S(1)}, bf16[2,4,16,2560]{3,2,1,0:T(8,128)(2,1)S(1)}, u32[]{:S(2)}, u32[]{:S(2)}) collective-permute-start(bf16[2,4,16,2560]{3,2,1,0:T(8,128)(2,1)S(1)} %pad_maximum_fusion.1), channel_id=1, source_target_pairs={{0,8},{8,16},{16,24},{24,0},{1,9},{9,17},{17,25},{25,1},{2,10},{10... | collective-permute-start | bytes 1966088 | tf_op jit(solution)/shard_map/ppermute | solution.py:27
  120.1 34.5 %all-to-all-start.1 = ((bf16[8,128,768]{2,1,0:T(8,128)(2,1)}), bf16[8,128,768]{2,1,0:T(8,128)(2,1)S(1)}, u32[]{:S(2)}, u32[]{:S(2)}) async-start(bf16[8,128,768]{2,1,0:T(8,128)(2,1)} %maximum_bitcast_fusion), calls=%async_computation.1 | async-start | bytes 3145728 | tf_op jit(solution)/shard_map/all_to_all | solution.py:285
  133.0 0.9 copy-start.8
  141.6 13.0 %collective-permute-start.17 = (bf16[1024,512]{1,0:T(8,128)(2,1)}, bf16[1024,512]{1,0:T(8,128)(2,1)S(1)}, u32[]{:S(2)}, u32[]{:S(2)}) collective-permute-start(bf16[1024,512]{1,0:T(8,128)(2,1)} %shard_map.105), channel_id=1, source_target_pairs={{0,32},{32,0},{1,33},{33,1},{2,34},{34,2},{3,35},{35,3},{4,36},{36... | collective-permute-start | bytes 3145736 | tf_op jit(solution)/shard_map/ppermute | solution.py:35
  154.6 1.2 copy-start.1
  154.6 1.5 copy-start.13
  181.4 14.2 %collective-permute-start.18 = (bf16[2,16,2560]{2,1,0:T(8,128)(2,1)S(1)}, bf16[2,16,2560]{2,1,0:T(8,128)(2,1)S(1)}, u32[]{:S(2)}, u32[]{:S(2)}) collective-permute-start(bf16[2,16,2560]{2,1,0:T(8,128)(2,1)S(1)} %get-tuple-element.60), channel_id=1, source_target_pairs={{0,8},{8,16},{16,24},{24,0},{1,9},{9,17},{17,25},{25,1},{2,10},{10... | collective-permute-start | bytes 491528 | tf_op jit(solution)/shard_map/ppermute | solution.py:27
  182.9 12.6 %collective-permute-start.20 = (bf16[2,16,2560]{2,1,0:T(8,128)(2,1)S(1)}, bf16[2,16,2560]{2,1,0:T(8,128)(2,1)S(1)}, u32[]{:S(2)}, u32[]{:S(2)}) collective-permute-start(bf16[2,16,2560]{2,1,0:T(8,128)(2,1)S(1)} %get-tuple-element.61), channel_id=1, source_target_pairs={{0,24},{8,0},{16,8},{24,16},{1,25},{9,1},{17,9},{25,17},{2,26},{10... | collective-permute-start | bytes 491528 | tf_op jit(solution)/shard_map/ppermute | solution.py:27
  184.1 11.4 %collective-permute-start.19 = (bf16[2,16,2560]{2,1,0:T(8,128)(2,1)S(1)}, bf16[2,16,2560]{2,1,0:T(8,128)(2,1)S(1)}, u32[]{:S(2)}, u32[]{:S(2)}) collective-permute-start(bf16[2,16,2560]{2,1,0:T(8,128)(2,1)S(1)} %get-tuple-element.62), channel_id=1, source_target_pairs={{0,16},{8,24},{16,0},{24,8},{1,17},{9,25},{17,1},{25,9},{2,18},{10... | collective-permute-start | bytes 491528 | tf_op jit(solution)/shard_map/ppermute | solution.py:27
  185.6 30.6 %all-to-all-start.2 = ((bf16[8,128,768]{2,1,0:T(8,128)(2,1)}), bf16[8,128,768]{2,1,0:T(8,128)(2,1)S(1)}, u32[]{:S(2)}, u32[]{:S(2)}) async-start(bf16[8,128,768]{2,1,0:T(8,128)(2,1)} %bitcast.70), calls=%async_computation.2 | async-start | bytes 3145728 | tf_op jit(solution)/shard_map/all_to_all | solution.py:312
  195.6 24.3 %collective-permute-start.21 = (f32[16,2560]{1,0:T(8,128)S(1)}, f32[16,2560]{1,0:T(8,128)S(1)}, u32[]{:S(2)}, u32[]{:S(2)}) collective-permute-start(f32[16,2560]{1,0:T(8,128)S(1)} %select_bitcast_fusion), channel_id=1, source_target_pairs={{0,32},{32,0},{1,33},{33,1},{2,34},{34,2},{3,35},{35,3},{4,36},{36... | collective-permute-start | bytes 491528 | tf_op jit(solution)/shard_map/ppermute | solution.py:35
Sparse Core Ops, SparseCore 0:
  13.3 36.4 all-gather.2
  96.9 37.1 reduce-scatter.2
  136.7 43.4 reduce-scatter.4
where the time goes:
time: 228 us; the launch traced here: 227 us
  waiting for transfers between devices  82 us (36%)
  starting transfers between devices  55.8 us (24%)
  Pallas kernels  48.1 us (21%)
  local copies, waits for them, and re-layouts  18.9 us (8%)
  between operations  14.1 us (6%)
  other arithmetic  8.48 us (4%)
    ppermute x17, waiting for transfers between devices, shift(): lax.ppermute(value, axis, [(i, (i + by) % size) for i in range(size)])  30.8 us
    all_gather x1, waiting for transfers between devices, per_device(): gathered = lax.all_gather(weight_pair, 'z', axis=0, tiled=False)  24.4 us
    ppermute x17, starting transfers between devices, shift(): lax.ppermute(value, axis, [(i, (i + by) % size) for i in range(size)])  19.9 us
    all_to_all x1, waiting for transfers between devices, per_device(): lax.all_to_all(grads.reshape(8, TOK, 768), ('x', 'core'), split_axis=0, c...  19.8 us
    pallas_call x1, Pallas kernels, attention(): pl.pallas_call(attention_kernel, out_shape=jax.ShapeDtypeStruct((1024, 76...  18 us
    pallas_call x2, Pallas kernels, project(): pl.pallas_call(project_kernel, out_shape=jax.ShapeDtypeStruct((1024, 512)...  16.1 us
    pallas_call x2, Pallas kernels, weight_piece(): pl.pallas_call(functools.partial(weight_kernel, factor), out_shape=(jax.S...  14 us
    ppermute x5, starting transfers between devices, swap(): return lax.ppermute(value, 'core', [(0, 1), (1, 0)])  13.7 us
  transfers between devices with their start and end apart: 28, of which 13 were waited for; matrix products, arithmetic and copies ran while one was open for 9% of the time, Pallas kernels for 21%

commit v1 on v0

--- a/solution.py
+++ b/solution.py
@@ -11,8 +11,7 @@
 
 TOK = 128
 QB = 256
-WIDTHS = (1280, 1280)
-PIECES = 2
+COLS = 512
 F32 = jnp.float32
 BF16 = jnp.bfloat16
 VMEM = 56 * 1024 * 1024
@@ -35,9 +34,13 @@
     return lax.ppermute(value, "core", [(0, 1), (1, 0)])
 
 
-def weight_kernel(factor, info, own, prev, succ, far0, far1, o_own, o_sib, *outs):
-    *terms, rows = outs
-    here = info[0]
+def weight_kernel(factor, info, own, prev, succ, far0, far1, o_own, o_sib, term, rows, turned):
+    here, y = info[0], info[1]
+
+    @pl.when(pl.program_id(0) == 0)
+    def _():
+        turned[:, :512] = o_own[...].T
+        turned[:, 512:] = o_sib[...].T
 
     def put(chip, rc, value):
         rows[pl.ds(pl.multiple_of(rc * 512 + chip * TOK, TOK), TOK), :] = value
@@ -49,87 +52,82 @@
         put(lax.rem(here + 1, 4), rc, succ[part, :])
     put(lax.rem(here + 2, 4), 0, far0[...])
     put(lax.rem(here + 2, 4), 1, far1[...])
-    y = info[1]
-    low = rows[:512, :]
-    high = rows[512:, :]
-    for kk in range(2):
-        for part in range(2):
-            cols = slice(kk * 512 + part * 256, kk * 512 + part * 256 + 256)
-            dims = (((0,), (0,)), ((), ()))
-            term = lax.dot_general(o_own[:, cols], low, dims, preferred_element_type=F32)
-            term += lax.dot_general(o_sib[:, cols], high, dims, preferred_element_type=F32)
-            term = (term * factor).astype(BF16)
-            for at in range(16):
-                f = part * 16 + at
-                ry = lax.rem(f // 8 - y + 4, 4)
-                terms[0][f % 8, ry, kk] = term[at * 16 : at * 16 + 16, :]
-
-
-def weight_piece(info, parts, o_own, o_sib, factor):
-    width = parts[0].shape[1]
-    whole = pl.BlockSpec(memory_space=pltpu.VMEM)
+    for part in range(4):
+        product = jnp.dot(
+            turned[part * 256 : part * 256 + 256, :], rows[...], preferred_element_type=F32
+        )
+        product = (product * factor).astype(BF16)
+        for at in range(16):
+            f = part % 2 * 16 + at
+            ry = lax.rem(f // 8 - y + 4, 4)
+            term[f % 8, ry, part // 2] = product[at * 16 : at * 16 + 16, :]
+
+
+def weight_product(info, parts, o_own, o_sib, factor):
+    grid_spec = pltpu.PrefetchScalarGridSpec(
+        num_scalar_prefetch=1,
+        grid=(2560 // COLS,),
+        in_specs=[pl.BlockSpec((p.shape[0], COLS), lambda n, info: (0, n)) for p in parts]
+        + [pl.BlockSpec((512, 1024), lambda n, info: (0, 0))] * 2,
+        out_specs=(
+            pl.BlockSpec((8, 4, 2, 16, COLS), lambda n, info: (0, 0, 0, 0, n)),
+            pl.BlockSpec((1024, COLS), lambda n, info: (0, n)),
+        ),
+        scratch_shapes=[pltpu.VMEM((1024, 1024), BF16)],
+    )
     return pl.pallas_call(
         functools.partial(weight_kernel, factor),
         out_shape=(
-            jax.ShapeDtypeStruct((8, 4, 2, 16, width), BF16),
-            jax.ShapeDtypeStruct((1024, width), BF16),
-        ),
-        in_specs=[pl.BlockSpec(memory_space=pltpu.SMEM)] + [whole] * 7,
-        out_specs=(whole, whole),
+            jax.ShapeDtypeStruct((8, 4, 2, 16, 2560), BF16),
+            jax.ShapeDtypeStruct((1024, 2560), BF16),
+        ),
+        grid_spec=grid_spec,
         compiler_params=params(),
         cost_estimate=pl.CostEstimate(
-            flops=2 * 1024 * 1024 * width, bytes_accessed=12 * 1024 * 1024, transcendentals=0
+            flops=2 * 1024 * 1024 * 2560, bytes_accessed=18 * 1024 * 1024, transcendentals=0
         ),
     )(info, *parts, o_own, o_sib)
 
 
-def project_kernel(info, *refs):
-    first, last, near, prev, succ, far0, far1, out, weight = refs
-    rows = (first, last)
+def project_kernel(info, rows, block, out, weight, total):
     y, core = info[1], info[3]
-
-    def put(from_y, at, value):
-        row = lax.rem(from_y, 4) * 128 + at
-        count = value.shape[0] * 16
-        weight[pl.ds(pl.multiple_of(row, 64), count), :] = value.reshape(count, 2560)
-
-    put(y, 0, near[...])
-    put(y + 3, 0, prev[...])
-    put(y + 1, 0, succ[...])
-    put(y + 2, 0, far0[...])
-    put(y + 2, 64, far1[...])
-    for part in range(2):
-        block = slice(part * 256, part * 256 + 256)
-        total = None
-        begin = 0
-        for piece in rows:
-            width = piece.shape[1]
-            term = lax.dot_general(
-                piece[...],
-                weight[block, begin : begin + width],
-                (((1,), (1,)), ((), ())),
-                preferred_element_type=F32,
-            )
-            total = term if total is None else total + term
-            begin += width
-        total = total.astype(out.dtype)
+    step = pl.program_id(0)
+    for r in range(4):
+        for z in range(8):
+            row = (lax.rem(y - r + 4, 4) * 8 + z) * 16
+            weight[pl.ds(pl.multiple_of(row, 16), 16), :] = block[z, r]
+    product = lax.dot_general(
+        rows[...], weight[...], (((1,), (1,)), ((), ())), preferred_element_type=F32
+    )
+
+    @pl.when(step == 0)
+    def _():
+        total[...] = product
+
+    @pl.when(step > 0)
+    def _():
+        total[...] += product
+
+    @pl.when(step == pl.num_programs(0) - 1)
+    def _():
         for rc in range(2):
             for chip in range(4):
                 at = rc * 512 + chip * TOK
                 spot = chip * 256 + (core if rc == 0 else 1 - core) * TOK
-                out[pl.ds(pl.multiple_of(spot, TOK), TOK), block] = total[at : at + TOK, :]
-
-
-def project(info, pieces, parts, rc, dtype):
-    far = pl.BlockSpec((None, 4, 16, 2560), lambda n, info: (rc, 0, 0, 0))
+                spot = pl.ds(pl.multiple_of(spot, TOK), TOK)
+                out[spot, :] = total[at : at + TOK, :].astype(out.dtype)
+
+
+def project(info, rows, weight, rc, dtype):
     grid_spec = pltpu.PrefetchScalarGridSpec(
         num_scalar_prefetch=1,
-        grid=(1,),
-        in_specs=[pl.BlockSpec(p.shape, lambda n, info: (0, 0)) for p in pieces]
-        + [pl.BlockSpec((8, 16, 2560), lambda n, info: (0, 0, 0))] * 3
-        + [far, far],
+        grid=(2560 // COLS,),
+        in_specs=[
+            pl.BlockSpec((1024, COLS), lambda n, info: (0, n)),
+            pl.BlockSpec((8, 4, None, 16, COLS), lambda n, info: (0, 0, rc, 0, n)),
+        ],
         out_specs=pl.BlockSpec((1024, 512), lambda n, info: (0, 0)),
-        scratch_shapes=[pltpu.VMEM((512, 2560), BF16)],
+        scratch_shapes=[pltpu.VMEM((512, COLS), BF16), pltpu.VMEM((1024, 512), F32)],
     )
     return pl.pallas_call(
         project_kernel,
@@ -139,7 +137,7 @@
         cost_estimate=pl.CostEstimate(
             flops=2 * 1024 * 512 * 2560, bytes_accessed=10 * 1024 * 1024, transcendentals=0
         ),
-    )(info, *pieces, *parts)
+    )(info, rows, weight)
 
 
 def attention_kernel(info, query, key, value, mine, theirs, o_own, o_sib, out, key_acc, value_acc):
@@ -217,7 +215,7 @@
         grid_spec=grid_spec,
         compiler_params=params(),
         cost_estimate=pl.CostEstimate(
-            flops=4 * 10 * 256 * 256 * 128 * 10,
+            flops=14 * 10**9,
             bytes_accessed=8 * 1024 * 1024,
             transcendentals=4 * 10 * 256 * 256,
         ),
@@ -243,7 +241,8 @@
 
     weight_mine, weight_theirs = halves(out_weight)
     weight_pair = jnp.stack([weight_mine, swap(weight_theirs)])
-    gathered = lax.all_gather(weight_pair, "z", axis=0, tiled=False)
+    near = jnp.stack([weight_pair] + [shift(weight_pair, "y", r) for r in (1, 2, 3)])
+    weight = lax.all_gather(near, "z", axis=0, tiled=False)
 
     o_split = jnp.transpose(attn_out.reshape(TOK, 4, 1024), (1, 0, 2))
     o_own = lax.all_to_all(o_split, "x", split_axis=0, concat_axis=0, tiled=True)
@@ -262,45 +261,24 @@
     )
     packed = jnp.transpose(packed, (1, 0, 2))
 
-    first_own, last_own = grad_chip[:, : WIDTHS[0]], grad_chip[:, WIDTHS[0] :]
-
-    def weigh(parts):
-        return weight_piece(info, parts, o_own, o_sib, factor)
-
-    first_own = after(first_own, weight_pair)
-    prev, succ = shift(first_own, "x", 1), shift(first_own, "x", -1)
-    near0, near1 = gathered[:, 0], gathered[:, 1]
-    prev1, succ1 = shift(near1, "y", 1), shift(near1, "y", -1)
-    prev, succ, packed, near0 = lax.optimization_barrier((prev, succ, packed, near0))
-    far0, far1 = shift(prev[:TOK], "x", 1), shift(succ[TOK:], "x", -1)
-    far0, far1, prev1, succ1, last_own, near0 = lax.optimization_barrier(
-        (far0, far1, prev1, succ1, last_own, near0)
-    )
-    first_term, first_rows = weigh((first_own, prev, succ, far0, far1))
-    prev, succ = shift(last_own, "x", 1), shift(last_own, "x", -1)
-    prev0, succ0 = shift(near0, "y", 1), shift(near0, "y", -1)
-    prev, succ, packed, first_term, prev0, succ0 = lax.optimization_barrier(
-        (prev, succ, packed, first_term, prev0, succ0)
-    )
+    own = after(grad_chip, near)
+    prev, succ = shift(own, "x", 1), shift(own, "x", -1)
+    prev, succ, packed = lax.optimization_barrier((prev, succ, packed))
     packed = lax.all_to_all(packed, ("x", "core"), split_axis=0, concat_axis=0, tiled=True)
     packed = packed.reshape(1024, 768)
     far0, far1 = shift(prev[:TOK], "x", 1), shift(succ[TOK:], "x", -1)
-    weight_far0 = shift(jnp.stack([prev0[:4], prev1[:4]]), "y", 1)
-    weight_far1 = shift(jnp.stack([succ0[4:], succ1[4:]]), "y", -1)
-    last_term, last_rows = weigh((last_own, prev, succ, far0, far1))
-    pieces = (first_rows, last_rows)
-
-    summed = [
-        lax.psum_scatter(term, "z", scatter_dimension=0, tiled=True)[0]
-        for term in (first_term, last_term)
-    ]
-
-    sibling_part = project(info, pieces, (near1, prev1, succ1, weight_far0, weight_far1), 1, BF16)
-    theirs = swap(sibling_part)
-    mine = project(info, pieces, (near0, prev0, succ0, weight_far0, weight_far1), 0, F32)
+    term, rows = weight_product(info, (own, prev, succ, far0, far1), o_own, o_sib, factor)
+
+    summed = lax.psum_scatter(term, "z", scatter_dimension=0, tiled=True)[0]
+
+    theirs = swap(project(info, rows, weight, 1, BF16))
+    mine = project(info, rows, weight, 0, F32)
     grads = attention(info, packed, mine, theirs, o_own, o_sib)
-
-    summed = after(jnp.concatenate(summed, axis=-1), grads)
+    back = lax.all_to_all(
+        grads.reshape(8, TOK, 768), ("x", "core"), split_axis=0, concat_axis=0, tiled=True
+    )
+
+    summed = after(summed, back)
     summed = add(summed[0], *(shift(summed[r], "y", r) for r in (1, 2, 3)))
     keep = jnp.where(core == 0, summed[0], summed[1])
     give = jnp.where(core == 0, summed[1], summed[0])
@@ -309,9 +287,6 @@
         [jnp.where(core == 0, keep, come), jnp.where(core == 0, come, keep)], axis=-1
     ).astype(F32)
 
-    back = lax.all_to_all(
-        grads.reshape(8, TOK, 768), ("x", "core"), split_axis=0, concat_axis=0, tiled=True
-    )
     grad_queries = jnp.transpose(back[:, :, :512], (1, 0, 2)).reshape(1, TOK, 32, 128)
 
     def pair_sum(part):

time: 228 us -> 206 us (0.904)
  blocking collectives: 0 us -> 65.3 us
  waiting for transfers between devices: 82 us -> 38.8 us
  starting transfers between devices: 55.8 us -> 20.7 us
  local copies, waits for them, and re-layouts: 18.9 us -> 13.2 us
  other arithmetic: 8.48 us -> 5.36 us
    all_to_all x0 -> x2, blocking collectives: none -> 65.3 us  [the longest x1 40.2 us: per_device(): lax.all_to_all(o_split, 'x', split_axis=0, concat_axis=0, tiled=True)]
    all_gather x1, waiting for transfers between devices: 24.4 us -> 0.01 us  [per_device(): weight = lax.all_gather(near, 'z', axis=0, tiled=False)]
    all_to_all x2 -> x0, waiting for transfers between devices: 19.8 us -> none  [the longest x1 19.8 us: per_device(): lax.all_to_all(grads.reshape(8, TOK, 768), ('x', 'core'), split_axis=0, c...]
    all_to_all x2 -> x0, starting transfers between devices: 14.1 us -> none  [the longest x1 9.9 us: per_device(): lax.all_to_all(grads.reshape(8, TOK, 768), ('x', 'core'), split_axis=0, c...]
    ppermute x17 -> x10, starting transfers between devices: 19.9 us -> 9.25 us  [shift(): lax.ppermute(value, axis, [(i, (i + by) % size) for i in range(size)])]
    ppermute x5, starting transfers between devices: 13.7 us -> 5.95 us  [swap(): return lax.ppermute(value, 'core', [(0, 1), (1, 0)])]
    reduce_scatter x2 -> x1, waiting for transfers between devices: 6.08 us -> 0.01 us  [per_device(): summed = lax.psum_scatter(term, 'z', scatter_dimension=0, tiled=True)[0]]
    all_to_all x1, waiting for transfers between devices: 0.01 us -> 2.68 us  [per_device(): lax.all_to_all(packed, ('x', 'core'), split_axis=0, concat_axis=0, tiled=...]
  transfers between devices with their start and end apart: 28 -> 18, of which waited for: 13 -> 11; matrix products, arithmetic and copies ran while one was open for 9% -> 5% of each run, Pallas kernels for 21% -> 23%
where the time goes in v1:
time: 206 us
  blocking collectives  65.3 us (32%)
  Pallas kernels  47.9 us (23%)
  waiting for transfers between devices  38.8 us (19%)
  starting transfers between devices  20.7 us (10%)
  between operations  14.3 us (7%)
  local copies, waits for them, and re-layouts  13.2 us (6%)
  other arithmetic  5.36 us (3%)
    all_to_all x1, blocking collectives, per_device(): lax.all_to_all(o_split, 'x', split_axis=0, concat_axis=0, tiled=True)  40.2 us
    ppermute x10, waiting for transfers between devices, shift(): lax.ppermute(value, axis, [(i, (i + by) % size) for i in range(size)])  33.4 us
    all_to_all x1, blocking collectives, per_device(): lax.all_to_all(grads.reshape(8, TOK, 768), ('x', 'core'), split_axis=0, c...  25.1 us
    pallas_call x1, Pallas kernels, attention(): pl.pallas_call(attention_kernel, out_shape=jax.ShapeDtypeStruct((1024, 76...  18 us
    pallas_call x2, Pallas kernels, project(): pl.pallas_call(project_kernel, out_shape=jax.ShapeDtypeStruct((1024, 512)...  18 us
    pallas_call x1, Pallas kernels, weight_product(): pl.pallas_call(functools.partial(weight_kernel, factor), out_shape=(jax.S...  11.8 us
    ppermute x10, starting transfers between devices, shift(): lax.ppermute(value, axis, [(i, (i + by) % size) for i in range(size)])  9.25 us
    ppermute x5, starting transfers between devices, swap(): return lax.ppermute(value, 'core', [(0, 1), (1, 0)])  5.95 us
  transfers between devices with their start and end apart: 18, of which 11 were waited for; matrix products, arithmetic and copies ran while one was open for 5% of the time, Pallas kernels for 23%

profile of v1, /device:TPU:1, one launch (start us, length us, event | category | flops | bytes accessed | tf_op | source)
XLA Modules:
  0.0 205.5 jit_solution(1500164953618724271)
XLA Ops:
  7.2 1.0 select_bitcast_fusion.1
  8.3 3.3 %collective-permute-start.1 = (bf16[16,2560]{1,0:T(8,128)(2,1)S(1)}, bf16[16,2560]{1,0:T(8,128)(2,1)S(1)}, u32[]{:S(2)}, u32[]{:S(2)}) collective-permute-start(bf16[16,2560]{1,0:T(8,128)(2,1)S(1)} %get-tuple-element.34), channel_id=1, source_target_pairs={{0,32},{32,0},{1,33},{33,1},{2,34},{34,2},{3,35},{35,3},{4,36},{36... | collective-permute-start | bytes 245768 | tf_op jit(solution)/shard_map/ppermute | solution.py:34
  11.6 0.9 collective-permute-done.1
  12.5 1.1 collective-permute-start.4
  14.0 0.7 collective-permute-start.2
  14.7 3.4 %collective-permute-done.4 = bf16[2,16,2560]{2,1,0:T(8,128)(2,1)S(1)} collective-permute-done((bf16[2,16,2560]{2,1,0:T(8,128)(2,1)S(1)}, bf16[2,16,2560]{2,1,0:T(8,128)(2,1)S(1)}, u32[]{:S(2)}, u32[]{:S(2)}) %collective-permute-start.4) | collective-permute-done | bytes 163872 | tf_op jit(solution)/shard_map/ppermute | solution.py:26
  18.1 2.2 %collective-permute-done.3 = bf16[2,16,2560]{2,1,0:T(8,128)(2,1)S(1)} collective-permute-done((bf16[2,16,2560]{2,1,0:T(8,128)(2,1)S(1)}, bf16[2,16,2560]{2,1,0:T(8,128)(2,1)S(1)}, u32[]{:S(2)}, u32[]{:S(2)}) %collective-permute-start.3) | collective-permute-done | bytes 163872 | tf_op jit(solution)/shard_map/ppermute | solution.py:26
  20.3 4.5 %collective-permute-done.2 = bf16[2,16,2560]{2,1,0:T(8,128)(2,1)S(1)} collective-permute-done((bf16[2,16,2560]{2,1,0:T(8,128)(2,1)S(1)}, bf16[2,16,2560]{2,1,0:T(8,128)(2,1)S(1)}, u32[]{:S(2)}, u32[]{:S(2)}) %collective-permute-start.2) | collective-permute-done | bytes 163872 | tf_op jit(solution)/shard_map/ppermute | solution.py:26
  24.8 1.0 pad_maximum_fusion.1
  25.9 0.6 collective-permute-start
  26.5 1.7 collective-permute-done
  28.3 1.3 collective-permute-start.5
  29.6 1.5 collective-permute-start.6
  31.7 40.2 %all_to_all.15 = bf16[4,128,1024]{2,1,0:T(8,128)(2,1)} all-to-all(bf16[4,128,1024]{2,1,0:T(8,128)(2,1)S(1)} %bitcast.60), channel_id=1, replica_groups=mesh['x'=4,'core'=2,'y'=4,'z'=8] {'x'}, dimensions={0} | all-to-all | bytes 2097152 | tf_op jit(solution)/shard_map/all_to_all | solution.py:248
  71.9 1.2 collective-permute-start.9
  73.1 0.7 copy.17
  73.9 0.7 reshape.50
  74.9 0.6 copy-done.5
  75.5 1.3 maximum_bitcast_fusion
  76.8 1.1 slice.51
  78.0 0.9 collective-permute-start.7
  78.9 1.1 slice.52
  80.0 1.9 collective-permute-start.8
  81.9 0.6 concatenate.12.info
  82.6 13.1 %collective-permute-done.7.far0 = bf16[128,2560]{1,0:T(8,128)(2,1)S(1)} collective-permute-done((bf16[128,2560]{1,0:T(8,128)(2,1)S(1)}, bf16[128,2560]{1,0:T(8,128)(2,1)S(1)}, u32[]{:S(2)}, u32[]{:S(2)}) %collective-permute-start.7) | collective-permute-done | bytes 655392 | tf_op jit(solution)/shard_map/ppermute | solution.py:26
  95.6 0.5 collective-permute-done.8.far1
  96.5 0.9 copy-done.11
  97.3 11.8 %shard_map.102 = (bf16[8,4,2,16,2560]{4,3,2,1,0:T(8,128)(2,1)}, bf16[1024,2560]{1,0:T(8,128)(2,1)}) custom-call(s32[7]{0:T(128)} %concatenate.12.info, bf16[256,2560]{1,0:T(8,128)(2,1)} %copy-done.1, bf16[256,2560]{1,0:T(8,128)(2,1)} %collective-permute-done.5.prev, bf16[256,2560]{1,0:T(8,128)(2,1)} %collective-permute-done.6.succ, ...), custom_call_target="tpu_custom_call" | custom-call | flops 5368709120 | bytes 18874368 | tf_op jit(solution)/shard_map/pallas_call | solution.py:78
  109.2 5.4 %all-to-all-start = ((bf16[8,128,768]{2,1,0:T(8,128)(2,1)}), bf16[8,128,768]{2,1,0:T(8,128)(2,1)S(1)}, u32[]{:S(2)}, u32[]{:S(2)}) async-start(bf16[8,128,768]{2,1,0:T(8,128)(2,1)} %maximum_bitcast_fusion), calls=%async_computation | async-start | bytes 3145728 | tf_op jit(solution)/shard_map/all_to_all | solution.py:267
  114.6 8.8 %shard_map.104 = bf16[1024,512]{1,0:T(8,128)(2,1)} custom-call(s32[7]{0:T(128)} %concatenate.12.info, bf16[1024,2560]{1,0:T(8,128)(2,1)} %get-tuple-element.15.rows, bf16[8,4,2,16,2560]{4,3,2,1,0:T(8,128)(2,1)} %bitcast.58), custom_call_target="tpu_custom_call" | custom-call | flops 2684354560 | bytes 10485760 | tf_op jit(solution)/shard_map/pallas_call | solution.py:132
  123.4 9.2 %shard_map.103.mine = f32[1024,512]{1,0:T(8,128)} custom-call(s32[7]{0:T(128)} %concatenate.12.info, bf16[1024,2560]{1,0:T(8,128)(2,1)} %get-tuple-element.15.rows, bf16[8,4,2,16,2560]{4,3,2,1,0:T(8,128)(2,1)} %bitcast.59), custom_call_target="tpu_custom_call" | custom-call | flops 2684354560 | bytes 10485760 | tf_op jit(solution)/shard_map/pallas_call | solution.py:132
  132.6 2.7 %all-to-all-done = bf16[8,128,768]{2,1,0:T(8,128)(2,1)S(1)} async-done(((bf16[8,128,768]{2,1,0:T(8,128)(2,1)}), bf16[8,128,768]{2,1,0:T(8,128)(2,1)S(1)}, u32[]{:S(2)}, u32[]{:S(2)}) %all-to-all-start) | async-done | bytes 1572896 | tf_op jit(solution)/shard_map/all_to_all | solution.py:267
  135.3 1.2 copy-done
  136.8 18.0 %shard_map.105 = bf16[1024,768]{1,0:T(8,128)(2,1)} custom-call(s32[7]{0:T(128)} %concatenate.12.info, bf16[1024,768]{1,0:T(8,128)(2,1)} %bitcast.61, bf16[1024,768]{1,0:T(8,128)(2,1)} %bitcast.62, bf16[1024,768]{1,0:T(8,128)(2,1)} %bitcast.63, f32[1024,512]{1,0:T(8,128)} %shard_map.103.mine, bf16[1024,512]{1,0:T(8,128)(2,1)} %copy-done.9, ...), custom_call_target="tpu_custom_call" | custom-call | flops 14000000000 | bytes 8388608 | tf_op jit(solution)/shard_map/pallas_call | solution.py:212
  154.8 25.1 %all_to_all.16 = bf16[8,128,768]{2,1,0:T(8,128)(2,1)S(1)} all-to-all(bf16[8,128,768]{2,1,0:T(8,128)(2,1)} %bitcast.64), channel_id=1, replica_groups=mesh['x'=4,'core'=2,'y'=4,'z'=8] {'x','core'}, dimensions={0} | all-to-all | bytes 3145728 | tf_op jit(solution)/shard_map/all_to_all | solution.py:277
  180.0 1.1 slice_bitcast_fusion.3
  181.1 0.4 collective-permute-start.13
  181.7 0.9 collective-permute-start.11
  182.6 3.2 %collective-permute-done.13 = bf16[2,16,2560]{2,1,0:T(8,128)(2,1)S(1)} collective-permute-done((bf16[2,16,2560]{2,1,0:T(8,128)(2,1)S(1)}, bf16[2,16,2560]{2,1,0:T(8,128)(2,1)S(1)}, u32[]{:S(2)}, u32[]{:S(2)}) %collective-permute-start.13) | collective-permute-done | bytes 163872 | tf_op jit(solution)/shard_map/ppermute | solution.py:26
  185.8 1.4 collective-permute-done.12
  187.2 5.1 %collective-permute-done.11 = bf16[2,16,2560]{2,1,0:T(8,128)(2,1)S(1)} collective-permute-done((bf16[2,16,2560]{2,1,0:T(8,128)(2,1)S(1)}, bf16[2,16,2560]{2,1,0:T(8,128)(2,1)S(1)}, u32[]{:S(2)}, u32[]{:S(2)}) %collective-permute-start.11) | collective-permute-done | bytes 163872 | tf_op jit(solution)/shard_map/ppermute | solution.py:26
  192.3 1.0 fusion.1
  193.3 0.8 collective-permute-start.14
  194.2 0.6 copy.20
  194.8 1.4 reshape.57
  196.4 0.8 copy.21
  197.1 0.8 copy.22
  197.9 0.7 pad_maximum_fusion.2
  (48 shorter events, 2.8 us)
Async XLA Ops:
  7.2 18.6 %copy-start.2 = (bf16[1,128,5120]{2,1,0:T(8,128)(2,1)S(1)}, bf16[1,128,5120]{2,1,0:T(8,128)(2,1)}, u32[]{:S(2)}) copy-start(bf16[1,128,5120]{2,1,0:T(8,128)(2,1)} %param.11) | copy-start | bytes 3932164
  7.2 107.4 %all-gather.3.cloned.1.call-start = ((), (), s32[]{:S(2)}) async-start(), calls=%async_computation.5 | async-start | bytes 5898240 | tf_op jit(solution)/shard_map/all_gather | solution.py:245
  8.3 4.3 %collective-permute-start.1 = (bf16[16,2560]{1,0:T(8,128)(2,1)S(1)}, bf16[16,2560]{1,0:T(8,128)(2,1)S(1)}, u32[]{:S(2)}, u32[]{:S(2)}) collective-permute-start(bf16[16,2560]{1,0:T(8,128)(2,1)S(1)} %get-tuple-element.34), channel_id=1, source_target_pairs={{0,32},{32,0},{1,33},{33,1},{2,34},{34,2},{3,35},{35,3},{4,36},{36... | collective-permute-start | bytes 245768 | tf_op jit(solution)/shard_map/ppermute | solution.py:34
  12.5 5.5 %collective-permute-start.4 = (bf16[2,16,2560]{2,1,0:T(8,128)(2,1)S(1)}, bf16[2,16,2560]{2,1,0:T(8,128)(2,1)S(1)}, u32[]{:S(2)}, u32[]{:S(2)}) collective-permute-start(bf16[2,16,2560]{2,1,0:T(8,128)(2,1)S(1)} %get-tuple-element.32), channel_id=1, source_target_pairs={{0,24},{8,0},{16,8},{24,16},{1,25},{9,1},{17,9},{25,17},{2,26},{10... | collective-permute-start | bytes 491528 | tf_op jit(solution)/shard_map/ppermute | solution.py:26
  13.6 6.7 %collective-permute-start.3 = (bf16[2,16,2560]{2,1,0:T(8,128)(2,1)S(1)}, bf16[2,16,2560]{2,1,0:T(8,128)(2,1)S(1)}, u32[]{:S(2)}, u32[]{:S(2)}) collective-permute-start(bf16[2,16,2560]{2,1,0:T(8,128)(2,1)S(1)} %get-tuple-element.32), channel_id=1, source_target_pairs={{0,16},{8,24},{16,0},{24,8},{1,17},{9,25},{17,1},{25,9},{2,18},{10... | collective-permute-start | bytes 491528 | tf_op jit(solution)/shard_map/ppermute | solution.py:26
  14.0 10.8 %collective-permute-start.2 = (bf16[2,16,2560]{2,1,0:T(8,128)(2,1)S(1)}, bf16[2,16,2560]{2,1,0:T(8,128)(2,1)S(1)}, u32[]{:S(2)}, u32[]{:S(2)}) collective-permute-start(bf16[2,16,2560]{2,1,0:T(8,128)(2,1)S(1)} %get-tuple-element.32), channel_id=1, source_target_pairs={{0,8},{8,16},{16,24},{24,0},{1,9},{9,17},{17,25},{25,1},{2,10},{10... | collective-permute-start | bytes 491528 | tf_op jit(solution)/shard_map/ppermute | solution.py:26
  25.8 154.2 %reduce-scatter.2.cloned.1.call-start = ((), (), s32[]{:S(2)}) async-start(), calls=%async_computation.4 | async-start | bytes 5898240 | tf_op jit(solution)/shard_map/reduce_scatter | solution.py:272
  25.9 5.2 %copy-start.3 = (bf16[1,128,32,128]{3,2,1,0:T(8,128)(2,1)S(1)}, bf16[1,128,32,128]{3,2,1,0:T(8,128)(2,1)}, u32[]{:S(2)}) copy-start(bf16[1,128,32,128]{3,2,1,0:T(8,128)(2,1)} %param.10) | copy-start | bytes 3145732
  25.9 2.3 %collective-permute-start = (bf16[128,2560]{1,0:T(8,128)(2,1)S(1)}, bf16[128,2560]{1,0:T(8,128)(2,1)S(1)}, u32[]{:S(2)}, u32[]{:S(2)}) collective-permute-start(bf16[128,2560]{1,0:T(8,128)(2,1)S(1)} %get-tuple-element.25), channel_id=1, source_target_pairs={{0,32},{32,0},{1,33},{33,1},{2,34},{34,2},{3,35},{35,3},{4,36},{36... | collective-permute-start | bytes 1966088 | tf_op jit(solution)/shard_map/ppermute | solution.py:34
  28.3 3.4 %copy-start.1 = (bf16[256,2560]{1,0:T(8,128)(2,1)}, bf16[256,2560]{1,0:T(8,128)(2,1)S(1)}, u32[]{:S(2)}) copy-start(bf16[256,2560]{1,0:T(8,128)(2,1)S(1)} %pad_maximum_fusion.own) | copy-start | bytes 3932164
  28.3 48.5 %collective-permute-start.5 = (bf16[256,2560]{1,0:T(8,128)(2,1)S(1)}, bf16[256,2560]{1,0:T(8,128)(2,1)}, u32[]{:S(2)}, u32[]{:S(2)}) collective-permute-start(bf16[256,2560]{1,0:T(8,128)(2,1)S(1)} %pad_maximum_fusion.own), channel_id=1, source_target_pairs={{0,64},{64,128},{128,192},{192,0},{1,65},{65,129},{129,193},{193,1... | collective-permute-start | bytes 3932168 | tf_op jit(solution)/shard_map/ppermute | solution.py:26
  29.6 47.2 %collective-permute-start.6 = (bf16[256,2560]{1,0:T(8,128)(2,1)S(1)}, bf16[256,2560]{1,0:T(8,128)(2,1)}, u32[]{:S(2)}, u32[]{:S(2)}) collective-permute-start(bf16[256,2560]{1,0:T(8,128)(2,1)S(1)} %pad_maximum_fusion.own), channel_id=1, source_target_pairs={{0,192},{64,0},{128,64},{192,128},{1,193},{65,1},{129,65},{193,129... | collective-permute-start | bytes 3932168 | tf_op jit(solution)/shard_map/ppermute | solution.py:26
  31.7 41.4 %copy-start.6 = (bf16[1,128,4,128]{3,2,1,0:T(4,128)(2,1)S(1)}, bf16[1,128,4,128]{3,2,1,0:T(4,128)(2,1)}, u32[]{:S(2)}) copy-start(bf16[1,128,4,128]{3,2,1,0:T(4,128)(2,1)} %param.9) | copy-start | bytes 393220
  31.7 42.1 %copy-start.7 = (bf16[1,128,4,128]{3,2,1,0:T(4,128)(2,1)S(1)}, bf16[1,128,4,128]{3,2,1,0:T(4,128)(2,1)}, u32[]{:S(2)}) copy-start(bf16[1,128,4,128]{3,2,1,0:T(4,128)(2,1)} %param.8) | copy-start | bytes 393220
  31.7 42.1 %copy-start.4 = (bf16[1,128,32,128]{3,2,1,0:T(8,128)(2,1)S(1)}, bf16[1,128,32,128]{3,2,1,0:T(8,128)(2,1)}, u32[]{:S(2)}) copy-start(bf16[1,128,32,128]{3,2,1,0:T(8,128)(2,1)} %param.7) | copy-start | bytes 3145732
  71.9 10.6 %collective-permute-start.9 = (bf16[512,1024]{1,0:T(8,128)(2,1)}, bf16[512,1024]{1,0:T(8,128)(2,1)}, u32[]{:S(2)}, u32[]{:S(2)}) collective-permute-start(bf16[512,1024]{1,0:T(8,128)(2,1)} %bitcast.19.o_own), channel_id=1, source_target_pairs={{0,32},{32,0},{1,33},{33,1},{2,34},{34,2},{3,35},{35,3},{4,36},{36... | collective-permute-start | bytes 3145736 | tf_op jit(solution)/shard_map/ppermute | solution.py:34
  74.5 0.9 copy-start.5
  76.8 5.1 %copy-start.8 = (s32[1,3]{1,0:T(1,128)S(1)}, s32[1,3]{1,0:T(1,128)}, u32[]{:S(2)}) copy-start(s32[1,3]{1,0:T(1,128)} %param.13) | copy-start | bytes 40
  78.0 17.7 %collective-permute-start.7 = (bf16[128,2560]{1,0:T(8,128)(2,1)S(1)}, bf16[128,2560]{1,0:T(8,128)(2,1)S(1)}, u32[]{:S(2)}, u32[]{:S(2)}) collective-permute-start(bf16[128,2560]{1,0:T(8,128)(2,1)S(1)} %slice.51), channel_id=1, source_target_pairs={{0,64},{64,128},{128,192},{192,0},{1,65},{65,129},{129,193},{193,1... | collective-permute-start | bytes 1966088 | tf_op jit(solution)/shard_map/ppermute | solution.py:26
  80.0 16.1 %collective-permute-start.8 = (bf16[128,2560]{1,0:T(8,128)(2,1)S(1)}, bf16[128,2560]{1,0:T(8,128)(2,1)S(1)}, u32[]{:S(2)}, u32[]{:S(2)}) collective-permute-start(bf16[128,2560]{1,0:T(8,128)(2,1)S(1)} %slice.52), channel_id=1, source_target_pairs={{0,192},{64,0},{128,64},{192,128},{1,193},{65,1},{129,65},{193,129... | collective-permute-start | bytes 1966088 | tf_op jit(solution)/shard_map/ppermute | solution.py:26
  95.6 0.8 copy-start.10
  96.5 0.9 copy-start.11
  109.2 26.1 %all-to-all-start = ((bf16[8,128,768]{2,1,0:T(8,128)(2,1)}), bf16[8,128,768]{2,1,0:T(8,128)(2,1)S(1)}, u32[]{:S(2)}, u32[]{:S(2)}) async-start(bf16[8,128,768]{2,1,0:T(8,128)(2,1)} %maximum_bitcast_fusion), calls=%async_computation | async-start | bytes 3145728 | tf_op jit(solution)/shard_map/all_to_all | solution.py:267
  123.4 11.9 %collective-permute-start.10 = (bf16[1024,512]{1,0:T(8,128)(2,1)}, bf16[1024,512]{1,0:T(8,128)(2,1)S(1)}, u32[]{:S(2)}, u32[]{:S(2)}) collective-permute-start(bf16[1024,512]{1,0:T(8,128)(2,1)} %shard_map.104), channel_id=1, source_target_pairs={{0,32},{32,0},{1,33},{33,1},{2,34},{34,2},{3,35},{35,3},{4,36},{36... | collective-permute-start | bytes 3145736 | tf_op jit(solution)/shard_map/ppermute | solution.py:34
  135.3 1.2 copy-start
  135.3 1.5 copy-start.9
  181.1 4.7 %collective-permute-start.13 = (bf16[2,16,2560]{2,1,0:T(8,128)(2,1)S(1)}, bf16[2,16,2560]{2,1,0:T(8,128)(2,1)S(1)}, u32[]{:S(2)}, u32[]{:S(2)}) collective-permute-start(bf16[2,16,2560]{2,1,0:T(8,128)(2,1)S(1)} %get-tuple-element.27), channel_id=1, source_target_pairs={{0,24},{8,0},{16,8},{24,16},{1,25},{9,1},{17,9},{25,17},{2,26},{10... | collective-permute-start | bytes 491528 | tf_op jit(solution)/shard_map/ppermute | solution.py:26
  181.4 5.8 %collective-permute-start.12 = (bf16[2,16,2560]{2,1,0:T(8,128)(2,1)S(1)}, bf16[2,16,2560]{2,1,0:T(8,128)(2,1)S(1)}, u32[]{:S(2)}, u32[]{:S(2)}) collective-permute-start(bf16[2,16,2560]{2,1,0:T(8,128)(2,1)S(1)} %get-tuple-element.28), channel_id=1, source_target_pairs={{0,16},{8,24},{16,0},{24,8},{1,17},{9,25},{17,1},{25,9},{2,18},{10... | collective-permute-start | bytes 491528 | tf_op jit(solution)/shard_map/ppermute | solution.py:26
  181.7 10.6 %collective-permute-start.11 = (bf16[2,16,2560]{2,1,0:T(8,128)(2,1)S(1)}, bf16[2,16,2560]{2,1,0:T(8,128)(2,1)S(1)}, u32[]{:S(2)}, u32[]{:S(2)}) collective-permute-start(bf16[2,16,2560]{2,1,0:T(8,128)(2,1)S(1)} %get-tuple-element.26), channel_id=1, source_target_pairs={{0,8},{8,16},{16,24},{24,0},{1,9},{9,17},{17,25},{25,1},{2,10},{10... | collective-permute-start | bytes 491528 | tf_op jit(solution)/shard_map/ppermute | solution.py:26
  193.3 4.5 %collective-permute-start.14 = (f32[16,2560]{1,0:T(8,128)S(1)}, f32[16,2560]{1,0:T(8,128)S(1)}, u32[]{:S(2)}, u32[]{:S(2)}) collective-permute-start(f32[16,2560]{1,0:T(8,128)S(1)} %select_bitcast_fusion), channel_id=1, source_target_pairs={{0,32},{32,0},{1,33},{33,1},{2,34},{34,2},{3,35},{35,3},{4,36},{36... | collective-permute-start | bytes 491528 | tf_op jit(solution)/shard_map/ppermute | solution.py:34
Sparse Core Ops, SparseCore 0:
  25.9 64.8 all-gather.2
  109.3 66.0 reduce-scatter.1

commit v2 on v1

--- a/solution.py
+++ b/solution.py
@@ -12,6 +12,8 @@
 TOK = 128
 QB = 256
 COLS = 512
+PCOLS = 1280
+SPLIT = 3
 F32 = jnp.float32
 BF16 = jnp.bfloat16
 VMEM = 56 * 1024 * 1024
@@ -34,10 +36,12 @@
     return lax.ppermute(value, "core", [(0, 1), (1, 0)])
 
 
-def weight_kernel(factor, info, own, prev, succ, far0, far1, o_own, o_sib, term, rows, turned):
+def weight_kernel(factor, info, own, prev, succ, far0, far1, o_own, o_sib, *outs):
+    z_first, *y_first, rows, turned, product = outs
     here, y = info[0], info[1]
-
-    @pl.when(pl.program_id(0) == 0)
+    step = pl.program_id(0)
+
+    @pl.when(step == 0)
     def _():
         turned[:, :512] = o_own[...].T
         turned[:, 512:] = o_sib[...].T
@@ -53,32 +57,53 @@
     put(lax.rem(here + 2, 4), 0, far0[...])
     put(lax.rem(here + 2, 4), 1, far1[...])
     for part in range(4):
-        product = jnp.dot(
-            turned[part * 256 : part * 256 + 256, :], rows[...], preferred_element_type=F32
-        )
-        product = (product * factor).astype(BF16)
-        for at in range(16):
-            f = part % 2 * 16 + at
-            ry = lax.rem(f // 8 - y + 4, 4)
-            term[f % 8, ry, part // 2] = product[at * 16 : at * 16 + 16, :]
+        block = slice(part * 256, part * 256 + 256)
+        term = jnp.dot(turned[block, :], rows[...], preferred_element_type=F32)
+        product[block, :] = (term * factor).astype(BF16)
+
+    def take(kk, r, at):
+        row = kk * 512 + (lax.rem(y + r, 4) * 8 + at) * 16
+        return product[pl.ds(pl.multiple_of(row, 16), 16), :]
+
+    @pl.when(step < SPLIT)
+    def _():
+        for at in range(8):
+            for r in range(4):
+                for kk in range(2):
+                    z_first[at, r, kk] = take(kk, r, at)
+
+    @pl.when(step >= SPLIT)
+    def _():
+        for at in range(8):
+            for r in range(4):
+                for kk in range(2):
+                    y_first[r][at, kk] = take(kk, r, at)
 
 
 def weight_product(info, parts, o_own, o_sib, factor):
+    early, late = SPLIT * COLS, 2560 - SPLIT * COLS
     grid_spec = pltpu.PrefetchScalarGridSpec(
         num_scalar_prefetch=1,
         grid=(2560 // COLS,),
         in_specs=[pl.BlockSpec((p.shape[0], COLS), lambda n, info: (0, n)) for p in parts]
         + [pl.BlockSpec((512, 1024), lambda n, info: (0, 0))] * 2,
         out_specs=(
-            pl.BlockSpec((8, 4, 2, 16, COLS), lambda n, info: (0, 0, 0, 0, n)),
+            pl.BlockSpec(
+                (8, 4, 2, 16, COLS), lambda n, info: (0, 0, 0, 0, jnp.minimum(n, SPLIT - 1))
+            ),
+            *[
+                pl.BlockSpec((8, 2, 16, COLS), lambda n, info: (0, 0, 0, jnp.maximum(n - SPLIT, 0)))
+                for _ in range(4)
+            ],
             pl.BlockSpec((1024, COLS), lambda n, info: (0, n)),
         ),
-        scratch_shapes=[pltpu.VMEM((1024, 1024), BF16)],
+        scratch_shapes=[pltpu.VMEM((1024, 1024), BF16), pltpu.VMEM((1024, COLS), BF16)],
     )
     return pl.pallas_call(
         functools.partial(weight_kernel, factor),
         out_shape=(
-            jax.ShapeDtypeStruct((8, 4, 2, 16, 2560), BF16),
+            jax.ShapeDtypeStruct((8, 4, 2, 16, early), BF16),
+            *[jax.ShapeDtypeStruct((8, 2, 16, late), BF16) for _ in range(4)],
             jax.ShapeDtypeStruct((1024, 2560), BF16),
         ),
         grid_spec=grid_spec,
@@ -121,13 +146,13 @@
 def project(info, rows, weight, rc, dtype):
     grid_spec = pltpu.PrefetchScalarGridSpec(
         num_scalar_prefetch=1,
-        grid=(2560 // COLS,),
+        grid=(2560 // PCOLS,),
         in_specs=[
-            pl.BlockSpec((1024, COLS), lambda n, info: (0, n)),
-            pl.BlockSpec((8, 4, None, 16, COLS), lambda n, info: (0, 0, rc, 0, n)),
+            pl.BlockSpec((1024, PCOLS), lambda n, info: (0, n)),
+            pl.BlockSpec((8, 4, None, 16, PCOLS), lambda n, info: (0, 0, rc, 0, n)),
         ],
         out_specs=pl.BlockSpec((1024, 512), lambda n, info: (0, 0)),
-        scratch_shapes=[pltpu.VMEM((512, COLS), BF16), pltpu.VMEM((1024, 512), F32)],
+        scratch_shapes=[pltpu.VMEM((512, PCOLS), BF16), pltpu.VMEM((1024, 512), F32)],
     )
     return pl.pallas_call(
         project_kernel,
@@ -135,14 +160,15 @@
         grid_spec=grid_spec,
         compiler_params=params(),
         cost_estimate=pl.CostEstimate(
-            flops=2 * 1024 * 512 * 2560, bytes_accessed=10 * 1024 * 1024, transcendentals=0
+            flops=1024 * 1024, bytes_accessed=1024 * 1024, transcendentals=0
         ),
     )(info, rows, weight)
 
 
-def attention_kernel(info, query, key, value, mine, theirs, o_own, o_sib, out, key_acc, value_acc):
+def attention_kernel(info, query, key, value, mine, theirs, o_own, o_sib, *outs):
+    *outs, out, key_acc, value_acc, turned = outs
     head = pl.program_id(0)
-    core = info[3]
+    here, core = info[0], info[3]
     ends = (info[4], info[4] + info[5], info[4] + info[5] + info[6])
     scale = 128 ** (-0.5)
 
@@ -150,6 +176,7 @@
     def _():
         key_acc[...] = jnp.zeros_like(key_acc)
         value_acc[...] = jnp.zeros_like(value_acc)
+        turned[...] = key[...].T
 
     for block in range(4):
         at = block * QB
@@ -173,24 +200,25 @@
             start = jnp.where(i >= end, end, start)
         j = begin + lax.broadcasted_iota(jnp.int32, (span, QB), 0)
         scores = lax.dot_general(k, q, (((1,), (1,)), ((), ())), preferred_element_type=F32)
-        scores = scores * (scale * math.log2(math.e))
         scores = jnp.where((j <= i) & (j >= start), scores, -1e30)
         top = jnp.max(scores, axis=0, keepdims=True)
-        raised = jnp.exp2(scores - top)
+        raised = jnp.exp2((scores - top) * (scale * math.log2(math.e)))
         soft = raised * (1.0 / jnp.sum(raised, axis=0, keepdims=True))
         value_acc[cols, :] += jnp.dot(soft.astype(BF16), grad, preferred_element_type=F32)
         grad_soft = lax.dot_general(v, grad, (((1,), (1,)), ((), ())), preferred_element_type=F32)
-        grad_scores = (soft * (grad_soft - delta) * scale).astype(BF16)
+        grad_scores = (soft * (grad_soft - delta)).astype(BF16)
         key_acc[cols, :] += jnp.dot(grad_scores, q, preferred_element_type=F32)
-        grad_query = lax.dot_general(
-            grad_scores, k, (((0,), (0,)), ((), ())), preferred_element_type=F32
-        )
+        grad_query = jnp.dot(turned[:, cols], grad_scores, preferred_element_type=F32).T * scale
         out[rows, pl.ds(pl.multiple_of(head * 128, 128), 128)] = grad_query.astype(BF16)
 
     @pl.when(head == 3)
     def _():
-        out[:, 512:640] = key_acc[...].astype(BF16)
+        out[:, 512:640] = (key_acc[...] * scale).astype(BF16)
         out[:, 640:768] = value_acc[...].astype(BF16)
+        for step in range(4):
+            for rc in range(2):
+                row = lax.rem(here + step, 4) * 256 + (core if rc == 0 else 1 - core) * TOK
+                outs[step][rc] = out[pl.ds(pl.multiple_of(row, TOK), TOK), :]
 
 
 def attention(info, packed, mine, theirs, o_own, o_sib):
@@ -206,12 +234,17 @@
             pl.BlockSpec((512, 128), lambda h, info: (0, info[3] * 4 + h)),
             pl.BlockSpec((512, 128), lambda h, info: (0, info[3] * 4 + h)),
         ],
-        out_specs=pl.BlockSpec((1024, 768), lambda h, info: (0, 0)),
-        scratch_shapes=[pltpu.VMEM((1024, 128), F32), pltpu.VMEM((1024, 128), F32)],
+        out_specs=[pl.BlockSpec((2, TOK, 768), lambda h, info: (0, 0, 0))] * 4,
+        scratch_shapes=[
+            pltpu.VMEM((1024, 768), BF16),
+            pltpu.VMEM((1024, 128), F32),
+            pltpu.VMEM((1024, 128), F32),
+            pltpu.VMEM((128, 1024), BF16),
+        ],
     )
     return pl.pallas_call(
         attention_kernel,
-        out_shape=jax.ShapeDtypeStruct((1024, 768), BF16),
+        out_shape=[jax.ShapeDtypeStruct((2, TOK, 768), BF16)] * 4,
         grid_spec=grid_spec,
         compiler_params=params(),
         cost_estimate=pl.CostEstimate(
@@ -220,6 +253,37 @@
             transcendentals=4 * 10 * 256 * 256,
         ),
     )(info, packed, packed, packed, mine, theirs, o_own, o_sib)
+
+
+def merge_kernel(info, *refs):
+    *near, far, queries, keys, values = refs
+    here, core = info[0], info[3]
+    for step in range(4):
+        chip = lax.rem(here - step + 4, 4)
+        mine, theirs = near[step][0], far[step]
+        spot = chip * 1024 + core * 512
+        queries[:, pl.ds(pl.multiple_of(spot, 512), 512)] = mine[:, :512]
+        spot = chip * 1024 + (1 - core) * 512
+        queries[:, pl.ds(pl.multiple_of(spot, 512), 512)] = theirs[:, :512]
+        both = mine[:, 512:].astype(F32) + theirs[:, 512:].astype(F32)
+        spot = pl.ds(pl.multiple_of(chip * 128, 128), 128)
+        keys[:, spot] = both[:, :128].astype(BF16)
+        values[:, spot] = both[:, 128:].astype(BF16)
+
+
+def merge(info, near, far):
+    whole = pl.BlockSpec(memory_space=pltpu.VMEM)
+    return pl.pallas_call(
+        merge_kernel,
+        out_shape=(
+            jax.ShapeDtypeStruct((TOK, 4096), BF16),
+            jax.ShapeDtypeStruct((TOK, 512), BF16),
+            jax.ShapeDtypeStruct((TOK, 512), BF16),
+        ),
+        in_specs=[pl.BlockSpec(memory_space=pltpu.SMEM)] + [whole] * 5,
+        out_specs=(whole, whole, whole),
+        compiler_params=params(),
+    )(info, *near, far)
 
 
 def add(*terms):
@@ -261,25 +325,35 @@
     )
     packed = jnp.transpose(packed, (1, 0, 2))
 
-    own = after(grad_chip, near)
+    own = after(grad_chip, near, o_own)
     prev, succ = shift(own, "x", 1), shift(own, "x", -1)
     prev, succ, packed = lax.optimization_barrier((prev, succ, packed))
     packed = lax.all_to_all(packed, ("x", "core"), split_axis=0, concat_axis=0, tiled=True)
     packed = packed.reshape(1024, 768)
     far0, far1 = shift(prev[:TOK], "x", 1), shift(succ[TOK:], "x", -1)
-    term, rows = weight_product(info, (own, prev, succ, far0, far1), o_own, o_sib, factor)
-
-    summed = lax.psum_scatter(term, "z", scatter_dimension=0, tiled=True)[0]
+    z_first, *y_first, rows = weight_product(
+        info, (own, prev, succ, far0, far1), o_own, o_sib, factor
+    )
+
+    z_first = lax.psum_scatter(z_first, "z", scatter_dimension=0, tiled=True)[0]
+    y_first = [y_first[0]] + [shift(y_first[r], "y", r) for r in (1, 2, 3)]
 
     theirs = swap(project(info, rows, weight, 1, BF16))
     mine = project(info, rows, weight, 0, F32)
     grads = attention(info, packed, mine, theirs, o_own, o_sib)
-    back = lax.all_to_all(
-        grads.reshape(8, TOK, 768), ("x", "core"), split_axis=0, concat_axis=0, tiled=True
-    )
-
-    summed = after(summed, back)
-    summed = add(summed[0], *(shift(summed[r], "y", r) for r in (1, 2, 3)))
+    z_first = after(z_first, grads[0])
+    *y_first, g0, g1, g2, g3 = lax.optimization_barrier((*y_first, *grads))
+
+    back = [g0, shift(g1, "x", 1), shift(g2, "x", 2), shift(g3, "x", 3)]
+    grad_queries, grad_keys, grad_values = merge(
+        info, back, swap(jnp.stack([part[1] for part in back]))
+    )
+
+    y_first = add(*y_first).astype(BF16)
+    y_first = lax.all_to_all(y_first, "z", split_axis=0, concat_axis=0, tiled=True)
+    y_first = add(*(y_first[r] for r in range(8)))
+    z_first = add(z_first[0], *(shift(z_first[r], "y", r) for r in (1, 2, 3)))
+    summed = jnp.concatenate([z_first, y_first], axis=-1)
     keep = jnp.where(core == 0, summed[0], summed[1])
     give = jnp.where(core == 0, summed[1], summed[0])
     come = swap(give)
@@ -287,16 +361,10 @@
         [jnp.where(core == 0, keep, come), jnp.where(core == 0, come, keep)], axis=-1
     ).astype(F32)
 
-    grad_queries = jnp.transpose(back[:, :, :512], (1, 0, 2)).reshape(1, TOK, 32, 128)
-
-    def pair_sum(part):
-        part = part.astype(F32).reshape(4, 2, TOK, 128).sum(axis=1).astype(BF16)
-        return jnp.transpose(part, (1, 0, 2))[None]
-
     return (
-        grad_queries,
-        pair_sum(back[:, :, 512:640]),
-        pair_sum(back[:, :, 640:768]),
+        grad_queries.reshape(1, TOK, 32, 128),
+        grad_keys.reshape(1, TOK, 4, 128),
+        grad_values.reshape(1, TOK, 4, 128),
         grad_out_weight,
     )
 

time: 206 us -> 207 us (level)
  blocking collectives: 65.3 us -> 0 us
  waiting for transfers between devices: 38.8 us -> 74.7 us
  starting transfers between devices: 20.7 us -> 45.1 us
  other arithmetic: 5.36 us -> 8.58 us
  local copies, waits for them, and re-layouts: 13.2 us -> 15.3 us
    all_to_all x2 -> x0, blocking collectives: 65.3 us -> none  [the longest x1 40.2 us: per_device(): lax.all_to_all(o_split, 'x', split_axis=0, concat_axis=0, tiled=True)]
    all_to_all x0 -> x2, waiting for transfers between devices: none -> 22 us  [the longest x1 13.3 us: per_device(): lax.all_to_all(o_split, 'x', split_axis=0, concat_axis=0, tiled=True)]
    ppermute x10 -> x16, waiting for transfers between devices: 33.4 us -> 47.9 us  [shift(): lax.ppermute(value, axis, [(i, (i + by) % size) for i in range(size)])]
    all_to_all x0 -> x2, starting transfers between devices: none -> 12.6 us  [the longest x1 8.34 us: per_device(): lax.all_to_all(y_first, 'z', split_axis=0, concat_axis=0, tiled=True)]
    ppermute x10 -> x16, starting transfers between devices: 9.25 us -> 16.1 us  [shift(): lax.ppermute(value, axis, [(i, (i + by) % size) for i in range(size)])]
    pallas_call x2, Pallas kernels: 18 us -> 15.2 us  [project(): pl.pallas_call(project_kernel, out_shape=jax.ShapeDtypeStruct((1024, 512)...]
    ppermute x5 -> x6, starting transfers between devices: 5.95 us -> 8.46 us  [swap(): return lax.ppermute(value, 'core', [(0, 1), (1, 0)])]
    all_to_all x1, starting transfers between devices: 5.4 us -> 7.91 us  [per_device(): lax.all_to_all(packed, ('x', 'core'), split_axis=0, concat_axis=0, tiled=...]
  transfers between devices with their start and end apart: 18 -> 27, of which waited for: 11 -> 13; matrix products, arithmetic and copies ran while one was open for 5% -> 7% of each run, Pallas kernels for 23% -> 22%
where the time goes in v2:
time: 207 us; the launch traced here: 206 us
  waiting for transfers between devices  74.7 us (36%)
  Pallas kernels  47.9 us (23%)
  starting transfers between devices  45.1 us (22%)
  local copies, waits for them, and re-layouts  15.3 us (7%)
  between operations  14.4 us (7%)
  other arithmetic  8.58 us (4%)
    ppermute x16, waiting for transfers between devices, shift(): lax.ppermute(value, axis, [(i, (i + by) % size) for i in range(size)])  47.9 us
    pallas_call x1, Pallas kernels, attention(): pl.pallas_call(attention_kernel, out_shape=[jax.ShapeDtypeStruct((2, TOK,...  16.9 us
    ppermute x16, starting transfers between devices, shift(): lax.ppermute(value, axis, [(i, (i + by) % size) for i in range(size)])  16.1 us
    pallas_call x2, Pallas kernels, project(): pl.pallas_call(project_kernel, out_shape=jax.ShapeDtypeStruct((1024, 512)...  15.2 us
    all_to_all x1, waiting for transfers between devices, per_device(): lax.all_to_all(o_split, 'x', split_axis=0, concat_axis=0, tiled=True)  13.3 us
    pallas_call x1, Pallas kernels, weight_product(): pl.pallas_call(functools.partial(weight_kernel, factor), out_shape=(jax.S...  13 us
    all_to_all x1, waiting for transfers between devices, per_device(): lax.all_to_all(y_first, 'z', split_axis=0, concat_axis=0, tiled=True)  8.68 us
    ppermute x6, starting transfers between devices, swap(): return lax.ppermute(value, 'core', [(0, 1), (1, 0)])  8.46 us
  transfers between devices with their start and end apart: 27, of which 13 were waited for; matrix products, arithmetic and copies ran while one was open for 7% of the time, Pallas kernels for 22%

profile of v2, /device:TPU:1, one launch (start us, length us, event | category | flops | bytes accessed | tf_op | source)
XLA Modules:
  0.0 206.0 jit_solution(83778714705527501)
XLA Ops:
  7.2 1.0 select_bitcast_fusion.1
  8.3 3.3 %collective-permute-start.1 = (bf16[16,2560]{1,0:T(8,128)(2,1)S(1)}, bf16[16,2560]{1,0:T(8,128)(2,1)S(1)}, u32[]{:S(2)}, u32[]{:S(2)}) collective-permute-start(bf16[16,2560]{1,0:T(8,128)(2,1)S(1)} %get-tuple-element.66), channel_id=1, source_target_pairs={{0,32},{32,0},{1,33},{33,1},{2,34},{34,2},{3,35},{35,3},{4,36},{36... | collective-permute-start | bytes 245768 | tf_op jit(solution)/shard_map/ppermute | solution.py:36
  11.6 0.9 collective-permute-done.1
  12.5 1.1 collective-permute-start.4
  14.7 3.4 %collective-permute-done.4 = bf16[2,16,2560]{2,1,0:T(8,128)(2,1)S(1)} collective-permute-done((bf16[2,16,2560]{2,1,0:T(8,128)(2,1)S(1)}, bf16[2,16,2560]{2,1,0:T(8,128)(2,1)S(1)}, u32[]{:S(2)}, u32[]{:S(2)}) %collective-permute-start.4) | collective-permute-done | bytes 163872 | tf_op jit(solution)/shard_map/ppermute | solution.py:28
  18.1 2.2 %collective-permute-done.3 = bf16[2,16,2560]{2,1,0:T(8,128)(2,1)S(1)} collective-permute-done((bf16[2,16,2560]{2,1,0:T(8,128)(2,1)S(1)}, bf16[2,16,2560]{2,1,0:T(8,128)(2,1)S(1)}, u32[]{:S(2)}, u32[]{:S(2)}) %collective-permute-start.3) | collective-permute-done | bytes 163872 | tf_op jit(solution)/shard_map/ppermute | solution.py:28
  20.3 4.5 %collective-permute-done.2 = bf16[2,16,2560]{2,1,0:T(8,128)(2,1)S(1)} collective-permute-done((bf16[2,16,2560]{2,1,0:T(8,128)(2,1)S(1)}, bf16[2,16,2560]{2,1,0:T(8,128)(2,1)S(1)}, u32[]{:S(2)}, u32[]{:S(2)}) %collective-permute-start.2) | collective-permute-done | bytes 163872 | tf_op jit(solution)/shard_map/ppermute | solution.py:28
  24.8 0.9 pad_maximum_fusion.2
  25.7 0.9 broadcast_select_fusion.1
  27.4 1.3 copy.21
  28.7 4.2 %all-to-all-start = ((bf16[4,128,1024]{2,1,0:T(8,128)(2,1)}), bf16[4,128,1024]{2,1,0:T(8,128)(2,1)}, u32[]{:S(2)}, u32[]{:S(2)}) async-start(bf16[4,128,1024]{2,1,0:T(8,128)(2,1)} %bitcast.49), calls=%async_computation | async-start | bytes 2097152 | tf_op jit(solution)/shard_map/all_to_all | solution.py:312
  33.1 1.3 pad_maximum_fusion.own
  34.3 13.3 %all-to-all-done = bf16[4,128,1024]{2,1,0:T(8,128)(2,1)} async-done(((bf16[4,128,1024]{2,1,0:T(8,128)(2,1)}), bf16[4,128,1024]{2,1,0:T(8,128)(2,1)}, u32[]{:S(2)}, u32[]{:S(2)}) %all-to-all-start) | async-done | bytes 1048608 | tf_op jit(solution)/shard_map/all_to_all | solution.py:312
  47.9 2.4 %collective-permute-start.6 = (bf16[256,2560]{1,0:T(8,128)(2,1)S(1)}, bf16[256,2560]{1,0:T(8,128)(2,1)}, u32[]{:S(2)}, u32[]{:S(2)}) collective-permute-start(bf16[256,2560]{1,0:T(8,128)(2,1)S(1)} %pad_maximum_fusion.own), channel_id=1, source_target_pairs={{0,192},{64,0},{128,64},{192,128},{1,193},{65,1},{129,65},{193,129... | collective-permute-start | bytes 3932168 | tf_op jit(solution)/shard_map/ppermute | solution.py:28
  50.3 2.0 collective-permute-start.9
  54.7 1.3 maximum_bitcast_fusion
  56.0 21.8 %collective-permute-done.5.prev = bf16[256,2560]{1,0:T(8,128)(2,1)} collective-permute-done((bf16[256,2560]{1,0:T(8,128)(2,1)S(1)}, bf16[256,2560]{1,0:T(8,128)(2,1)}, u32[]{:S(2)}, u32[]{:S(2)}) %collective-permute-start.5) | collective-permute-done | bytes 1310752 | tf_op jit(solution)/shard_map/ppermute | solution.py:28
  77.8 1.1 slice.78
  79.0 1.1 slice.79
  80.1 2.7 %collective-permute-start.8 = (bf16[128,2560]{1,0:T(8,128)(2,1)S(1)}, bf16[128,2560]{1,0:T(8,128)(2,1)S(1)}, u32[]{:S(2)}, u32[]{:S(2)}) collective-permute-start(bf16[128,2560]{1,0:T(8,128)(2,1)S(1)} %slice.79), channel_id=1, source_target_pairs={{0,192},{64,0},{128,64},{192,128},{1,193},{65,1},{129,65},{193,129... | collective-permute-start | bytes 1966088 | tf_op jit(solution)/shard_map/ppermute | solution.py:28
  83.5 10.6 %collective-permute-done.7.far0 = bf16[128,2560]{1,0:T(8,128)(2,1)S(1)} collective-permute-done((bf16[128,2560]{1,0:T(8,128)(2,1)S(1)}, bf16[128,2560]{1,0:T(8,128)(2,1)S(1)}, u32[]{:S(2)}, u32[]{:S(2)}) %collective-permute-start.7) | collective-permute-done | bytes 655392 | tf_op jit(solution)/shard_map/ppermute | solution.py:28
  94.9 0.8 copy-done.18
  95.7 13.0 %shard_map.102 = (bf16[8,4,2,16,1536]{4,3,2,1,0:T(8,128)(2,1)}, bf16[8,2,16,1024]{3,2,1,0:T(8,128)(2,1)}, bf16[8,2,16,1024]{3,2,1,0:T(8,128)(2,1)}, bf16[8,2,16,...) custom-call(s32[7]{0:T(128)} %concatenate.15.info, ...), custom_call_target="tpu_custom_call" | custom-call | flops 5368709120 | bytes 18874368 | tf_op jit(solution)/shard_map/pallas_call | solution.py:102
  108.8 7.9 %all-to-all-start.1 = ((bf16[8,128,768]{2,1,0:T(8,128)(2,1)}), bf16[8,128,768]{2,1,0:T(8,128)(2,1)S(1)}, u32[]{:S(2)}, u32[]{:S(2)}) async-start(bf16[8,128,768]{2,1,0:T(8,128)(2,1)} %maximum_bitcast_fusion), calls=%async_computation.1 | async-start | bytes 3145728 | tf_op jit(solution)/shard_map/all_to_all | solution.py:331
  116.7 7.4 %shard_map.104 = bf16[1024,512]{1,0:T(8,128)(2,1)} custom-call(s32[7]{0:T(128)} %concatenate.15.info, bf16[1024,2560]{1,0:T(8,128)(2,1)} %get-tuple-element.38.rows, bf16[8,4,2,16,2560]{4,3,2,1,0:T(8,128)(2,1)} %bitcast.50), custom_call_target="tpu_custom_call" | custom-call | flops 1048576 | bytes 1048576 | tf_op jit(solution)/shard_map/pallas_call | solution.py:157
  124.1 1.6 collective-permute-start.11
  125.6 1.1 collective-permute-start.12
  126.8 7.8 %shard_map.103.mine = f32[1024,512]{1,0:T(8,128)} custom-call(s32[7]{0:T(128)} %concatenate.15.info, bf16[1024,2560]{1,0:T(8,128)(2,1)} %get-tuple-element.38.rows, bf16[8,4,2,16,2560]{4,3,2,1,0:T(8,128)(2,1)} %bitcast.51), custom_call_target="tpu_custom_call" | custom-call | flops 1048576 | bytes 1048576 | tf_op jit(solution)/shard_map/pallas_call | solution.py:157
  134.6 2.8 %all-to-all-done.1 = bf16[8,128,768]{2,1,0:T(8,128)(2,1)S(1)} async-done(((bf16[8,128,768]{2,1,0:T(8,128)(2,1)}), bf16[8,128,768]{2,1,0:T(8,128)(2,1)S(1)}, u32[]{:S(2)}, u32[]{:S(2)}) %all-to-all-start.1) | async-done | bytes 1572896 | tf_op jit(solution)/shard_map/all_to_all | solution.py:331
  137.4 1.2 copy-done
  138.6 16.9 %shard_map.105 = (bf16[2,128,768]{2,1,0:T(8,128)(2,1)}, bf16[2,128,768]{2,1,0:T(8,128)(2,1)}, bf16[2,128,768]{2,1,0:T(8,128)(2,1)}, bf16[2,128,768]{2,1,0:T(8,128)(2,1)}) custom-call(s32[7]{0:T(128)} %concatenate.15.info, bf16[1024,768]{1,0:T(8,128)(2,1)} %bitcast.52, bf16[1024,768]{1,0:T(8,128)(2,1)} %bitcast.53, bf16[1024,768]{1,0:T(8,128)(2,1)} %bitcast.54, ...), custom_call_target="tpu_custom_call" | custom-call | flops 14000000000 | bytes 8388608 | tf_op jit(solution)/shard_map/pallas_call | solution.py:245
  155.5 1.2 add_convert_fusion
  156.7 8.3 %all-to-all-start.2 = ((bf16[8,2,16,1024]{3,2,1,0:T(8,128)(2,1)}), bf16[8,2,16,1024]{3,2,1,0:T(8,128)(2,1)S(1)}, u32[]{:S(2)}, u32[]{:S(2)}) async-start(bf16[8,2,16,1024]{3,2,1,0:T(8,128)(2,1)} %add_convert_fusion), calls=%async_computation.3 | async-start | bytes 1048576 | tf_op jit(solution)/shard_map/all_to_all | solution.py:353
  165.1 1.0 slice_bitcast_fusion.2
  166.8 0.9 collective-permute-start.18
  168.3 2.4 %collective-permute-start.15 = (bf16[2,128,768]{2,1,0:T(8,128)(2,1)S(1)}, bf16[2,128,768]{2,1,0:T(8,128)(2,1)S(1)}, u32[]{:S(2)}, u32[]{:S(2)}) collective-permute-start(bf16[2,128,768]{2,1,0:T(8,128)(2,1)S(1)} %copy-done.20), channel_id=1, source_target_pairs={{0,128},{64,192},{128,0},{192,64},{1,129},{65,193},{129,1},{193,65... | collective-permute-start | bytes 1179656 | tf_op jit(solution)/shard_map/ppermute | solution.py:28
  170.7 1.2 collective-permute-start.16
  171.9 1.1 collective-permute-done.18
  173.0 0.9 fusion.1
  173.9 8.7 %all-to-all-done.2 = bf16[8,2,16,1024]{3,2,1,0:T(8,128)(2,1)S(1)} async-done(((bf16[8,2,16,1024]{3,2,1,0:T(8,128)(2,1)}), bf16[8,2,16,1024]{3,2,1,0:T(8,128)(2,1)S(1)}, u32[]{:S(2)}, u32[]{:S(2)}) %all-to-all-start.2) | async-done | bytes 524320 | tf_op jit(solution)/shard_map/all_to_all | solution.py:353
  182.7 1.0 collective-permute-start.21
  183.7 4.2 %collective-permute-done.16.refs_3_ = bf16[2,128,768]{2,1,0:T(8,128)(2,1)S(1)} collective-permute-done((bf16[2,128,768]{2,1,0:T(8,128)(2,1)S(1)}, bf16[2,128,768]{2,1,0:T(8,128)(2,1)S(1)}, u32[]{:S(2)}, u32[]{:S(2)}) %collective-permute-start.16) | collective-permute-done | bytes 393248 | tf_op jit(solution)/shard_map/ppermute | solution.py:28
  188.1 1.6 collective-permute-start.17
  189.8 0.7 pad_maximum_fusion.3
  190.5 1.1 collective-permute-done.17.refs_4_
  191.6 0.9 copy-done.9
  192.5 2.8 %shard_map.106 = (bf16[128,4096]{1,0:T(8,128)(2,1)}, bf16[128,512]{1,0:T(8,128)(2,1)}, bf16[128,512]{1,0:T(8,128)(2,1)}) custom-call(s32[7]{0:T(128)} %concatenate.15.info, bf16[2,128,768]{2,1,0:T(8,128)(2,1)} %get-tuple-element.43.refs_0_, bf16[2,128,768]{2,1,0:T(8,128)(2,1)} %copy-done.6, bf16[2,128,768]{2,1,0:T(8,128)(2,1)} %copy-done.7, ...), custom_call_target="tpu_custom_call" | custom-call | tf_op jit(solution)/shard_map/pallas_call | solution.py:276
  195.3 2.5 %copy.19 = bf16[16,8,32,128]{3,2,1,0:T(8,128)(2,1)} copy(bf16[16,8,32,128]{3,1,2,0:T(8,128)(2,1)} %bitcast.59) | data formatting | bytes 2097152
  (89 shorter events, 9.3 us)
Async XLA Ops:
  7.2 18.6 %copy-start.2 = (bf16[1,128,5120]{2,1,0:T(8,128)(2,1)S(1)}, bf16[1,128,5120]{2,1,0:T(8,128)(2,1)}, u32[]{:S(2)}) copy-start(bf16[1,128,5120]{2,1,0:T(8,128)(2,1)} %param.11) | copy-start | bytes 3932164
  7.2 109.5 %all-gather.3.cloned.1.call-start = ((), (), s32[]{:S(2)}) async-start(), calls=%async_computation.5 | async-start | bytes 5898240 | tf_op jit(solution)/shard_map/all_gather | solution.py:309
  8.3 4.3 %collective-permute-start.1 = (bf16[16,2560]{1,0:T(8,128)(2,1)S(1)}, bf16[16,2560]{1,0:T(8,128)(2,1)S(1)}, u32[]{:S(2)}, u32[]{:S(2)}) collective-permute-start(bf16[16,2560]{1,0:T(8,128)(2,1)S(1)} %get-tuple-element.66), channel_id=1, source_target_pairs={{0,32},{32,0},{1,33},{33,1},{2,34},{34,2},{3,35},{35,3},{4,36},{36... | collective-permute-start | bytes 245768 | tf_op jit(solution)/shard_map/ppermute | solution.py:36
  12.5 5.5 %collective-permute-start.4 = (bf16[2,16,2560]{2,1,0:T(8,128)(2,1)S(1)}, bf16[2,16,2560]{2,1,0:T(8,128)(2,1)S(1)}, u32[]{:S(2)}, u32[]{:S(2)}) collective-permute-start(bf16[2,16,2560]{2,1,0:T(8,128)(2,1)S(1)} %get-tuple-element.64), channel_id=1, source_target_pairs={{0,24},{8,0},{16,8},{24,16},{1,25},{9,1},{17,9},{25,17},{2,26},{10... | collective-permute-start | bytes 491528 | tf_op jit(solution)/shard_map/ppermute | solution.py:28
  13.6 6.7 %collective-permute-start.3 = (bf16[2,16,2560]{2,1,0:T(8,128)(2,1)S(1)}, bf16[2,16,2560]{2,1,0:T(8,128)(2,1)S(1)}, u32[]{:S(2)}, u32[]{:S(2)}) collective-permute-start(bf16[2,16,2560]{2,1,0:T(8,128)(2,1)S(1)} %get-tuple-element.64), channel_id=1, source_target_pairs={{0,16},{8,24},{16,0},{24,8},{1,17},{9,25},{17,1},{25,9},{2,18},{10... | collective-permute-start | bytes 491528 | tf_op jit(solution)/shard_map/ppermute | solution.py:28
  14.0 10.8 %collective-permute-start.2 = (bf16[2,16,2560]{2,1,0:T(8,128)(2,1)S(1)}, bf16[2,16,2560]{2,1,0:T(8,128)(2,1)S(1)}, u32[]{:S(2)}, u32[]{:S(2)}) collective-permute-start(bf16[2,16,2560]{2,1,0:T(8,128)(2,1)S(1)} %get-tuple-element.64), channel_id=1, source_target_pairs={{0,8},{8,16},{16,24},{24,0},{1,9},{9,17},{17,25},{25,1},{2,10},{10... | collective-permute-start | bytes 491528 | tf_op jit(solution)/shard_map/ppermute | solution.py:28
  25.7 1.5 copy-start.3
  26.7 6.4 %collective-permute-start = (bf16[128,2560]{1,0:T(8,128)(2,1)}, bf16[128,2560]{1,0:T(8,128)(2,1)}, u32[]{:S(2)}, u32[]{:S(2)}) collective-permute-start(bf16[128,2560]{1,0:T(8,128)(2,1)} %get-tuple-element.57), channel_id=1, source_target_pairs={{0,32},{32,0},{1,33},{33,1},{2,34},{34,2},{3,35},{35,3},{4,36},{36... | collective-permute-start | bytes 1966088 | tf_op jit(solution)/shard_map/ppermute | solution.py:36
  28.7 18.9 %all-to-all-start = ((bf16[4,128,1024]{2,1,0:T(8,128)(2,1)}), bf16[4,128,1024]{2,1,0:T(8,128)(2,1)}, u32[]{:S(2)}, u32[]{:S(2)}) async-start(bf16[4,128,1024]{2,1,0:T(8,128)(2,1)} %bitcast.49), calls=%async_computation | async-start | bytes 2097152 | tf_op jit(solution)/shard_map/all_to_all | solution.py:312
  33.0 19.3 %copy-start.12 = (bf16[1,128,4,128]{3,2,1,0:T(4,128)(2,1)S(1)}, bf16[1,128,4,128]{3,2,1,0:T(4,128)(2,1)}, u32[]{:S(2)}) copy-start(bf16[1,128,4,128]{3,2,1,0:T(4,128)(2,1)} %param.9) | copy-start | bytes 393220
  33.0 20.0 %copy-start.13 = (bf16[1,128,4,128]{3,2,1,0:T(4,128)(2,1)S(1)}, bf16[1,128,4,128]{3,2,1,0:T(4,128)(2,1)}, u32[]{:S(2)}) copy-start(bf16[1,128,4,128]{3,2,1,0:T(4,128)(2,1)} %param.8) | copy-start | bytes 393220
  33.0 132.1 %reduce-scatter.2.cloned.1.call-start = ((), (), s32[]{:S(2)}) async-start(), calls=%async_computation.4 | async-start | bytes 3538944 | tf_op jit(solution)/shard_map/reduce_scatter | solution.py:338
  33.0 20.0 %copy-start.4 = (bf16[1,128,32,128]{3,2,1,0:T(8,128)(2,1)S(1)}, bf16[1,128,32,128]{3,2,1,0:T(8,128)(2,1)}, u32[]{:S(2)}) copy-start(bf16[1,128,32,128]{3,2,1,0:T(8,128)(2,1)} %param.7) | copy-start | bytes 3145732
  34.3 19.7 %copy-start.1 = (bf16[256,2560]{1,0:T(8,128)(2,1)}, bf16[256,2560]{1,0:T(8,128)(2,1)S(1)}, u32[]{:S(2)}) copy-start(bf16[256,2560]{1,0:T(8,128)(2,1)S(1)} %pad_maximum_fusion.own) | copy-start | bytes 3932164
  47.6 30.1 %collective-permute-start.5 = (bf16[256,2560]{1,0:T(8,128)(2,1)S(1)}, bf16[256,2560]{1,0:T(8,128)(2,1)}, u32[]{:S(2)}, u32[]{:S(2)}) collective-permute-start(bf16[256,2560]{1,0:T(8,128)(2,1)S(1)} %pad_maximum_fusion.own), channel_id=1, source_target_pairs={{0,64},{64,128},{128,192},{192,0},{1,65},{65,129},{129,193},{193,1... | collective-permute-start | bytes 3932168 | tf_op jit(solution)/shard_map/ppermute | solution.py:28
  47.9 29.9 %collective-permute-start.6 = (bf16[256,2560]{1,0:T(8,128)(2,1)S(1)}, bf16[256,2560]{1,0:T(8,128)(2,1)}, u32[]{:S(2)}, u32[]{:S(2)}) collective-permute-start(bf16[256,2560]{1,0:T(8,128)(2,1)S(1)} %pad_maximum_fusion.own), channel_id=1, source_target_pairs={{0,192},{64,0},{128,64},{192,128},{1,193},{65,1},{129,65},{193,129... | collective-permute-start | bytes 3932168 | tf_op jit(solution)/shard_map/ppermute | solution.py:28
  50.3 33.2 %collective-permute-start.9 = (bf16[512,1024]{1,0:T(8,128)(2,1)}, bf16[512,1024]{1,0:T(8,128)(2,1)}, u32[]{:S(2)}, u32[]{:S(2)}) collective-permute-start(bf16[512,1024]{1,0:T(8,128)(2,1)} %bitcast.13.o_own), channel_id=1, source_target_pairs={{0,32},{32,0},{1,33},{33,1},{2,34},{34,2},{3,35},{35,3},{4,36},{36... | collective-permute-start | bytes 3145736 | tf_op jit(solution)/shard_map/ppermute | solution.py:36
  53.7 0.9 copy-start.11
  56.0 26.9 %copy-start.16 = (s32[1,3]{1,0:T(1,128)S(1)}, s32[1,3]{1,0:T(1,128)}, u32[]{:S(2)}) copy-start(s32[1,3]{1,0:T(1,128)} %param.13) | copy-start | bytes 40
  78.9 15.1 %collective-permute-start.7 = (bf16[128,2560]{1,0:T(8,128)(2,1)S(1)}, bf16[128,2560]{1,0:T(8,128)(2,1)S(1)}, u32[]{:S(2)}, u32[]{:S(2)}) collective-permute-start(bf16[128,2560]{1,0:T(8,128)(2,1)S(1)} %slice.78), channel_id=1, source_target_pairs={{0,64},{64,128},{128,192},{192,0},{1,65},{65,129},{129,193},{193,1... | collective-permute-start | bytes 1966088 | tf_op jit(solution)/shard_map/ppermute | solution.py:28
  80.1 14.1 %collective-permute-start.8 = (bf16[128,2560]{1,0:T(8,128)(2,1)S(1)}, bf16[128,2560]{1,0:T(8,128)(2,1)S(1)}, u32[]{:S(2)}, u32[]{:S(2)}) collective-permute-start(bf16[128,2560]{1,0:T(8,128)(2,1)S(1)} %slice.79), channel_id=1, source_target_pairs={{0,192},{64,0},{128,64},{192,128},{1,193},{65,1},{129,65},{193,129... | collective-permute-start | bytes 1966088 | tf_op jit(solution)/shard_map/ppermute | solution.py:28
  94.9 0.8 copy-start.18
  108.8 28.6 %all-to-all-start.1 = ((bf16[8,128,768]{2,1,0:T(8,128)(2,1)}), bf16[8,128,768]{2,1,0:T(8,128)(2,1)S(1)}, u32[]{:S(2)}, u32[]{:S(2)}) async-start(bf16[8,128,768]{2,1,0:T(8,128)(2,1)} %maximum_bitcast_fusion), calls=%async_computation.1 | async-start | bytes 3145728 | tf_op jit(solution)/shard_map/all_to_all | solution.py:331
  124.1 13.3 %collective-permute-start.13 = (bf16[1024,512]{1,0:T(8,128)(2,1)}, bf16[1024,512]{1,0:T(8,128)(2,1)}, u32[]{:S(2)}, u32[]{:S(2)}) collective-permute-start(bf16[1024,512]{1,0:T(8,128)(2,1)} %shard_map.104), channel_id=1, source_target_pairs={{0,32},{32,0},{1,33},{33,1},{2,34},{34,2},{3,35},{35,3},{4,36},{36... | collective-permute-start | bytes 3145736 | tf_op jit(solution)/shard_map/ppermute | solution.py:36
  124.1 31.4 %collective-permute-start.10 = (bf16[8,2,16,1024]{3,2,1,0:T(8,128)(2,1)}, bf16[8,2,16,1024]{3,2,1,0:T(8,128)(2,1)S(1)}, u32[]{:S(2)}, u32[]{:S(2)}) collective-permute-start(bf16[8,2,16,1024]{3,2,1,0:T(8,128)(2,1)} %get-tuple-element.34), channel_id=1, source_target_pairs={{0,8},{8,16},{16,24},{24,0},{1,9},{9,17},{17,25},{25,1},{2,10},{10... | collective-permute-start | bytes 1572872 | tf_op jit(solution)/shard_map/ppermute | solution.py:28
  124.1 31.4 %collective-permute-start.11 = (bf16[8,2,16,1024]{3,2,1,0:T(8,128)(2,1)}, bf16[8,2,16,1024]{3,2,1,0:T(8,128)(2,1)S(1)}, u32[]{:S(2)}, u32[]{:S(2)}) collective-permute-start(bf16[8,2,16,1024]{3,2,1,0:T(8,128)(2,1)} %get-tuple-element.35), channel_id=1, source_target_pairs={{0,16},{8,24},{16,0},{24,8},{1,17},{9,25},{17,1},{25,9},{2,18},{10... | collective-permute-start | bytes 1572872 | tf_op jit(solution)/shard_map/ppermute | solution.py:28
  125.6 29.9 %collective-permute-start.12 = (bf16[8,2,16,1024]{3,2,1,0:T(8,128)(2,1)}, bf16[8,2,16,1024]{3,2,1,0:T(8,128)(2,1)S(1)}, u32[]{:S(2)}, u32[]{:S(2)}) collective-permute-start(bf16[8,2,16,1024]{3,2,1,0:T(8,128)(2,1)} %get-tuple-element.36), channel_id=1, source_target_pairs={{0,24},{8,0},{16,8},{24,16},{1,25},{9,1},{17,9},{25,17},{2,26},{10... | collective-permute-start | bytes 1572872 | tf_op jit(solution)/shard_map/ppermute | solution.py:28
  137.4 1.2 copy-start
  138.6 16.9 %copy-start.10 = (bf16[8,2,16,1024]{3,2,1,0:T(8,128)(2,1)S(1)}, bf16[8,2,16,1024]{3,2,1,0:T(8,128)(2,1)}, u32[]{:S(2)}) copy-start(bf16[8,2,16,1024]{3,2,1,0:T(8,128)(2,1)} %get-tuple-element.52) | copy-start | bytes 1572868
  155.5 12.1 %copy-start.19 = (bf16[2,128,768]{2,1,0:T(8,128)(2,1)S(1)}, bf16[2,128,768]{2,1,0:T(8,128)(2,1)}, u32[]{:S(2)}) copy-start(bf16[2,128,768]{2,1,0:T(8,128)(2,1)} %get-tuple-element.44) | copy-start | bytes 1179652
  156.7 11.6 %copy-start.20 = (bf16[2,128,768]{2,1,0:T(8,128)(2,1)S(1)}, bf16[2,128,768]{2,1,0:T(8,128)(2,1)}, u32[]{:S(2)}) copy-start(bf16[2,128,768]{2,1,0:T(8,128)(2,1)} %get-tuple-element.45) | copy-start | bytes 1179652
  156.7 14.0 %copy-start.21 = (bf16[2,128,768]{2,1,0:T(8,128)(2,1)S(1)}, bf16[2,128,768]{2,1,0:T(8,128)(2,1)}, u32[]{:S(2)}) copy-start(bf16[2,128,768]{2,1,0:T(8,128)(2,1)} %get-tuple-element.46) | copy-start | bytes 1179652
  156.7 27.0 %copy-start.5 = (bf16[2,128,768]{2,1,0:T(8,128)(2,1)S(1)}, bf16[2,128,768]{2,1,0:T(8,128)(2,1)}, u32[]{:S(2)}) copy-start(bf16[2,128,768]{2,1,0:T(8,128)(2,1)} %get-tuple-element.43.refs_0_) | copy-start | bytes 1179652
  156.7 25.9 %all-to-all-start.2 = ((bf16[8,2,16,1024]{3,2,1,0:T(8,128)(2,1)}), bf16[8,2,16,1024]{3,2,1,0:T(8,128)(2,1)S(1)}, u32[]{:S(2)}, u32[]{:S(2)}) async-start(bf16[8,2,16,1024]{3,2,1,0:T(8,128)(2,1)} %add_convert_fusion), calls=%async_computation.3 | async-start | bytes 1048576 | tf_op jit(solution)/shard_map/all_to_all | solution.py:353
  166.1 4.6 %collective-permute-start.20 = (bf16[2,16,1536]{2,1,0:T(8,128)(2,1)S(1)}, bf16[2,16,1536]{2,1,0:T(8,128)(2,1)S(1)}, u32[]{:S(2)}, u32[]{:S(2)}) collective-permute-start(bf16[2,16,1536]{2,1,0:T(8,128)(2,1)S(1)} %get-tuple-element.61), channel_id=1, source_target_pairs={{0,24},{8,0},{16,8},{24,16},{1,25},{9,1},{17,9},{25,17},{2,26},{10... | collective-permute-start | bytes 294920 | tf_op jit(solution)/shard_map/ppermute | solution.py:28
  166.5 5.4 %collective-permute-start.19 = (bf16[2,16,1536]{2,1,0:T(8,128)(2,1)S(1)}, bf16[2,16,1536]{2,1,0:T(8,128)(2,1)S(1)}, u32[]{:S(2)}, u32[]{:S(2)}) collective-permute-start(bf16[2,16,1536]{2,1,0:T(8,128)(2,1)S(1)} %get-tuple-element.62), channel_id=1, source_target_pairs={{0,16},{8,24},{16,0},{24,8},{1,17},{9,25},{17,1},{25,9},{2,18},{10... | collective-permute-start | bytes 294920 | tf_op jit(solution)/shard_map/ppermute | solution.py:28
  166.8 6.2 %collective-permute-start.18 = (bf16[2,16,1536]{2,1,0:T(8,128)(2,1)S(1)}, bf16[2,16,1536]{2,1,0:T(8,128)(2,1)S(1)}, u32[]{:S(2)}, u32[]{:S(2)}) collective-permute-start(bf16[2,16,1536]{2,1,0:T(8,128)(2,1)S(1)} %get-tuple-element.60), channel_id=1, source_target_pairs={{0,8},{8,16},{16,24},{24,0},{1,9},{9,17},{17,25},{25,1},{2,10},{10... | collective-permute-start | bytes 294920 | tf_op jit(solution)/shard_map/ppermute | solution.py:28
  167.6 20.3 %collective-permute-start.14 = (bf16[2,128,768]{2,1,0:T(8,128)(2,1)S(1)}, bf16[2,128,768]{2,1,0:T(8,128)(2,1)S(1)}, u32[]{:S(2)}, u32[]{:S(2)}) collective-permute-start(bf16[2,128,768]{2,1,0:T(8,128)(2,1)S(1)} %copy-done.19), channel_id=1, source_target_pairs={{0,64},{64,128},{128,192},{192,0},{1,65},{65,129},{129,193},{193,1... | collective-permute-start | bytes 1179656 | tf_op jit(solution)/shard_map/ppermute | solution.py:28
  168.3 19.6 %collective-permute-start.15 = (bf16[2,128,768]{2,1,0:T(8,128)(2,1)S(1)}, bf16[2,128,768]{2,1,0:T(8,128)(2,1)S(1)}, u32[]{:S(2)}, u32[]{:S(2)}) collective-permute-start(bf16[2,128,768]{2,1,0:T(8,128)(2,1)S(1)} %copy-done.20), channel_id=1, source_target_pairs={{0,128},{64,192},{128,0},{192,64},{1,129},{65,193},{129,1},{193,65... | collective-permute-start | bytes 1179656 | tf_op jit(solution)/shard_map/ppermute | solution.py:28
  170.7 17.1 %collective-permute-start.16 = (bf16[2,128,768]{2,1,0:T(8,128)(2,1)S(1)}, bf16[2,128,768]{2,1,0:T(8,128)(2,1)S(1)}, u32[]{:S(2)}, u32[]{:S(2)}) collective-permute-start(bf16[2,128,768]{2,1,0:T(8,128)(2,1)S(1)} %copy-done.21), channel_id=1, source_target_pairs={{0,192},{64,0},{128,64},{192,128},{1,193},{65,1},{129,65},{193,129... | collective-permute-start | bytes 1179656 | tf_op jit(solution)/shard_map/ppermute | solution.py:28
  182.7 7.0 %collective-permute-start.21 = (f32[16,2560]{1,0:T(8,128)S(1)}, f32[16,2560]{1,0:T(8,128)S(1)}, u32[]{:S(2)}, u32[]{:S(2)}) collective-permute-start(f32[16,2560]{1,0:T(8,128)S(1)} %select_bitcast_fusion), channel_id=1, source_target_pairs={{0,32},{32,0},{1,33},{33,1},{2,34},{34,2},{3,35},{35,3},{4,36},{36... | collective-permute-start | bytes 491528 | tf_op jit(solution)/shard_map/ppermute | solution.py:36
  187.9 1.9 copy-start.8
  187.9 1.9 copy-start.7
  187.9 2.6 %copy-start.6 = (bf16[2,128,768]{2,1,0:T(8,128)(2,1)}, bf16[2,128,768]{2,1,0:T(8,128)(2,1)S(1)}, u32[]{:S(2)}) copy-start(bf16[2,128,768]{2,1,0:T(8,128)(2,1)S(1)} %collective-permute-done.14.refs_1_) | copy-start | bytes 1179652
  188.1 3.6 %collective-permute-start.17 = (bf16[4,128,768]{2,1,0:T(8,128)(2,1)S(1)}, bf16[4,128,768]{2,1,0:T(8,128)(2,1)S(1)}, u32[]{:S(2)}, u32[]{:S(2)}) collective-permute-start(bf16[4,128,768]{2,1,0:T(8,128)(2,1)S(1)} %pad_maximum_fusion.1), channel_id=1, source_target_pairs={{0,32},{32,0},{1,33},{33,1},{2,34},{34,2},{3,35},{35,3},{4,36},{36... | collective-permute-start | bytes 2359304 | tf_op jit(solution)/shard_map/ppermute | solution.py:36
  191.6 0.9 copy-start.9
  195.3 2.5 %copy-start.15 = (bf16[128,512]{1,0:T(8,128)(2,1)S(1)}, bf16[128,512]{1,0:T(8,128)(2,1)}, u32[]{:S(2)}) copy-start(bf16[128,512]{1,0:T(8,128)(2,1)} %get-tuple-element.48) | copy-start | bytes 393220
  195.3 3.2 %copy-start.14 = (bf16[128,512]{1,0:T(8,128)(2,1)S(1)}, bf16[128,512]{1,0:T(8,128)(2,1)}, u32[]{:S(2)}) copy-start(bf16[128,512]{1,0:T(8,128)(2,1)} %get-tuple-element.49) | copy-start | bytes 393220
  (1 other events, 0.8 us)
Sparse Core Ops, SparseCore 0:
  25.8 64.8 all-gather.2
  108.9 47.3 reduce-scatter.1

commit v3 on v2

--- a/solution.py
+++ b/solution.py
@@ -13,7 +13,6 @@
 QB = 256
 COLS = 512
 PCOLS = 1280
-SPLIT = 3
 F32 = jnp.float32
 BF16 = jnp.bfloat16
 VMEM = 56 * 1024 * 1024
@@ -36,12 +35,10 @@
     return lax.ppermute(value, "core", [(0, 1), (1, 0)])
 
 
-def weight_kernel(factor, info, own, prev, succ, far0, far1, o_own, o_sib, *outs):
-    z_first, *y_first, rows, turned, product = outs
+def weight_kernel(factor, info, own, prev, succ, far0, far1, o_own, o_sib, term, rows, turned):
     here, y = info[0], info[1]
-    step = pl.program_id(0)
-
-    @pl.when(step == 0)
+
+    @pl.when(pl.program_id(0) == 0)
     def _():
         turned[:, :512] = o_own[...].T
         turned[:, 512:] = o_sib[...].T
@@ -57,59 +54,38 @@
     put(lax.rem(here + 2, 4), 0, far0[...])
     put(lax.rem(here + 2, 4), 1, far1[...])
     for part in range(4):
-        block = slice(part * 256, part * 256 + 256)
-        term = jnp.dot(turned[block, :], rows[...], preferred_element_type=F32)
-        product[block, :] = (term * factor).astype(BF16)
-
-    def take(kk, r, at):
-        row = kk * 512 + (lax.rem(y + r, 4) * 8 + at) * 16
-        return product[pl.ds(pl.multiple_of(row, 16), 16), :]
-
-    @pl.when(step < SPLIT)
-    def _():
-        for at in range(8):
-            for r in range(4):
-                for kk in range(2):
-                    z_first[at, r, kk] = take(kk, r, at)
-
-    @pl.when(step >= SPLIT)
-    def _():
-        for at in range(8):
-            for r in range(4):
-                for kk in range(2):
-                    y_first[r][at, kk] = take(kk, r, at)
+        product = jnp.dot(
+            turned[part * 256 : part * 256 + 256, :], rows[...], preferred_element_type=F32
+        )
+        product = (product * factor).astype(BF16)
+        for at in range(16):
+            f = part % 2 * 16 + at
+            ry = lax.rem(f // 8 - y + 4, 4)
+            term[f % 8, ry, part // 2] = product[at * 16 : at * 16 + 16, :]
 
 
 def weight_product(info, parts, o_own, o_sib, factor):
-    early, late = SPLIT * COLS, 2560 - SPLIT * COLS
     grid_spec = pltpu.PrefetchScalarGridSpec(
         num_scalar_prefetch=1,
         grid=(2560 // COLS,),
         in_specs=[pl.BlockSpec((p.shape[0], COLS), lambda n, info: (0, n)) for p in parts]
         + [pl.BlockSpec((512, 1024), lambda n, info: (0, 0))] * 2,
         out_specs=(
-            pl.BlockSpec(
-                (8, 4, 2, 16, COLS), lambda n, info: (0, 0, 0, 0, jnp.minimum(n, SPLIT - 1))
-            ),
-            *[
-                pl.BlockSpec((8, 2, 16, COLS), lambda n, info: (0, 0, 0, jnp.maximum(n - SPLIT, 0)))
-                for _ in range(4)
-            ],
+            pl.BlockSpec((8, 4, 2, 16, COLS), lambda n, info: (0, 0, 0, 0, n)),
             pl.BlockSpec((1024, COLS), lambda n, info: (0, n)),
         ),
-        scratch_shapes=[pltpu.VMEM((1024, 1024), BF16), pltpu.VMEM((1024, COLS), BF16)],
+        scratch_shapes=[pltpu.VMEM((1024, 1024), BF16)],
     )
     return pl.pallas_call(
         functools.partial(weight_kernel, factor),
         out_shape=(
-            jax.ShapeDtypeStruct((8, 4, 2, 16, early), BF16),
-            *[jax.ShapeDtypeStruct((8, 2, 16, late), BF16) for _ in range(4)],
+            jax.ShapeDtypeStruct((8, 4, 2, 16, 2560), BF16),
             jax.ShapeDtypeStruct((1024, 2560), BF16),
         ),
         grid_spec=grid_spec,
         compiler_params=params(),
         cost_estimate=pl.CostEstimate(
-            flops=2 * 1024 * 1024 * 2560, bytes_accessed=18 * 1024 * 1024, transcendentals=0
+            flops=1024 * 1024, bytes_accessed=1024 * 1024, transcendentals=0
         ),
     )(info, *parts, o_own, o_sib)
 
@@ -306,15 +282,14 @@
     weight_mine, weight_theirs = halves(out_weight)
     weight_pair = jnp.stack([weight_mine, swap(weight_theirs)])
     near = jnp.stack([weight_pair] + [shift(weight_pair, "y", r) for r in (1, 2, 3)])
-    weight = lax.all_gather(near, "z", axis=0, tiled=False)
-
     o_split = jnp.transpose(attn_out.reshape(TOK, 4, 1024), (1, 0, 2))
     o_own = lax.all_to_all(o_split, "x", split_axis=0, concat_axis=0, tiled=True)
     o_own = o_own.reshape(512, 1024)
-    o_sib = swap(o_own)
 
     grad_mine, grad_theirs = halves(out_grad[0])
     grad_chip = jnp.concatenate([grad_mine, swap(grad_theirs)], axis=0)
+    weight = lax.all_gather(after(near, grad_chip), "z", axis=0, tiled=False)
+
     packed = jnp.concatenate(
         [
             queries.reshape(TOK, 8, 512),
@@ -325,35 +300,28 @@
     )
     packed = jnp.transpose(packed, (1, 0, 2))
 
-    own = after(grad_chip, near, o_own)
+    own = after(grad_chip, weight_pair, o_split)
     prev, succ = shift(own, "x", 1), shift(own, "x", -1)
-    prev, succ, packed = lax.optimization_barrier((prev, succ, packed))
+    prev, succ, packed, o_own = lax.optimization_barrier((prev, succ, packed, o_own))
     packed = lax.all_to_all(packed, ("x", "core"), split_axis=0, concat_axis=0, tiled=True)
     packed = packed.reshape(1024, 768)
     far0, far1 = shift(prev[:TOK], "x", 1), shift(succ[TOK:], "x", -1)
-    z_first, *y_first, rows = weight_product(
-        info, (own, prev, succ, far0, far1), o_own, o_sib, factor
-    )
-
-    z_first = lax.psum_scatter(z_first, "z", scatter_dimension=0, tiled=True)[0]
-    y_first = [y_first[0]] + [shift(y_first[r], "y", r) for r in (1, 2, 3)]
+    o_sib = swap(o_own)
+    term, rows = weight_product(info, (own, prev, succ, far0, far1), o_own, o_sib, factor)
+
+    summed = lax.psum_scatter(term, "z", scatter_dimension=0, tiled=True)[0]
 
     theirs = swap(project(info, rows, weight, 1, BF16))
     mine = project(info, rows, weight, 0, F32)
     grads = attention(info, packed, mine, theirs, o_own, o_sib)
-    z_first = after(z_first, grads[0])
-    *y_first, g0, g1, g2, g3 = lax.optimization_barrier((*y_first, *grads))
-
-    back = [g0, shift(g1, "x", 1), shift(g2, "x", 2), shift(g3, "x", 3)]
+
+    back = [grads[0]] + [shift(grads[r], "x", r) for r in (1, 2, 3)]
     grad_queries, grad_keys, grad_values = merge(
         info, back, swap(jnp.stack([part[1] for part in back]))
     )
 
-    y_first = add(*y_first).astype(BF16)
-    y_first = lax.all_to_all(y_first, "z", split_axis=0, concat_axis=0, tiled=True)
-    y_first = add(*(y_first[r] for r in range(8)))
-    z_first = add(z_first[0], *(shift(z_first[r], "y", r) for r in (1, 2, 3)))
-    summed = jnp.concatenate([z_first, y_first], axis=-1)
+    summed = after(summed, *back[1:])
+    summed = add(summed[0], *(shift(summed[r], "y", r) for r in (1, 2, 3)))
     keep = jnp.where(core == 0, summed[0], summed[1])
     give = jnp.where(core == 0, summed[1], summed[0])
     come = swap(give)

time: 207 us -> 206 us (level)
  starting transfers between devices: 45.1 us -> 30.8 us
  waiting for transfers between devices: 74.7 us -> 87.5 us
  local copies, waits for them, and re-layouts: 15.3 us -> 18.1 us
    all_to_all x1, waiting for transfers between devices: 13.3 us -> 32.3 us  [per_device(): lax.all_to_all(o_split, 'x', split_axis=0, concat_axis=0, tiled=True)]
    all_to_all x1 -> x0, waiting for transfers between devices: 8.68 us -> none  [per_device(): lax.all_to_all(y_first, 'z', split_axis=0, concat_axis=0, tiled=True)]
    all_to_all x1 -> x0, starting transfers between devices: 8.34 us -> none  [per_device(): lax.all_to_all(y_first, 'z', split_axis=0, concat_axis=0, tiled=True)]
    all_to_all x1, waiting for transfers between devices: 2.84 us -> 5.49 us  [per_device(): lax.all_to_all(packed, ('x', 'core'), split_axis=0, concat_axis=0, tiled=...]
    ppermute x16 -> x13, starting transfers between devices: 16.1 us -> 14.2 us  [shift(): lax.ppermute(value, axis, [(i, (i + by) % size) for i in range(size)])]
    unnamed x45 -> x35, local copies, waits for them, and re-layouts: 6.66 us -> 7.43 us
    ppermute x16 -> x13, waiting for transfers between devices: 47.9 us -> 48.2 us  [shift(): lax.ppermute(value, axis, [(i, (i + by) % size) for i in range(size)])]
  transfers between devices with their start and end apart: 27 -> 23, of which waited for: 13 -> 13; matrix products, arithmetic and copies ran while one was open for 7% -> 8% of each run, Pallas kernels for 22% -> 23%
where the time goes in v3:
time: 206 us; the launch traced here: 205 us
  waiting for transfers between devices  87.5 us (42%)
  Pallas kernels  46.6 us (23%)
  starting transfers between devices  30.8 us (15%)
  local copies, waits for them, and re-layouts  18.1 us (9%)
  between operations  14.3 us (7%)
  other arithmetic  7.72 us (4%)
    ppermute x13, waiting for transfers between devices, shift(): lax.ppermute(value, axis, [(i, (i + by) % size) for i in range(size)])  48.2 us
    all_to_all x1, waiting for transfers between devices, per_device(): lax.all_to_all(o_split, 'x', split_axis=0, concat_axis=0, tiled=True)  32.3 us
    pallas_call x1, Pallas kernels, attention(): pl.pallas_call(attention_kernel, out_shape=[jax.ShapeDtypeStruct((2, TOK,...  16.8 us
    pallas_call x2, Pallas kernels, project(): pl.pallas_call(project_kernel, out_shape=jax.ShapeDtypeStruct((1024, 512)...  15.2 us
    ppermute x13, starting transfers between devices, shift(): lax.ppermute(value, axis, [(i, (i + by) % size) for i in range(size)])  14.2 us
    pallas_call x1, Pallas kernels, weight_product(): pl.pallas_call(functools.partial(weight_kernel, factor), out_shape=(jax.S...  11.8 us
    unnamed x35, local copies, waits for them, and re-layouts  7.43 us
    ppermute x6, starting transfers between devices, swap(): return lax.ppermute(value, 'core', [(0, 1), (1, 0)])  6.99 us
  transfers between devices with their start and end apart: 23, of which 13 were waited for; matrix products, arithmetic and copies ran while one was open for 8% of the time, Pallas kernels for 23%

profile of v3, /device:TPU:1, one launch (start us, length us, event | category | flops | bytes accessed | tf_op | source)
XLA Modules:
  0.0 205.0 jit_solution(12027237041417439328)
XLA Ops:
  7.2 0.9 select_bitcast_fusion.1
  8.2 3.3 %collective-permute-start.1 = (bf16[16,2560]{1,0:T(8,128)(2,1)S(1)}, bf16[16,2560]{1,0:T(8,128)(2,1)S(1)}, u32[]{:S(2)}, u32[]{:S(2)}) collective-permute-start(bf16[16,2560]{1,0:T(8,128)(2,1)S(1)} %get-tuple-element.46), channel_id=1, source_target_pairs={{0,32},{32,0},{1,33},{33,1},{2,34},{34,2},{3,35},{35,3},{4,36},{36... | collective-permute-start | bytes 245768 | tf_op jit(solution)/shard_map/ppermute | solution.py:35
  11.5 1.4 broadcast_select_fusion.1
  13.0 1.1 collective-permute-start.9
  15.1 3.2 %collective-permute-done.9 = bf16[2,16,2560]{2,1,0:T(8,128)(2,1)S(1)} collective-permute-done((bf16[2,16,2560]{2,1,0:T(8,128)(2,1)S(1)}, bf16[2,16,2560]{2,1,0:T(8,128)(2,1)S(1)}, u32[]{:S(2)}, u32[]{:S(2)}) %collective-permute-start.9) | collective-permute-done | bytes 163872 | tf_op jit(solution)/shard_map/ppermute | solution.py:27
  18.4 2.2 %collective-permute-done.8 = bf16[2,16,2560]{2,1,0:T(8,128)(2,1)S(1)} collective-permute-done((bf16[2,16,2560]{2,1,0:T(8,128)(2,1)S(1)}, bf16[2,16,2560]{2,1,0:T(8,128)(2,1)S(1)}, u32[]{:S(2)}, u32[]{:S(2)}) %collective-permute-start.8) | collective-permute-done | bytes 163872 | tf_op jit(solution)/shard_map/ppermute | solution.py:27
  20.6 4.6 %collective-permute-done.7 = bf16[2,16,2560]{2,1,0:T(8,128)(2,1)S(1)} collective-permute-done((bf16[2,16,2560]{2,1,0:T(8,128)(2,1)S(1)}, bf16[2,16,2560]{2,1,0:T(8,128)(2,1)S(1)}, u32[]{:S(2)}, u32[]{:S(2)}) %collective-permute-start.7) | collective-permute-done | bytes 163872 | tf_op jit(solution)/shard_map/ppermute | solution.py:27
  25.2 0.9 pad_maximum_fusion.2
  26.2 0.8 copy-done.9
  27.0 1.3 pad_maximum_fusion.own
  28.7 1.3 copy.21
  30.0 1.2 collective-permute-start.2
  31.2 1.5 collective-permute-start.3
  32.7 3.5 %all-to-all-start = ((bf16[4,128,1024]{2,1,0:T(8,128)(2,1)}), bf16[4,128,1024]{2,1,0:T(8,128)(2,1)S(1)}, u32[]{:S(2)}, u32[]{:S(2)}) async-start(bf16[4,128,1024]{2,1,0:T(8,128)(2,1)} %bitcast.47), calls=%async_computation | async-start | bytes 2097152 | tf_op jit(solution)/shard_map/all_to_all | solution.py:286
  37.0 1.7 reshape.42
  39.7 1.3 maximum_bitcast_fusion
  41.0 32.3 %all-to-all-done = bf16[4,128,1024]{2,1,0:T(8,128)(2,1)S(1)} async-done(((bf16[4,128,1024]{2,1,0:T(8,128)(2,1)}), bf16[4,128,1024]{2,1,0:T(8,128)(2,1)S(1)}, u32[]{:S(2)}, u32[]{:S(2)}) %all-to-all-start) | async-done | bytes 1048608 | tf_op jit(solution)/shard_map/all_to_all | solution.py:286
  73.3 1.4 collective-permute-start.6
  74.7 1.1 slice.54
  75.8 1.0 collective-permute-start.4
  76.8 1.1 slice.55
  77.9 1.9 collective-permute-start.5
  80.5 12.8 %collective-permute-done.4.far0 = bf16[128,2560]{1,0:T(8,128)(2,1)} collective-permute-done((bf16[128,2560]{1,0:T(8,128)(2,1)S(1)}, bf16[128,2560]{1,0:T(8,128)(2,1)}, u32[]{:S(2)}, u32[]{:S(2)}) %collective-permute-start.4) | collective-permute-done | bytes 655392 | tf_op jit(solution)/shard_map/ppermute | solution.py:27
  93.8 1.0 copy-done.4
  94.8 11.8 %shard_map.102 = (bf16[8,4,2,16,2560]{4,3,2,1,0:T(8,128)(2,1)}, bf16[1024,2560]{1,0:T(8,128)(2,1)}) custom-call(s32[7]{0:T(128)} %concatenate.12.info, bf16[256,2560]{1,0:T(8,128)(2,1)} %copy-done, bf16[256,2560]{1,0:T(8,128)(2,1)} %collective-permute-done.2.prev, bf16[256,2560]{1,0:T(8,128)(2,1)} %collective-permute-done.3.succ, ...), custom_call_target="tpu_custom_call" | custom-call | flops 1048576 | bytes 1048576 | tf_op jit(solution)/shard_map/pallas_call | solution.py:79
  106.7 6.0 %all-to-all-start.1 = ((bf16[8,128,768]{2,1,0:T(8,128)(2,1)}), bf16[8,128,768]{2,1,0:T(8,128)(2,1)S(1)}, u32[]{:S(2)}, u32[]{:S(2)}) async-start(bf16[8,128,768]{2,1,0:T(8,128)(2,1)} %maximum_bitcast_fusion), calls=%async_computation.1 | async-start | bytes 3145728 | tf_op jit(solution)/shard_map/all_to_all | solution.py:306
  112.7 7.4 %shard_map.104 = bf16[1024,512]{1,0:T(8,128)(2,1)} custom-call(s32[7]{0:T(128)} %concatenate.12.info, bf16[1024,2560]{1,0:T(8,128)(2,1)} %get-tuple-element.25.rows, bf16[8,4,2,16,2560]{4,3,2,1,0:T(8,128)(2,1)} %bitcast.48), custom_call_target="tpu_custom_call" | custom-call | flops 1048576 | bytes 1048576 | tf_op jit(solution)/shard_map/pallas_call | solution.py:133
  120.1 7.8 %shard_map.103.mine = f32[1024,512]{1,0:T(8,128)} custom-call(s32[7]{0:T(128)} %concatenate.12.info, bf16[1024,2560]{1,0:T(8,128)(2,1)} %get-tuple-element.25.rows, bf16[8,4,2,16,2560]{4,3,2,1,0:T(8,128)(2,1)} %bitcast.49), custom_call_target="tpu_custom_call" | custom-call | flops 1048576 | bytes 1048576 | tf_op jit(solution)/shard_map/pallas_call | solution.py:133
  127.9 5.5 %all-to-all-done.1 = bf16[8,128,768]{2,1,0:T(8,128)(2,1)S(1)} async-done(((bf16[8,128,768]{2,1,0:T(8,128)(2,1)}), bf16[8,128,768]{2,1,0:T(8,128)(2,1)S(1)}, u32[]{:S(2)}, u32[]{:S(2)}) %all-to-all-start.1) | async-done | bytes 1572896 | tf_op jit(solution)/shard_map/all_to_all | solution.py:306
  133.4 1.2 copy-done.2
  134.9 16.8 %shard_map.105 = (bf16[2,128,768]{2,1,0:T(8,128)(2,1)}, bf16[2,128,768]{2,1,0:T(8,128)(2,1)}, bf16[2,128,768]{2,1,0:T(8,128)(2,1)}, bf16[2,128,768]{2,1,0:T(8,128)(2,1)}) custom-call(s32[7]{0:T(128)} %concatenate.12.info, bf16[1024,768]{1,0:T(8,128)(2,1)} %bitcast.53, bf16[1024,768]{1,0:T(8,128)(2,1)} %bitcast.54, bf16[1024,768]{1,0:T(8,128)(2,1)} %bitcast.55, ...), custom_call_target="tpu_custom_call" | custom-call | flops 14000000000 | bytes 8388608 | tf_op jit(solution)/shard_map/pallas_call | solution.py:221
  152.1 1.7 collective-permute-start.12
  153.8 0.8 collective-permute-start.13
  154.6 9.0 %collective-permute-done.11.refs_1_ = bf16[2,128,768]{2,1,0:T(8,128)(2,1)S(1)} collective-permute-done((bf16[2,128,768]{2,1,0:T(8,128)(2,1)}, bf16[2,128,768]{2,1,0:T(8,128)(2,1)S(1)}, u32[]{:S(2)}, u32[]{:S(2)}) %collective-permute-start.11) | collective-permute-done | bytes 393248 | tf_op jit(solution)/shard_map/ppermute | solution.py:27
  163.6 7.2 %collective-permute-done.12.refs_2_ = bf16[2,128,768]{2,1,0:T(8,128)(2,1)S(1)} collective-permute-done((bf16[2,128,768]{2,1,0:T(8,128)(2,1)}, bf16[2,128,768]{2,1,0:T(8,128)(2,1)S(1)}, u32[]{:S(2)}, u32[]{:S(2)}) %collective-permute-start.12) | collective-permute-done | bytes 393248 | tf_op jit(solution)/shard_map/ppermute | solution.py:27
  170.8 1.3 collective-permute-done.13.refs_3_
  172.0 1.4 reduce-scatter.2.cloned.1.call-done
  173.4 1.1 slice_bitcast_fusion.2
  174.5 2.5 %collective-permute-start.17 = (bf16[2,16,2560]{2,1,0:T(8,128)(2,1)S(1)}, bf16[2,16,2560]{2,1,0:T(8,128)(2,1)S(1)}, u32[]{:S(2)}, u32[]{:S(2)}) collective-permute-start(bf16[2,16,2560]{2,1,0:T(8,128)(2,1)S(1)} %get-tuple-element.39), channel_id=1, source_target_pairs={{0,24},{8,0},{16,8},{24,16},{1,25},{9,1},{17,9},{25,17},{2,26},{10... | collective-permute-start | bytes 491528 | tf_op jit(solution)/shard_map/ppermute | solution.py:27
  178.2 0.9 slice.56
  179.4 1.5 collective-permute-start.14
  180.9 2.5 %collective-permute-done.16 = bf16[2,16,2560]{2,1,0:T(8,128)(2,1)S(1)} collective-permute-done((bf16[2,16,2560]{2,1,0:T(8,128)(2,1)S(1)}, bf16[2,16,2560]{2,1,0:T(8,128)(2,1)S(1)}, u32[]{:S(2)}, u32[]{:S(2)}) %collective-permute-start.16) | collective-permute-done | bytes 163872 | tf_op jit(solution)/shard_map/ppermute | solution.py:27
  183.4 4.8 %collective-permute-done.15 = bf16[2,16,2560]{2,1,0:T(8,128)(2,1)S(1)} collective-permute-done((bf16[2,16,2560]{2,1,0:T(8,128)(2,1)S(1)}, bf16[2,16,2560]{2,1,0:T(8,128)(2,1)S(1)}, u32[]{:S(2)}, u32[]{:S(2)}) %collective-permute-start.15) | collective-permute-done | bytes 163872 | tf_op jit(solution)/shard_map/ppermute | solution.py:27
  188.2 1.0 fusion.1
  189.8 0.9 copy-done.8
  190.7 2.8 %shard_map.106 = (bf16[128,4096]{1,0:T(8,128)(2,1)}, bf16[128,512]{1,0:T(8,128)(2,1)}, bf16[128,512]{1,0:T(8,128)(2,1)}) custom-call(s32[7]{0:T(128)} %concatenate.12.info, bf16[2,128,768]{2,1,0:T(8,128)(2,1)} %get-tuple-element.27.refs_0_, bf16[2,128,768]{2,1,0:T(8,128)(2,1)} %copy-done.5, bf16[2,128,768]{2,1,0:T(8,128)(2,1)} %copy-done.6, ...), custom_call_target="tpu_custom_call" | custom-call | tf_op jit(solution)/shard_map/pallas_call | solution.py:252
  193.5 2.5 %copy.19 = bf16[16,8,32,128]{3,2,1,0:T(8,128)(2,1)} copy(bf16[16,8,32,128]{3,1,2,0:T(8,128)(2,1)} %bitcast.60) | data formatting | bytes 2097152
  197.4 0.7 pad_maximum_fusion.3
  (69 shorter events, 8.7 us)
Async XLA Ops:
  7.2 105.5 %all-gather.3.cloned.1.call-start = ((), (), s32[]{:S(2)}) async-start(), calls=%async_computation.4 | async-start | bytes 5898240 | tf_op jit(solution)/shard_map/all_gather | solution.py:291
  8.2 4.8 %collective-permute-start.1 = (bf16[16,2560]{1,0:T(8,128)(2,1)S(1)}, bf16[16,2560]{1,0:T(8,128)(2,1)S(1)}, u32[]{:S(2)}, u32[]{:S(2)}) collective-permute-start(bf16[16,2560]{1,0:T(8,128)(2,1)S(1)} %get-tuple-element.46), channel_id=1, source_target_pairs={{0,32},{32,0},{1,33},{33,1},{2,34},{34,2},{3,35},{35,3},{4,36},{36... | collective-permute-start | bytes 245768 | tf_op jit(solution)/shard_map/ppermute | solution.py:35
  12.9 13.3 %collective-permute-start = (bf16[128,2560]{1,0:T(8,128)(2,1)S(1)}, bf16[128,2560]{1,0:T(8,128)(2,1)S(1)}, u32[]{:S(2)}, u32[]{:S(2)}) collective-permute-start(bf16[128,2560]{1,0:T(8,128)(2,1)S(1)} %get-tuple-element.37), channel_id=1, source_target_pairs={{0,32},{32,0},{1,33},{33,1},{2,34},{34,2},{3,35},{35,3},{4,36},{36... | collective-permute-start | bytes 1966088 | tf_op jit(solution)/shard_map/ppermute | solution.py:35
  13.0 5.4 %collective-permute-start.9 = (bf16[2,16,2560]{2,1,0:T(8,128)(2,1)S(1)}, bf16[2,16,2560]{2,1,0:T(8,128)(2,1)S(1)}, u32[]{:S(2)}, u32[]{:S(2)}) collective-permute-start(bf16[2,16,2560]{2,1,0:T(8,128)(2,1)S(1)} %get-tuple-element.44), channel_id=1, source_target_pairs={{0,24},{8,0},{16,8},{24,16},{1,25},{9,1},{17,9},{25,17},{2,26},{10... | collective-permute-start | bytes 491528 | tf_op jit(solution)/shard_map/ppermute | solution.py:27
  14.1 6.5 %collective-permute-start.8 = (bf16[2,16,2560]{2,1,0:T(8,128)(2,1)S(1)}, bf16[2,16,2560]{2,1,0:T(8,128)(2,1)S(1)}, u32[]{:S(2)}, u32[]{:S(2)}) collective-permute-start(bf16[2,16,2560]{2,1,0:T(8,128)(2,1)S(1)} %get-tuple-element.44), channel_id=1, source_target_pairs={{0,16},{8,24},{16,0},{24,8},{1,17},{9,25},{17,1},{25,9},{2,18},{10... | collective-permute-start | bytes 491528 | tf_op jit(solution)/shard_map/ppermute | solution.py:27
  14.4 10.8 %collective-permute-start.7 = (bf16[2,16,2560]{2,1,0:T(8,128)(2,1)S(1)}, bf16[2,16,2560]{2,1,0:T(8,128)(2,1)S(1)}, u32[]{:S(2)}, u32[]{:S(2)}) collective-permute-start(bf16[2,16,2560]{2,1,0:T(8,128)(2,1)S(1)} %get-tuple-element.44), channel_id=1, source_target_pairs={{0,8},{8,16},{16,24},{24,0},{1,9},{9,17},{17,25},{25,1},{2,10},{10... | collective-permute-start | bytes 491528 | tf_op jit(solution)/shard_map/ppermute | solution.py:27
  26.2 0.8 copy-start.9
  27.0 1.4 copy-start.3
  28.3 2.9 %copy-start = (bf16[256,2560]{1,0:T(8,128)(2,1)}, bf16[256,2560]{1,0:T(8,128)(2,1)S(1)}, u32[]{:S(2)}) copy-start(bf16[256,2560]{1,0:T(8,128)(2,1)S(1)} %pad_maximum_fusion.own) | copy-start | bytes 3932164
  30.0 6.3 %copy-start.11 = (bf16[1,128,4,128]{3,2,1,0:T(4,128)(2,1)S(1)}, bf16[1,128,4,128]{3,2,1,0:T(4,128)(2,1)}, u32[]{:S(2)}) copy-start(bf16[1,128,4,128]{3,2,1,0:T(4,128)(2,1)} %param.9) | copy-start | bytes 393220
  30.0 6.9 %copy-start.12 = (bf16[1,128,4,128]{3,2,1,0:T(4,128)(2,1)S(1)}, bf16[1,128,4,128]{3,2,1,0:T(4,128)(2,1)}, u32[]{:S(2)}) copy-start(bf16[1,128,4,128]{3,2,1,0:T(4,128)(2,1)} %param.8) | copy-start | bytes 393220
  30.0 43.3 %collective-permute-start.2 = (bf16[256,2560]{1,0:T(8,128)(2,1)S(1)}, bf16[256,2560]{1,0:T(8,128)(2,1)}, u32[]{:S(2)}, u32[]{:S(2)}) collective-permute-start(bf16[256,2560]{1,0:T(8,128)(2,1)S(1)} %pad_maximum_fusion.own), channel_id=1, source_target_pairs={{0,64},{64,128},{128,192},{192,0},{1,65},{65,129},{129,193},{193,1... | collective-permute-start | bytes 3932168 | tf_op jit(solution)/shard_map/ppermute | solution.py:27
  31.2 42.1 %collective-permute-start.3 = (bf16[256,2560]{1,0:T(8,128)(2,1)S(1)}, bf16[256,2560]{1,0:T(8,128)(2,1)}, u32[]{:S(2)}, u32[]{:S(2)}) collective-permute-start(bf16[256,2560]{1,0:T(8,128)(2,1)S(1)} %pad_maximum_fusion.own), channel_id=1, source_target_pairs={{0,192},{64,0},{128,64},{192,128},{1,193},{65,1},{129,65},{193,129... | collective-permute-start | bytes 3932168 | tf_op jit(solution)/shard_map/ppermute | solution.py:27
  32.7 40.6 %all-to-all-start = ((bf16[4,128,1024]{2,1,0:T(8,128)(2,1)}), bf16[4,128,1024]{2,1,0:T(8,128)(2,1)S(1)}, u32[]{:S(2)}, u32[]{:S(2)}) async-start(bf16[4,128,1024]{2,1,0:T(8,128)(2,1)} %bitcast.47), calls=%async_computation | async-start | bytes 2097152 | tf_op jit(solution)/shard_map/all_to_all | solution.py:286
  36.2 137.2 %reduce-scatter.2.cloned.1.call-start = ((), (), s32[]{:S(2)}) async-start(), calls=%async_computation.3 | async-start | bytes 5898240 | tf_op jit(solution)/shard_map/reduce_scatter | solution.py:312
  38.7 0.9 copy-start.10
  41.0 38.9 %copy-start.15 = (s32[1,3]{1,0:T(1,128)S(1)}, s32[1,3]{1,0:T(1,128)}, u32[]{:S(2)}) copy-start(s32[1,3]{1,0:T(1,128)} %param.13) | copy-start | bytes 40
  73.3 20.6 %copy-start.1 = (bf16[4,128,1024]{2,1,0:T(8,128)(2,1)}, bf16[4,128,1024]{2,1,0:T(8,128)(2,1)S(1)}, u32[]{:S(2)}) copy-start(bf16[4,128,1024]{2,1,0:T(8,128)(2,1)S(1)} %all-to-all-done) | copy-start | bytes 3145732
  73.3 20.6 %collective-permute-start.6 = (bf16[512,1024]{1,0:T(8,128)(2,1)S(1)}, bf16[512,1024]{1,0:T(8,128)(2,1)S(1)}, u32[]{:S(2)}, u32[]{:S(2)}) collective-permute-start(bf16[512,1024]{1,0:T(8,128)(2,1)S(1)} %bitcast.50), channel_id=1, source_target_pairs={{0,32},{32,0},{1,33},{33,1},{2,34},{34,2},{3,35},{35,3},{4,36},{36... | collective-permute-start | bytes 3145736 | tf_op jit(solution)/shard_map/ppermute | solution.py:35
  75.8 17.4 %collective-permute-start.4 = (bf16[128,2560]{1,0:T(8,128)(2,1)S(1)}, bf16[128,2560]{1,0:T(8,128)(2,1)}, u32[]{:S(2)}, u32[]{:S(2)}) collective-permute-start(bf16[128,2560]{1,0:T(8,128)(2,1)S(1)} %slice.54), channel_id=1, source_target_pairs={{0,64},{64,128},{128,192},{192,0},{1,65},{65,129},{129,193},{193,1... | collective-permute-start | bytes 1966088 | tf_op jit(solution)/shard_map/ppermute | solution.py:27
  77.9 15.9 %collective-permute-start.5 = (bf16[128,2560]{1,0:T(8,128)(2,1)S(1)}, bf16[128,2560]{1,0:T(8,128)(2,1)}, u32[]{:S(2)}, u32[]{:S(2)}) collective-permute-start(bf16[128,2560]{1,0:T(8,128)(2,1)S(1)} %slice.55), channel_id=1, source_target_pairs={{0,192},{64,0},{128,64},{192,128},{1,193},{65,1},{129,65},{193,129... | collective-permute-start | bytes 1966088 | tf_op jit(solution)/shard_map/ppermute | solution.py:27
  93.8 1.0 copy-start.4
  106.7 26.7 %all-to-all-start.1 = ((bf16[8,128,768]{2,1,0:T(8,128)(2,1)}), bf16[8,128,768]{2,1,0:T(8,128)(2,1)S(1)}, u32[]{:S(2)}, u32[]{:S(2)}) async-start(bf16[8,128,768]{2,1,0:T(8,128)(2,1)} %maximum_bitcast_fusion), calls=%async_computation.1 | async-start | bytes 3145728 | tf_op jit(solution)/shard_map/all_to_all | solution.py:306
  120.1 13.3 %collective-permute-start.10 = (bf16[1024,512]{1,0:T(8,128)(2,1)}, bf16[1024,512]{1,0:T(8,128)(2,1)S(1)}, u32[]{:S(2)}, u32[]{:S(2)}) collective-permute-start(bf16[1024,512]{1,0:T(8,128)(2,1)} %shard_map.104), channel_id=1, source_target_pairs={{0,32},{32,0},{1,33},{33,1},{2,34},{34,2},{3,35},{35,3},{4,36},{36... | collective-permute-start | bytes 3145736 | tf_op jit(solution)/shard_map/ppermute | solution.py:35
  133.4 1.2 copy-start.2
  133.4 1.5 copy-start.16
  151.7 11.9 %collective-permute-start.11 = (bf16[2,128,768]{2,1,0:T(8,128)(2,1)}, bf16[2,128,768]{2,1,0:T(8,128)(2,1)S(1)}, u32[]{:S(2)}, u32[]{:S(2)}) collective-permute-start(bf16[2,128,768]{2,1,0:T(8,128)(2,1)} %get-tuple-element.28), channel_id=1, source_target_pairs={{0,64},{64,128},{128,192},{192,0},{1,65},{65,129},{129,193},{193,1... | collective-permute-start | bytes 1179656 | tf_op jit(solution)/shard_map/ppermute | solution.py:27
  152.1 18.7 %collective-permute-start.12 = (bf16[2,128,768]{2,1,0:T(8,128)(2,1)}, bf16[2,128,768]{2,1,0:T(8,128)(2,1)S(1)}, u32[]{:S(2)}, u32[]{:S(2)}) collective-permute-start(bf16[2,128,768]{2,1,0:T(8,128)(2,1)} %get-tuple-element.29), channel_id=1, source_target_pairs={{0,128},{64,192},{128,0},{192,64},{1,129},{65,193},{129,1},{193,65... | collective-permute-start | bytes 1179656 | tf_op jit(solution)/shard_map/ppermute | solution.py:27
  153.8 18.2 %collective-permute-start.13 = (bf16[2,128,768]{2,1,0:T(8,128)(2,1)}, bf16[2,128,768]{2,1,0:T(8,128)(2,1)S(1)}, u32[]{:S(2)}, u32[]{:S(2)}) collective-permute-start(bf16[2,128,768]{2,1,0:T(8,128)(2,1)} %get-tuple-element.30), channel_id=1, source_target_pairs={{0,192},{64,0},{128,64},{192,128},{1,193},{65,1},{129,65},{193,129... | collective-permute-start | bytes 1179656 | tf_op jit(solution)/shard_map/ppermute | solution.py:27
  163.6 15.7 %copy-start.5 = (bf16[2,128,768]{2,1,0:T(8,128)(2,1)}, bf16[2,128,768]{2,1,0:T(8,128)(2,1)S(1)}, u32[]{:S(2)}) copy-start(bf16[2,128,768]{2,1,0:T(8,128)(2,1)S(1)} %collective-permute-done.11.refs_1_) | copy-start | bytes 1179652
  170.8 8.6 %copy-start.6 = (bf16[2,128,768]{2,1,0:T(8,128)(2,1)}, bf16[2,128,768]{2,1,0:T(8,128)(2,1)S(1)}, u32[]{:S(2)}) copy-start(bf16[2,128,768]{2,1,0:T(8,128)(2,1)S(1)} %collective-permute-done.12.refs_2_) | copy-start | bytes 1179652
  172.0 7.3 %copy-start.7 = (bf16[2,128,768]{2,1,0:T(8,128)(2,1)}, bf16[2,128,768]{2,1,0:T(8,128)(2,1)S(1)}, u32[]{:S(2)}) copy-start(bf16[2,128,768]{2,1,0:T(8,128)(2,1)S(1)} %collective-permute-done.13.refs_3_) | copy-start | bytes 1179652
  174.5 6.4 %collective-permute-start.17 = (bf16[2,16,2560]{2,1,0:T(8,128)(2,1)S(1)}, bf16[2,16,2560]{2,1,0:T(8,128)(2,1)S(1)}, u32[]{:S(2)}, u32[]{:S(2)}) collective-permute-start(bf16[2,16,2560]{2,1,0:T(8,128)(2,1)S(1)} %get-tuple-element.39), channel_id=1, source_target_pairs={{0,24},{8,0},{16,8},{24,16},{1,25},{9,1},{17,9},{25,17},{2,26},{10... | collective-permute-start | bytes 491528 | tf_op jit(solution)/shard_map/ppermute | solution.py:27
  177.1 6.3 %collective-permute-start.16 = (bf16[2,16,2560]{2,1,0:T(8,128)(2,1)S(1)}, bf16[2,16,2560]{2,1,0:T(8,128)(2,1)S(1)}, u32[]{:S(2)}, u32[]{:S(2)}) collective-permute-start(bf16[2,16,2560]{2,1,0:T(8,128)(2,1)S(1)} %get-tuple-element.40), channel_id=1, source_target_pairs={{0,16},{8,24},{16,0},{24,8},{1,17},{9,25},{17,1},{25,9},{2,18},{10... | collective-permute-start | bytes 491528 | tf_op jit(solution)/shard_map/ppermute | solution.py:27
  177.6 10.6 %collective-permute-start.15 = (bf16[2,16,2560]{2,1,0:T(8,128)(2,1)S(1)}, bf16[2,16,2560]{2,1,0:T(8,128)(2,1)S(1)}, u32[]{:S(2)}, u32[]{:S(2)}) collective-permute-start(bf16[2,16,2560]{2,1,0:T(8,128)(2,1)S(1)} %get-tuple-element.38), channel_id=1, source_target_pairs={{0,8},{8,16},{16,24},{24,0},{1,9},{9,17},{17,25},{25,1},{2,10},{10... | collective-permute-start | bytes 491528 | tf_op jit(solution)/shard_map/ppermute | solution.py:27
  179.4 10.4 %collective-permute-start.14 = (bf16[4,128,768]{2,1,0:T(8,128)(2,1)S(1)}, bf16[4,128,768]{2,1,0:T(8,128)(2,1)S(1)}, u32[]{:S(2)}, u32[]{:S(2)}) collective-permute-start(bf16[4,128,768]{2,1,0:T(8,128)(2,1)S(1)} %pad_maximum_fusion.1), channel_id=1, source_target_pairs={{0,32},{32,0},{1,33},{33,1},{2,34},{34,2},{3,35},{35,3},{4,36},{36... | collective-permute-start | bytes 2359304 | tf_op jit(solution)/shard_map/ppermute | solution.py:35
  189.2 8.1 %collective-permute-start.18 = (f32[16,2560]{1,0:T(8,128)S(1)}, f32[16,2560]{1,0:T(8,128)S(1)}, u32[]{:S(2)}, u32[]{:S(2)}) collective-permute-start(f32[16,2560]{1,0:T(8,128)S(1)} %select_bitcast_fusion), channel_id=1, source_target_pairs={{0,32},{32,0},{1,33},{33,1},{2,34},{34,2},{3,35},{35,3},{4,36},{36... | collective-permute-start | bytes 491528 | tf_op jit(solution)/shard_map/ppermute | solution.py:35
  189.8 0.9 copy-start.8
  193.5 2.5 %copy-start.14 = (bf16[128,512]{1,0:T(8,128)(2,1)S(1)}, bf16[128,512]{1,0:T(8,128)(2,1)}, u32[]{:S(2)}) copy-start(bf16[128,512]{1,0:T(8,128)(2,1)} %get-tuple-element.32) | copy-start | bytes 393220
  193.5 3.2 %copy-start.13 = (bf16[128,512]{1,0:T(8,128)(2,1)S(1)}, bf16[128,512]{1,0:T(8,128)(2,1)}, u32[]{:S(2)}) copy-start(bf16[128,512]{1,0:T(8,128)(2,1)} %get-tuple-element.33) | copy-start | bytes 393220
Sparse Core Ops, SparseCore 0:
  28.4 64.8 all-gather.2
  106.8 66.6 reduce-scatter.1

commit v4 on v3

--- a/solution.py
+++ b/solution.py
@@ -90,15 +90,14 @@
     )(info, *parts, o_own, o_sib)
 
 
-def project_kernel(info, rows, block, out, weight, total):
-    y, core = info[1], info[3]
+def project_kernel(info, rows, block, out, total):
+    core = info[3]
     step = pl.program_id(0)
-    for r in range(4):
-        for z in range(8):
-            row = (lax.rem(y - r + 4, 4) * 8 + z) * 16
-            weight[pl.ds(pl.multiple_of(row, 16), 16), :] = block[z, r]
     product = lax.dot_general(
-        rows[...], weight[...], (((1,), (1,)), ((), ())), preferred_element_type=F32
+        rows[...],
+        block[...].reshape(512, PCOLS),
+        (((1,), (1,)), ((), ())),
+        preferred_element_type=F32,
     )
 
     @pl.when(step == 0)
@@ -125,10 +124,10 @@
         grid=(2560 // PCOLS,),
         in_specs=[
             pl.BlockSpec((1024, PCOLS), lambda n, info: (0, n)),
-            pl.BlockSpec((8, 4, None, 16, PCOLS), lambda n, info: (0, 0, rc, 0, n)),
+            pl.BlockSpec((32, None, 16, PCOLS), lambda n, info: (0, rc, 0, n)),
         ],
         out_specs=pl.BlockSpec((1024, 512), lambda n, info: (0, 0)),
-        scratch_shapes=[pltpu.VMEM((512, PCOLS), BF16), pltpu.VMEM((1024, 512), F32)],
+        scratch_shapes=[pltpu.VMEM((1024, 512), F32)],
     )
     return pl.pallas_call(
         project_kernel,
@@ -281,15 +280,14 @@
 
     weight_mine, weight_theirs = halves(out_weight)
     weight_pair = jnp.stack([weight_mine, swap(weight_theirs)])
-    near = jnp.stack([weight_pair] + [shift(weight_pair, "y", r) for r in (1, 2, 3)])
+    weight = lax.all_gather(weight_pair, ("y", "z"), axis=0, tiled=False)
+
     o_split = jnp.transpose(attn_out.reshape(TOK, 4, 1024), (1, 0, 2))
     o_own = lax.all_to_all(o_split, "x", split_axis=0, concat_axis=0, tiled=True)
     o_own = o_own.reshape(512, 1024)
 
     grad_mine, grad_theirs = halves(out_grad[0])
     grad_chip = jnp.concatenate([grad_mine, swap(grad_theirs)], axis=0)
-    weight = lax.all_gather(after(near, grad_chip), "z", axis=0, tiled=False)
-
     packed = jnp.concatenate(
         [
             queries.reshape(TOK, 8, 512),

time: 206 us -> 198 us (0.961)
  waiting for transfers between devices: 87.5 us -> 78.8 us
    ppermute x13 -> x10, waiting for transfers between devices: 48.2 us -> 38.3 us  [shift(): lax.ppermute(value, axis, [(i, (i + by) % size) for i in range(size)])]
    ppermute x13 -> x10, starting transfers between devices: 14.2 us -> 11.9 us  [shift(): lax.ppermute(value, axis, [(i, (i + by) % size) for i in range(size)])]
    unnamed x35 -> x33, local copies, waits for them, and re-layouts: 7.43 us -> 6.43 us
  transfers between devices with their start and end apart: 23 -> 20, of which waited for: 13 -> 12; matrix products, arithmetic and copies ran while one was open for 8% -> 10% of each run, Pallas kernels for 23% -> 24%
where the time goes in v4:
time: 198 us; the launch traced here: 197 us
  waiting for transfers between devices  78.8 us (40%)
  Pallas kernels  47 us (24%)
  starting transfers between devices  29.5 us (15%)
  local copies, waits for them, and re-layouts  18.1 us (9%)
  between operations  15.7 us (8%)
  other arithmetic  8.19 us (4%)
    ppermute x10, waiting for transfers between devices, shift(): lax.ppermute(value, axis, [(i, (i + by) % size) for i in range(size)])  38.3 us
    all_to_all x1, waiting for transfers between devices, per_device(): lax.all_to_all(o_split, 'x', split_axis=0, concat_axis=0, tiled=True)  30.8 us
    pallas_call x1, Pallas kernels, attention(): pl.pallas_call(attention_kernel, out_shape=[jax.ShapeDtypeStruct((2, TOK,...  16.8 us
    pallas_call x2, Pallas kernels, project(): pl.pallas_call(project_kernel, out_shape=jax.ShapeDtypeStruct((1024, 512)...  15.4 us
    pallas_call x1, Pallas kernels, weight_product(): pl.pallas_call(functools.partial(weight_kernel, factor), out_shape=(jax.S...  11.9 us
    ppermute x10, starting transfers between devices, shift(): lax.ppermute(value, axis, [(i, (i + by) % size) for i in range(size)])  11.9 us
    ppermute x6, starting transfers between devices, swap(): return lax.ppermute(value, 'core', [(0, 1), (1, 0)])  7.9 us
    unnamed x33, local copies, waits for them, and re-layouts  6.43 us
  transfers between devices with their start and end apart: 20, of which 12 were waited for; matrix products, arithmetic and copies ran while one was open for 10% of the time, Pallas kernels for 24%

profile of v4, /device:TPU:1, one launch (start us, length us, event | category | flops | bytes accessed | tf_op | source)
XLA Modules:
  0.0 197.3 jit_solution(13642646330876032316)
XLA Ops:
  8.1 0.9 select_bitcast_fusion.1
  9.0 3.3 %collective-permute-start.1 = (bf16[16,2560]{1,0:T(8,128)(2,1)S(1)}, bf16[16,2560]{1,0:T(8,128)(2,1)S(1)}, u32[]{:S(2)}, u32[]{:S(2)}) collective-permute-start(bf16[16,2560]{1,0:T(8,128)(2,1)S(1)} %get-tuple-element.42), channel_id=1, source_target_pairs={{0,32},{32,0},{1,33},{33,1},{2,34},{34,2},{3,35},{35,3},{4,36},{36... | collective-permute-start | bytes 245768 | tf_op jit(solution)/shard_map/ppermute | solution.py:35
  12.3 0.9 collective-permute-done.1
  13.3 0.7 pad_maximum_fusion.3
  14.0 2.2 %broadcast_select_fusion.1 = (bf16[128,2560]{1,0:T(8,128)(2,1)S(1)}, bf16[128,2560]{1,0:T(8,128)(2,1)}) fusion(pred[]{:T(512)S(6)} %eq.2, bf16[128,5120]{1,0:T(8,128)(2,1)} %bitcast.51), kind=kLoop, calls=%fused_computation.5 | loop fusion | flops 655360 | bytes 2621441 | tf_op jit(solution)/shard_map/jit(_where)/select_n | solution.py:279
  16.8 1.3 copy.21
  18.6 1.2 pad_maximum_fusion.own
  19.9 2.7 %collective-permute-start.3 = (bf16[256,2560]{1,0:T(8,128)(2,1)S(1)}, bf16[256,2560]{1,0:T(8,128)(2,1)}, u32[]{:S(2)}, u32[]{:S(2)}) collective-permute-start(bf16[256,2560]{1,0:T(8,128)(2,1)S(1)} %pad_maximum_fusion.own), channel_id=1, source_target_pairs={{0,192},{64,0},{128,64},{192,128},{1,193},{65,1},{129,65},{193,129... | collective-permute-start | bytes 3932168 | tf_op jit(solution)/shard_map/ppermute | solution.py:27
  22.6 3.5 %all-to-all-start = ((bf16[4,128,1024]{2,1,0:T(8,128)(2,1)}), bf16[4,128,1024]{2,1,0:T(8,128)(2,1)S(1)}, u32[]{:S(2)}, u32[]{:S(2)}) async-start(bf16[4,128,1024]{2,1,0:T(8,128)(2,1)} %bitcast.42), calls=%async_computation | async-start | bytes 2097152 | tf_op jit(solution)/shard_map/all_to_all | solution.py:286
  26.2 0.7 copy.17
  26.9 1.7 reshape.42
  29.6 1.3 maximum_bitcast_fusion
  30.9 30.8 %all-to-all-done = bf16[4,128,1024]{2,1,0:T(8,128)(2,1)S(1)} async-done(((bf16[4,128,1024]{2,1,0:T(8,128)(2,1)}), bf16[4,128,1024]{2,1,0:T(8,128)(2,1)S(1)}, u32[]{:S(2)}, u32[]{:S(2)}) %all-to-all-start) | async-done | bytes 1048608 | tf_op jit(solution)/shard_map/all_to_all | solution.py:286
  61.7 2.0 %collective-permute-start.6 = (bf16[512,1024]{1,0:T(8,128)(2,1)S(1)}, bf16[512,1024]{1,0:T(8,128)(2,1)S(1)}, u32[]{:S(2)}, u32[]{:S(2)}) collective-permute-start(bf16[512,1024]{1,0:T(8,128)(2,1)S(1)} %bitcast.45), channel_id=1, source_target_pairs={{0,32},{32,0},{1,33},{33,1},{2,34},{34,2},{3,35},{35,3},{4,36},{36... | collective-permute-start | bytes 3145736 | tf_op jit(solution)/shard_map/ppermute | solution.py:35
  63.7 1.1 slice.54
  64.8 0.7 collective-permute-start.4
  65.4 2.1 %slice.55 = bf16[128,2560]{1,0:T(8,128)(2,1)} slice(bf16[256,2560]{1,0:T(8,128)(2,1)} %collective-permute-done.3.succ), slice={[128:256], [0:2560]} | slice | bytes 1310720 | tf_op jit(solution)/shard_map/slice | solution.py:306
  67.6 2.0 collective-permute-start.5
  70.1 12.1 %collective-permute-done.4.far0 = bf16[128,2560]{1,0:T(8,128)(2,1)} collective-permute-done((bf16[128,2560]{1,0:T(8,128)(2,1)S(1)}, bf16[128,2560]{1,0:T(8,128)(2,1)}, u32[]{:S(2)}, u32[]{:S(2)}) %collective-permute-start.4) | collective-permute-done | bytes 655392 | tf_op jit(solution)/shard_map/ppermute | solution.py:27
  82.2 1.5 collective-permute-done.5.far1
  83.7 1.0 copy-done.4
  84.7 11.9 %shard_map.102 = (bf16[8,4,2,16,2560]{4,3,2,1,0:T(8,128)(2,1)}, bf16[1024,2560]{1,0:T(8,128)(2,1)}) custom-call(s32[7]{0:T(128)} %concatenate.12.info, bf16[256,2560]{1,0:T(8,128)(2,1)} %copy-done, bf16[256,2560]{1,0:T(8,128)(2,1)} %collective-permute-done.2.prev, bf16[256,2560]{1,0:T(8,128)(2,1)} %collective-permute-done.3.succ, ...), custom_call_target="tpu_custom_call" | custom-call | flops 1048576 | bytes 1048576 | tf_op jit(solution)/shard_map/pallas_call | solution.py:79
  96.7 6.1 %all-to-all-start.1 = ((bf16[8,128,768]{2,1,0:T(8,128)(2,1)}), bf16[8,128,768]{2,1,0:T(8,128)(2,1)S(1)}, u32[]{:S(2)}, u32[]{:S(2)}) async-start(bf16[8,128,768]{2,1,0:T(8,128)(2,1)} %maximum_bitcast_fusion), calls=%async_computation.1 | async-start | bytes 3145728 | tf_op jit(solution)/shard_map/all_to_all | solution.py:304
  102.8 7.3 %shard_map.104 = bf16[1024,512]{1,0:T(8,128)(2,1)} custom-call(s32[7]{0:T(128)} %concatenate.12.info, bf16[1024,2560]{1,0:T(8,128)(2,1)} %get-tuple-element.24.rows, bf16[32,2,16,2560]{3,2,1,0:T(8,128)(2,1)} %bitcast.43), custom_call_target="tpu_custom_call" | custom-call | flops 1048576 | bytes 1048576 | tf_op jit(solution)/shard_map/pallas_call | solution.py:132
  110.1 8.1 %shard_map.103.mine = f32[1024,512]{1,0:T(8,128)} custom-call(s32[7]{0:T(128)} %concatenate.12.info, bf16[1024,2560]{1,0:T(8,128)(2,1)} %get-tuple-element.24.rows, bf16[32,2,16,2560]{3,2,1,0:T(8,128)(2,1)} %bitcast.44), custom_call_target="tpu_custom_call" | custom-call | flops 1048576 | bytes 1048576 | tf_op jit(solution)/shard_map/pallas_call | solution.py:132
  118.2 5.3 %all-to-all-done.1 = bf16[8,128,768]{2,1,0:T(8,128)(2,1)S(1)} async-done(((bf16[8,128,768]{2,1,0:T(8,128)(2,1)}), bf16[8,128,768]{2,1,0:T(8,128)(2,1)S(1)}, u32[]{:S(2)}, u32[]{:S(2)}) %all-to-all-start.1) | async-done | bytes 1572896 | tf_op jit(solution)/shard_map/all_to_all | solution.py:304
  123.5 1.2 copy-done.2
  125.0 16.8 %shard_map.105 = (bf16[2,128,768]{2,1,0:T(8,128)(2,1)}, bf16[2,128,768]{2,1,0:T(8,128)(2,1)}, bf16[2,128,768]{2,1,0:T(8,128)(2,1)}, bf16[2,128,768]{2,1,0:T(8,128)(2,1)}) custom-call(s32[7]{0:T(128)} %concatenate.12.info, bf16[1024,768]{1,0:T(8,128)(2,1)} %bitcast.48, bf16[1024,768]{1,0:T(8,128)(2,1)} %bitcast.49, bf16[1024,768]{1,0:T(8,128)(2,1)} %bitcast.50, ...), custom_call_target="tpu_custom_call" | custom-call | flops 14000000000 | bytes 8388608 | tf_op jit(solution)/shard_map/pallas_call | solution.py:220
  142.2 1.7 collective-permute-start.9
  143.9 0.8 collective-permute-start.10
  144.7 9.0 %collective-permute-done.8.refs_1_ = bf16[2,128,768]{2,1,0:T(8,128)(2,1)S(1)} collective-permute-done((bf16[2,128,768]{2,1,0:T(8,128)(2,1)}, bf16[2,128,768]{2,1,0:T(8,128)(2,1)S(1)}, u32[]{:S(2)}, u32[]{:S(2)}) %collective-permute-start.8) | collective-permute-done | bytes 393248 | tf_op jit(solution)/shard_map/ppermute | solution.py:27
  153.7 7.2 %collective-permute-done.9.refs_2_ = bf16[2,128,768]{2,1,0:T(8,128)(2,1)S(1)} collective-permute-done((bf16[2,128,768]{2,1,0:T(8,128)(2,1)}, bf16[2,128,768]{2,1,0:T(8,128)(2,1)S(1)}, u32[]{:S(2)}, u32[]{:S(2)}) %collective-permute-start.9) | collective-permute-done | bytes 393248 | tf_op jit(solution)/shard_map/ppermute | solution.py:27
  160.9 1.2 collective-permute-done.10.refs_3_
  162.1 3.0 %reduce-scatter.2.cloned.1.call-done = bf16[1,4,2,16,2560]{4,3,2,1,0:T(8,128)(2,1)} async-done(((bf16[8,4,2,16,2560]{4,3,2,1,0:T(8,128)(2,1)}), bf16[1,4,2,16,2560]{4,3,2,1,0:T(8,128)(2,1)}) %reduce-scatter.2.cloned.1.call-update) | async-done | bytes 655376 | tf_op jit(solution)/shard_map/reduce_scatter | solution.py:310
  165.1 1.1 slice_bitcast_fusion.2
  166.3 2.5 %collective-permute-start.14 = (bf16[2,16,2560]{2,1,0:T(8,128)(2,1)S(1)}, bf16[2,16,2560]{2,1,0:T(8,128)(2,1)S(1)}, u32[]{:S(2)}, u32[]{:S(2)}) collective-permute-start(bf16[2,16,2560]{2,1,0:T(8,128)(2,1)S(1)} %get-tuple-element.37), channel_id=1, source_target_pairs={{0,24},{8,0},{16,8},{24,16},{1,25},{9,1},{17,9},{25,17},{2,26},{10... | collective-permute-start | bytes 491528 | tf_op jit(solution)/shard_map/ppermute | solution.py:27
  169.3 0.6 collective-permute-start.12
  169.9 0.9 slice.56
  171.1 1.6 collective-permute-start.11
  172.7 2.3 %collective-permute-done.13 = bf16[2,16,2560]{2,1,0:T(8,128)(2,1)S(1)} collective-permute-done((bf16[2,16,2560]{2,1,0:T(8,128)(2,1)S(1)}, bf16[2,16,2560]{2,1,0:T(8,128)(2,1)S(1)}, u32[]{:S(2)}, u32[]{:S(2)}) %collective-permute-start.13) | collective-permute-done | bytes 163872 | tf_op jit(solution)/shard_map/ppermute | solution.py:27
  175.0 4.9 %collective-permute-done.12 = bf16[2,16,2560]{2,1,0:T(8,128)(2,1)S(1)} collective-permute-done((bf16[2,16,2560]{2,1,0:T(8,128)(2,1)S(1)}, bf16[2,16,2560]{2,1,0:T(8,128)(2,1)S(1)}, u32[]{:S(2)}, u32[]{:S(2)}) %collective-permute-start.12) | collective-permute-done | bytes 163872 | tf_op jit(solution)/shard_map/ppermute | solution.py:27
  179.9 1.0 fusion.1
  181.5 0.9 copy-done.8
  182.4 2.8 %shard_map.106 = (bf16[128,4096]{1,0:T(8,128)(2,1)}, bf16[128,512]{1,0:T(8,128)(2,1)}, bf16[128,512]{1,0:T(8,128)(2,1)}) custom-call(s32[7]{0:T(128)} %concatenate.12.info, bf16[2,128,768]{2,1,0:T(8,128)(2,1)} %get-tuple-element.25.refs_0_, bf16[2,128,768]{2,1,0:T(8,128)(2,1)} %copy-done.5, bf16[2,128,768]{2,1,0:T(8,128)(2,1)} %copy-done.6, ...), custom_call_target="tpu_custom_call" | custom-call | tf_op jit(solution)/shard_map/pallas_call | solution.py:251
  185.2 2.5 %copy.19 = bf16[16,8,32,128]{3,2,1,0:T(8,128)(2,1)} copy(bf16[16,8,32,128]{3,1,2,0:T(8,128)(2,1)} %bitcast.55) | data formatting | bytes 2097152
  187.7 0.7 reshape.48
  188.4 0.7 reshape.49
  189.1 0.7 pad_maximum_fusion.2
  (60 shorter events, 5.0 us)
Async XLA Ops:
  8.0 94.8 %all-gather.3.cloned.1.call-start = ((), (), s32[]{:S(2)}) async-start(), calls=%async_computation.4 | async-start | bytes 5406720 | tf_op jit(solution)/shard_map/all_gather | solution.py:283
  9.0 7.5 %copy-start.3 = (bf16[1,128,32,128]{3,2,1,0:T(8,128)(2,1)S(1)}, bf16[1,128,32,128]{3,2,1,0:T(8,128)(2,1)}, u32[]{:S(2)}) copy-start(bf16[1,128,32,128]{3,2,1,0:T(8,128)(2,1)} %param.10) | copy-start | bytes 3145732
  9.0 4.3 %collective-permute-start.1 = (bf16[16,2560]{1,0:T(8,128)(2,1)S(1)}, bf16[16,2560]{1,0:T(8,128)(2,1)S(1)}, u32[]{:S(2)}, u32[]{:S(2)}) collective-permute-start(bf16[16,2560]{1,0:T(8,128)(2,1)S(1)} %get-tuple-element.42), channel_id=1, source_target_pairs={{0,32},{32,0},{1,33},{33,1},{2,34},{34,2},{3,35},{35,3},{4,36},{36... | collective-permute-start | bytes 245768 | tf_op jit(solution)/shard_map/ppermute | solution.py:35
  16.2 2.4 %collective-permute-start = (bf16[128,2560]{1,0:T(8,128)(2,1)}, bf16[128,2560]{1,0:T(8,128)(2,1)}, u32[]{:S(2)}, u32[]{:S(2)}) collective-permute-start(bf16[128,2560]{1,0:T(8,128)(2,1)} %get-tuple-element.35), channel_id=1, source_target_pairs={{0,32},{32,0},{1,33},{33,1},{2,34},{34,2},{3,35},{35,3},{4,36},{36... | collective-permute-start | bytes 1966088 | tf_op jit(solution)/shard_map/ppermute | solution.py:35
  19.8 8.8 %copy-start = (bf16[256,2560]{1,0:T(8,128)(2,1)}, bf16[256,2560]{1,0:T(8,128)(2,1)S(1)}, u32[]{:S(2)}) copy-start(bf16[256,2560]{1,0:T(8,128)(2,1)S(1)} %pad_maximum_fusion.own) | copy-start | bytes 3932164
  19.8 6.4 %copy-start.10 = (bf16[1,128,4,128]{3,2,1,0:T(4,128)(2,1)S(1)}, bf16[1,128,4,128]{3,2,1,0:T(4,128)(2,1)}, u32[]{:S(2)}) copy-start(bf16[1,128,4,128]{3,2,1,0:T(4,128)(2,1)} %param.9) | copy-start | bytes 393220
  19.8 7.0 %copy-start.11 = (bf16[1,128,4,128]{3,2,1,0:T(4,128)(2,1)S(1)}, bf16[1,128,4,128]{3,2,1,0:T(4,128)(2,1)}, u32[]{:S(2)}) copy-start(bf16[1,128,4,128]{3,2,1,0:T(4,128)(2,1)} %param.8) | copy-start | bytes 393220
  19.8 41.8 %collective-permute-start.2 = (bf16[256,2560]{1,0:T(8,128)(2,1)S(1)}, bf16[256,2560]{1,0:T(8,128)(2,1)}, u32[]{:S(2)}, u32[]{:S(2)}) collective-permute-start(bf16[256,2560]{1,0:T(8,128)(2,1)S(1)} %pad_maximum_fusion.own), channel_id=1, source_target_pairs={{0,64},{64,128},{128,192},{192,0},{1,65},{65,129},{129,193},{193,1... | collective-permute-start | bytes 3932168 | tf_op jit(solution)/shard_map/ppermute | solution.py:27
  19.9 41.7 %collective-permute-start.3 = (bf16[256,2560]{1,0:T(8,128)(2,1)S(1)}, bf16[256,2560]{1,0:T(8,128)(2,1)}, u32[]{:S(2)}, u32[]{:S(2)}) collective-permute-start(bf16[256,2560]{1,0:T(8,128)(2,1)S(1)} %pad_maximum_fusion.own), channel_id=1, source_target_pairs={{0,192},{64,0},{128,64},{192,128},{1,193},{65,1},{129,65},{193,129... | collective-permute-start | bytes 3932168 | tf_op jit(solution)/shard_map/ppermute | solution.py:27
  22.6 39.1 %all-to-all-start = ((bf16[4,128,1024]{2,1,0:T(8,128)(2,1)}), bf16[4,128,1024]{2,1,0:T(8,128)(2,1)S(1)}, u32[]{:S(2)}, u32[]{:S(2)}) async-start(bf16[4,128,1024]{2,1,0:T(8,128)(2,1)} %bitcast.42), calls=%async_computation | async-start | bytes 2097152 | tf_op jit(solution)/shard_map/all_to_all | solution.py:286
  26.1 139.0 %reduce-scatter.2.cloned.1.call-start = ((), (), s32[]{:S(2)}) async-start(), calls=%async_computation.3 | async-start | bytes 5898240 | tf_op jit(solution)/shard_map/reduce_scatter | solution.py:310
  28.6 0.9 copy-start.9
  30.9 38.7 %copy-start.14 = (s32[1,3]{1,0:T(1,128)S(1)}, s32[1,3]{1,0:T(1,128)}, u32[]{:S(2)}) copy-start(s32[1,3]{1,0:T(1,128)} %param.13) | copy-start | bytes 40
  61.7 22.0 %copy-start.1 = (bf16[4,128,1024]{2,1,0:T(8,128)(2,1)}, bf16[4,128,1024]{2,1,0:T(8,128)(2,1)S(1)}, u32[]{:S(2)}) copy-start(bf16[4,128,1024]{2,1,0:T(8,128)(2,1)S(1)} %all-to-all-done) | copy-start | bytes 3145732
  61.7 22.0 %collective-permute-start.6 = (bf16[512,1024]{1,0:T(8,128)(2,1)S(1)}, bf16[512,1024]{1,0:T(8,128)(2,1)S(1)}, u32[]{:S(2)}, u32[]{:S(2)}) collective-permute-start(bf16[512,1024]{1,0:T(8,128)(2,1)S(1)} %bitcast.45), channel_id=1, source_target_pairs={{0,32},{32,0},{1,33},{33,1},{2,34},{34,2},{3,35},{35,3},{4,36},{36... | collective-permute-start | bytes 3145736 | tf_op jit(solution)/shard_map/ppermute | solution.py:35
  64.8 17.4 %collective-permute-start.4 = (bf16[128,2560]{1,0:T(8,128)(2,1)S(1)}, bf16[128,2560]{1,0:T(8,128)(2,1)}, u32[]{:S(2)}, u32[]{:S(2)}) collective-permute-start(bf16[128,2560]{1,0:T(8,128)(2,1)S(1)} %slice.54), channel_id=1, source_target_pairs={{0,64},{64,128},{128,192},{192,0},{1,65},{65,129},{129,193},{193,1... | collective-permute-start | bytes 1966088 | tf_op jit(solution)/shard_map/ppermute | solution.py:27
  67.6 16.1 %collective-permute-start.5 = (bf16[128,2560]{1,0:T(8,128)(2,1)}, bf16[128,2560]{1,0:T(8,128)(2,1)}, u32[]{:S(2)}, u32[]{:S(2)}) collective-permute-start(bf16[128,2560]{1,0:T(8,128)(2,1)} %slice.55), channel_id=1, source_target_pairs={{0,192},{64,0},{128,64},{192,128},{1,193},{65,1},{129,65},{193,129... | collective-permute-start | bytes 1966088 | tf_op jit(solution)/shard_map/ppermute | solution.py:27
  83.7 1.0 copy-start.4
  96.7 26.8 %all-to-all-start.1 = ((bf16[8,128,768]{2,1,0:T(8,128)(2,1)}), bf16[8,128,768]{2,1,0:T(8,128)(2,1)S(1)}, u32[]{:S(2)}, u32[]{:S(2)}) async-start(bf16[8,128,768]{2,1,0:T(8,128)(2,1)} %maximum_bitcast_fusion), calls=%async_computation.1 | async-start | bytes 3145728 | tf_op jit(solution)/shard_map/all_to_all | solution.py:304
  110.1 13.4 %collective-permute-start.7 = (bf16[1024,512]{1,0:T(8,128)(2,1)}, bf16[1024,512]{1,0:T(8,128)(2,1)S(1)}, u32[]{:S(2)}, u32[]{:S(2)}) collective-permute-start(bf16[1024,512]{1,0:T(8,128)(2,1)} %shard_map.104), channel_id=1, source_target_pairs={{0,32},{32,0},{1,33},{33,1},{2,34},{34,2},{3,35},{35,3},{4,36},{36... | collective-permute-start | bytes 3145736 | tf_op jit(solution)/shard_map/ppermute | solution.py:35
  123.5 1.2 copy-start.2
  123.5 1.5 copy-start.15
  141.8 11.9 %collective-permute-start.8 = (bf16[2,128,768]{2,1,0:T(8,128)(2,1)}, bf16[2,128,768]{2,1,0:T(8,128)(2,1)S(1)}, u32[]{:S(2)}, u32[]{:S(2)}) collective-permute-start(bf16[2,128,768]{2,1,0:T(8,128)(2,1)} %get-tuple-element.26), channel_id=1, source_target_pairs={{0,64},{64,128},{128,192},{192,0},{1,65},{65,129},{129,193},{193,1... | collective-permute-start | bytes 1179656 | tf_op jit(solution)/shard_map/ppermute | solution.py:27
  142.2 18.7 %collective-permute-start.9 = (bf16[2,128,768]{2,1,0:T(8,128)(2,1)}, bf16[2,128,768]{2,1,0:T(8,128)(2,1)S(1)}, u32[]{:S(2)}, u32[]{:S(2)}) collective-permute-start(bf16[2,128,768]{2,1,0:T(8,128)(2,1)} %get-tuple-element.27), channel_id=1, source_target_pairs={{0,128},{64,192},{128,0},{192,64},{1,129},{65,193},{129,1},{193,65... | collective-permute-start | bytes 1179656 | tf_op jit(solution)/shard_map/ppermute | solution.py:27
  143.9 18.2 %collective-permute-start.10 = (bf16[2,128,768]{2,1,0:T(8,128)(2,1)}, bf16[2,128,768]{2,1,0:T(8,128)(2,1)S(1)}, u32[]{:S(2)}, u32[]{:S(2)}) collective-permute-start(bf16[2,128,768]{2,1,0:T(8,128)(2,1)} %get-tuple-element.28), channel_id=1, source_target_pairs={{0,192},{64,0},{128,64},{192,128},{1,193},{65,1},{129,65},{193,129... | collective-permute-start | bytes 1179656 | tf_op jit(solution)/shard_map/ppermute | solution.py:27
  153.7 17.4 %copy-start.5 = (bf16[2,128,768]{2,1,0:T(8,128)(2,1)}, bf16[2,128,768]{2,1,0:T(8,128)(2,1)S(1)}, u32[]{:S(2)}) copy-start(bf16[2,128,768]{2,1,0:T(8,128)(2,1)S(1)} %collective-permute-done.8.refs_1_) | copy-start | bytes 1179652
  160.9 10.2 %copy-start.6 = (bf16[2,128,768]{2,1,0:T(8,128)(2,1)}, bf16[2,128,768]{2,1,0:T(8,128)(2,1)S(1)}, u32[]{:S(2)}) copy-start(bf16[2,128,768]{2,1,0:T(8,128)(2,1)S(1)} %collective-permute-done.9.refs_2_) | copy-start | bytes 1179652
  162.1 8.9 %copy-start.7 = (bf16[2,128,768]{2,1,0:T(8,128)(2,1)}, bf16[2,128,768]{2,1,0:T(8,128)(2,1)S(1)}, u32[]{:S(2)}) copy-start(bf16[2,128,768]{2,1,0:T(8,128)(2,1)S(1)} %collective-permute-done.10.refs_3_) | copy-start | bytes 1179652
  166.3 6.5 %collective-permute-start.14 = (bf16[2,16,2560]{2,1,0:T(8,128)(2,1)S(1)}, bf16[2,16,2560]{2,1,0:T(8,128)(2,1)S(1)}, u32[]{:S(2)}, u32[]{:S(2)}) collective-permute-start(bf16[2,16,2560]{2,1,0:T(8,128)(2,1)S(1)} %get-tuple-element.37), channel_id=1, source_target_pairs={{0,24},{8,0},{16,8},{24,16},{1,25},{9,1},{17,9},{25,17},{2,26},{10... | collective-permute-start | bytes 491528 | tf_op jit(solution)/shard_map/ppermute | solution.py:27
  168.8 6.2 %collective-permute-start.13 = (bf16[2,16,2560]{2,1,0:T(8,128)(2,1)S(1)}, bf16[2,16,2560]{2,1,0:T(8,128)(2,1)S(1)}, u32[]{:S(2)}, u32[]{:S(2)}) collective-permute-start(bf16[2,16,2560]{2,1,0:T(8,128)(2,1)S(1)} %get-tuple-element.38), channel_id=1, source_target_pairs={{0,16},{8,24},{16,0},{24,8},{1,17},{9,25},{17,1},{25,9},{2,18},{10... | collective-permute-start | bytes 491528 | tf_op jit(solution)/shard_map/ppermute | solution.py:27
  169.3 10.6 %collective-permute-start.12 = (bf16[2,16,2560]{2,1,0:T(8,128)(2,1)S(1)}, bf16[2,16,2560]{2,1,0:T(8,128)(2,1)S(1)}, u32[]{:S(2)}, u32[]{:S(2)}) collective-permute-start(bf16[2,16,2560]{2,1,0:T(8,128)(2,1)S(1)} %get-tuple-element.36), channel_id=1, source_target_pairs={{0,8},{8,16},{16,24},{24,0},{1,9},{9,17},{17,25},{25,1},{2,10},{10... | collective-permute-start | bytes 491528 | tf_op jit(solution)/shard_map/ppermute | solution.py:27
  171.1 10.4 %collective-permute-start.11 = (bf16[4,128,768]{2,1,0:T(8,128)(2,1)S(1)}, bf16[4,128,768]{2,1,0:T(8,128)(2,1)S(1)}, u32[]{:S(2)}, u32[]{:S(2)}) collective-permute-start(bf16[4,128,768]{2,1,0:T(8,128)(2,1)S(1)} %pad_maximum_fusion.1), channel_id=1, source_target_pairs={{0,32},{32,0},{1,33},{33,1},{2,34},{34,2},{3,35},{35,3},{4,36},{36... | collective-permute-start | bytes 2359304 | tf_op jit(solution)/shard_map/ppermute | solution.py:35
  180.9 8.1 %collective-permute-start.15 = (f32[16,2560]{1,0:T(8,128)S(1)}, f32[16,2560]{1,0:T(8,128)S(1)}, u32[]{:S(2)}, u32[]{:S(2)}) collective-permute-start(f32[16,2560]{1,0:T(8,128)S(1)} %select_bitcast_fusion), channel_id=1, source_target_pairs={{0,32},{32,0},{1,33},{33,1},{2,34},{34,2},{3,35},{35,3},{4,36},{36... | collective-permute-start | bytes 491528 | tf_op jit(solution)/shard_map/ppermute | solution.py:35
  181.5 0.9 copy-start.8
  185.2 2.5 %copy-start.13 = (bf16[128,512]{1,0:T(8,128)(2,1)S(1)}, bf16[128,512]{1,0:T(8,128)(2,1)}, u32[]{:S(2)}) copy-start(bf16[128,512]{1,0:T(8,128)(2,1)} %get-tuple-element.30) | copy-start | bytes 393220
  185.2 3.2 %copy-start.12 = (bf16[128,512]{1,0:T(8,128)(2,1)S(1)}, bf16[128,512]{1,0:T(8,128)(2,1)}, u32[]{:S(2)}) copy-start(bf16[128,512]{1,0:T(8,128)(2,1)} %get-tuple-element.31) | copy-start | bytes 393220
Sparse Core Ops, SparseCore 0:
  14.1 84.5 all-gather.2
Sparse Core Ops, SparseCore 1:
  96.8 68.3 reduce-scatter.1

commit v5 on v3

--- a/solution.py
+++ b/solution.py
@@ -35,24 +35,28 @@
     return lax.ppermute(value, "core", [(0, 1), (1, 0)])
 
 
-def weight_kernel(factor, info, own, prev, succ, far0, far1, o_own, o_sib, term, rows, turned):
+def turn_kernel(o_own, o_sib, turned):
+    turned[:, :512] = o_own[...].T
+    turned[:, 512:] = o_sib[...].T
+
+
+def turn(o_own, o_sib):
+    whole = pl.BlockSpec(memory_space=pltpu.VMEM)
+    return pl.pallas_call(
+        turn_kernel,
+        out_shape=jax.ShapeDtypeStruct((1024, 1024), BF16),
+        in_specs=[whole, whole],
+        out_specs=whole,
+        compiler_params=params(),
+    )(o_own, o_sib)
+
+
+def weight_kernel(factor, info, *refs):
+    *parts, turned, term, rows = refs
     here, y = info[0], info[1]
-
-    @pl.when(pl.program_id(0) == 0)
-    def _():
-        turned[:, :512] = o_own[...].T
-        turned[:, 512:] = o_sib[...].T
-
-    def put(chip, rc, value):
-        rows[pl.ds(pl.multiple_of(rc * 512 + chip * TOK, TOK), TOK), :] = value
-
-    for rc in range(2):
-        part = slice(rc * TOK, (rc + 1) * TOK)
-        put(here, rc, own[part, :])
-        put(lax.rem(here + 3, 4), rc, prev[part, :])
-        put(lax.rem(here + 1, 4), rc, succ[part, :])
-    put(lax.rem(here + 2, 4), 0, far0[...])
-    put(lax.rem(here + 2, 4), 1, far1[...])
+    for place, (chip, rc) in enumerate((step, rc) for step in (0, 3, 1, 2) for rc in range(2)):
+        spot = rc * 512 + lax.rem(here + chip, 4) * TOK
+        rows[pl.ds(pl.multiple_of(spot, TOK), TOK), :] = parts[place][...]
     for part in range(4):
         product = jnp.dot(
             turned[part * 256 : part * 256 + 256, :], rows[...], preferred_element_type=F32
@@ -64,17 +68,16 @@
             term[f % 8, ry, part // 2] = product[at * 16 : at * 16 + 16, :]
 
 
-def weight_product(info, parts, o_own, o_sib, factor):
+def weight_product(info, parts, turned, factor):
     grid_spec = pltpu.PrefetchScalarGridSpec(
         num_scalar_prefetch=1,
         grid=(2560 // COLS,),
         in_specs=[pl.BlockSpec((p.shape[0], COLS), lambda n, info: (0, n)) for p in parts]
-        + [pl.BlockSpec((512, 1024), lambda n, info: (0, 0))] * 2,
+        + [pl.BlockSpec((1024, 1024), lambda n, info: (0, 0))],
         out_specs=(
             pl.BlockSpec((8, 4, 2, 16, COLS), lambda n, info: (0, 0, 0, 0, n)),
             pl.BlockSpec((1024, COLS), lambda n, info: (0, n)),
         ),
-        scratch_shapes=[pltpu.VMEM((1024, 1024), BF16)],
     )
     return pl.pallas_call(
         functools.partial(weight_kernel, factor),
@@ -87,7 +90,7 @@
         cost_estimate=pl.CostEstimate(
             flops=1024 * 1024, bytes_accessed=1024 * 1024, transcendentals=0
         ),
-    )(info, *parts, o_own, o_sib)
+    )(info, *parts, turned)
 
 
 def project_kernel(info, rows, block, out, weight, total):
@@ -282,13 +285,13 @@
     weight_mine, weight_theirs = halves(out_weight)
     weight_pair = jnp.stack([weight_mine, swap(weight_theirs)])
     near = jnp.stack([weight_pair] + [shift(weight_pair, "y", r) for r in (1, 2, 3)])
+
     o_split = jnp.transpose(attn_out.reshape(TOK, 4, 1024), (1, 0, 2))
+    grad_mine, grad_theirs = halves(out_grad[0])
+    own = (grad_mine, swap(grad_theirs))
+    weight = lax.all_gather(after(near, o_split, grad_mine), "z", axis=0, tiled=False)
     o_own = lax.all_to_all(o_split, "x", split_axis=0, concat_axis=0, tiled=True)
     o_own = o_own.reshape(512, 1024)
-
-    grad_mine, grad_theirs = halves(out_grad[0])
-    grad_chip = jnp.concatenate([grad_mine, swap(grad_theirs)], axis=0)
-    weight = lax.all_gather(after(near, grad_chip), "z", axis=0, tiled=False)
 
     packed = jnp.concatenate(
         [
@@ -300,14 +303,15 @@
     )
     packed = jnp.transpose(packed, (1, 0, 2))
 
-    own = after(grad_chip, weight_pair, o_split)
-    prev, succ = shift(own, "x", 1), shift(own, "x", -1)
-    prev, succ, packed, o_own = lax.optimization_barrier((prev, succ, packed, o_own))
+    prev0, prev1 = (shift(part, "x", 1) for part in own)
+    succ0, succ1 = (shift(part, "x", -1) for part in own)
+    prev0, succ1, packed, o_own = lax.optimization_barrier((prev0, succ1, packed, o_own))
     packed = lax.all_to_all(packed, ("x", "core"), split_axis=0, concat_axis=0, tiled=True)
     packed = packed.reshape(1024, 768)
-    far0, far1 = shift(prev[:TOK], "x", 1), shift(succ[TOK:], "x", -1)
     o_sib = swap(o_own)
-    term, rows = weight_product(info, (own, prev, succ, far0, far1), o_own, o_sib, factor)
+    far0, far1 = shift(prev0, "x", 1), shift(succ1, "x", -1)
+    parts = (*own, prev0, prev1, succ0, succ1, far0, far1)
+    term, rows = weight_product(info, parts, turn(o_own, o_sib), factor)
 
     summed = lax.psum_scatter(term, "z", scatter_dimension=0, tiled=True)[0]
 
@@ -321,7 +325,12 @@
     )
 
     summed = after(summed, *back[1:])
-    summed = add(summed[0], *(shift(summed[r], "y", r) for r in (1, 2, 3)))
+    summed = [summed[0]] + [shift(summed[r], "y", r) for r in (1, 2, 3)]
+    grad_queries = grad_queries.reshape(1, TOK, 32, 128)
+    *summed, grad_queries, grad_keys, grad_values = lax.optimization_barrier(
+        (*summed, grad_queries, grad_keys, grad_values)
+    )
+    summed = add(*summed)
     keep = jnp.where(core == 0, summed[0], summed[1])
     give = jnp.where(core == 0, summed[1], summed[0])
     come = swap(give)
@@ -330,7 +339,7 @@
     ).astype(F32)
 
     return (
-        grad_queries.reshape(1, TOK, 32, 128),
+        grad_queries,
         grad_keys.reshape(1, TOK, 4, 128),
         grad_values.reshape(1, TOK, 4, 128),
         grad_out_weight,

time: 206 us -> 193 us (0.937)
  waiting for transfers between devices: 87.5 us -> 72.3 us
  local copies, waits for them, and re-layouts: 18.1 us -> 14.2 us
  starting transfers between devices: 30.8 us -> 34.3 us
  Pallas kernels: 46.6 us -> 49.8 us
    all_to_all x1, waiting for transfers between devices: 32.3 us -> 0.01 us  [per_device(): lax.all_to_all(o_split, 'x', split_axis=0, concat_axis=0, tiled=True)]
    ppermute x13 -> x15, waiting for transfers between devices: 48.2 us -> 66.1 us  [shift(): lax.ppermute(value, axis, [(i, (i + by) % size) for i in range(size)])]
    pallas_call x0 -> x1, Pallas kernels: none -> 3.55 us  [turn(): pl.pallas_call(turn_kernel, out_shape=jax.ShapeDtypeStruct((1024, 1024),...]
    ppermute x13 -> x15, starting transfers between devices: 14.2 us -> 17.2 us  [shift(): lax.ppermute(value, axis, [(i, (i + by) % size) for i in range(size)])]
    slice x2 -> x0, local copies, waits for them, and re-layouts: 2.26 us -> none  [per_device(): far0, far1 = (shift(prev[:TOK], 'x', 1), shift(succ[TOK:], 'x', -1))]
    unnamed x35 -> x33, local copies, waits for them, and re-layouts: 7.43 us -> 6.42 us
  transfers between devices with their start and end apart: 23 -> 25, of which waited for: 13 -> 13; matrix products, arithmetic and copies ran while one was open for 8% -> 7% of each run, Pallas kernels for 23% -> 26%
where the time goes in v5:
time: 193 us; the launch traced here: 192 us
  waiting for transfers between devices  72.3 us (37%)
  Pallas kernels  49.8 us (26%)
  starting transfers between devices  34.3 us (18%)
  local copies, waits for them, and re-layouts  14.2 us (7%)
  between operations  14.2 us (7%)
  other arithmetic  7.14 us (4%)
    ppermute x15, waiting for transfers between devices, shift(): lax.ppermute(value, axis, [(i, (i + by) % size) for i in range(size)])  66.1 us
    ppermute x15, starting transfers between devices, shift(): lax.ppermute(value, axis, [(i, (i + by) % size) for i in range(size)])  17.2 us
    pallas_call x1, Pallas kernels, attention(): pl.pallas_call(attention_kernel, out_shape=[jax.ShapeDtypeStruct((2, TOK,...  16.8 us
    pallas_call x2, Pallas kernels, project(): pl.pallas_call(project_kernel, out_shape=jax.ShapeDtypeStruct((1024, 512)...  15.2 us
    pallas_call x1, Pallas kernels, weight_product(): pl.pallas_call(functools.partial(weight_kernel, factor), out_shape=(jax.S...  11.5 us
    ppermute x6, starting transfers between devices, swap(): return lax.ppermute(value, 'core', [(0, 1), (1, 0)])  8.81 us
    unnamed x33, local copies, waits for them, and re-layouts  6.42 us
    all_to_all x1, waiting for transfers between devices, per_device(): lax.all_to_all(packed, ('x', 'core'), split_axis=0, concat_axis=0, tiled=...  5.23 us
  transfers between devices with their start and end apart: 25, of which 13 were waited for; matrix products, arithmetic and copies ran while one was open for 7% of the time, Pallas kernels for 26%

profile of v5, /device:TPU:1, one launch (start us, length us, event | category | flops | bytes accessed | tf_op | source)
XLA Modules:
  0.0 192.0 jit_solution(8929328686605075906)
XLA Ops:
  7.2 1.0 select_bitcast_fusion.1
  8.3 3.3 %collective-permute-start.8 = (bf16[16,2560]{1,0:T(8,128)(2,1)S(1)}, bf16[16,2560]{1,0:T(8,128)(2,1)S(1)}, u32[]{:S(2)}, u32[]{:S(2)}) collective-permute-start(bf16[16,2560]{1,0:T(8,128)(2,1)S(1)} %get-tuple-element.59), channel_id=1, source_target_pairs={{0,32},{32,0},{1,33},{33,1},{2,34},{34,2},{3,35},{35,3},{4,36},{36... | collective-permute-start | bytes 245768 | tf_op jit(solution)/shard_map/ppermute | solution.py:35
  11.6 0.9 collective-permute-done.8
  13.2 2.2 %collective-permute-start.10 = (bf16[2,16,2560]{2,1,0:T(8,128)(2,1)}, bf16[2,16,2560]{2,1,0:T(8,128)(2,1)S(1)}, u32[]{:S(2)}, u32[]{:S(2)}) collective-permute-start(bf16[2,16,2560]{2,1,0:T(8,128)(2,1)} %get-tuple-element.57), channel_id=1, source_target_pairs={{0,16},{8,24},{16,0},{24,8},{1,17},{9,25},{17,1},{25,9},{2,18},{10... | collective-permute-start | bytes 491528 | tf_op jit(solution)/shard_map/ppermute | solution.py:27
  15.4 1.1 collective-permute-start.11
  16.4 2.2 %broadcast_select_fusion = (bf16[128,2560]{1,0:T(8,128)(2,1)}, bf16[128,2560]{1,0:T(8,128)(2,1)S(1)}) fusion(pred[]{:T(512)S(6)} %eq.2, bf16[128,5120]{1,0:T(8,128)(2,1)} %bitcast.55), kind=kLoop, calls=%fused_computation.4 | loop fusion | flops 655360 | bytes 2621441 | tf_op jit(solution)/shard_map/jit(_where)/select_n | solution.py:283
  19.0 1.3 copy.21
  20.5 2.6 %collective-permute-done.10 = bf16[2,16,2560]{2,1,0:T(8,128)(2,1)S(1)} collective-permute-done((bf16[2,16,2560]{2,1,0:T(8,128)(2,1)}, bf16[2,16,2560]{2,1,0:T(8,128)(2,1)S(1)}, u32[]{:S(2)}, u32[]{:S(2)}) %collective-permute-start.10) | collective-permute-done | bytes 163872 | tf_op jit(solution)/shard_map/ppermute | solution.py:27
  23.1 0.8 collective-permute-done.11
  23.9 0.9 pad_maximum_fusion.1
  24.9 1.5 collective-permute-start
  26.4 3.5 %all-to-all-start = ((bf16[4,128,1024]{2,1,0:T(8,128)(2,1)}), bf16[4,128,1024]{2,1,0:T(8,128)(2,1)S(1)}, u32[]{:S(2)}, u32[]{:S(2)}) async-start(bf16[4,128,1024]{2,1,0:T(8,128)(2,1)} %bitcast.46), calls=%async_computation | async-start | bytes 2097152 | tf_op jit(solution)/shard_map/all_to_all | solution.py:293
  30.0 1.4 collective-permute-start.1
  31.4 1.4 collective-permute-start.2
  32.8 1.7 reshape.39
  35.5 1.3 maximum_bitcast_fusion
  36.8 22.2 %collective-permute-done.1.refs_2_ = bf16[128,2560]{1,0:T(8,128)(2,1)} collective-permute-done((bf16[128,2560]{1,0:T(8,128)(2,1)S(1)}, bf16[128,2560]{1,0:T(8,128)(2,1)}, u32[]{:S(2)}, u32[]{:S(2)}) %collective-permute-start.1) | collective-permute-done | bytes 655392 | tf_op jit(solution)/shard_map/ppermute | solution.py:27
  59.0 0.9 collective-permute-start.7
  60.6 0.8 collective-permute-start.3
  61.4 2.6 %collective-permute-start.6 = (bf16[128,2560]{1,0:T(8,128)(2,1)}, bf16[128,2560]{1,0:T(8,128)(2,1)}, u32[]{:S(2)}, u32[]{:S(2)}) collective-permute-start(bf16[128,2560]{1,0:T(8,128)(2,1)} %collective-permute-done.2.refs_5_), channel_id=1, source_target_pairs={{0,192},{64,0},{128,64},{192,128},{1,193},{65,1},{129,65},{193,129... | collective-permute-start | bytes 1966088 | tf_op jit(solution)/shard_map/ppermute | solution.py:27
  64.7 1.0 copy-done.4
  65.6 3.6 %shard_map.102.refs_8_ = bf16[1024,1024]{1,0:T(8,128)(2,1)} custom-call(bf16[512,1024]{1,0:T(8,128)(2,1)} %bitcast.50, bf16[512,1024]{1,0:T(8,128)(2,1)} %copy-done.4), custom_call_target="tpu_custom_call" | custom-call | tf_op jit(solution)/shard_map/pallas_call | solution.py:45
  69.2 7.1 %collective-permute-done.4.refs_4_ = bf16[128,2560]{1,0:T(8,128)(2,1)} collective-permute-done((bf16[128,2560]{1,0:T(8,128)(2,1)S(1)}, bf16[128,2560]{1,0:T(8,128)(2,1)}, u32[]{:S(2)}, u32[]{:S(2)}) %collective-permute-start.4) | collective-permute-done | bytes 655392 | tf_op jit(solution)/shard_map/ppermute | solution.py:27
  76.3 1.5 collective-permute-done.3.refs_3_
  77.8 14.0 %collective-permute-done.5.refs_6_ = bf16[128,2560]{1,0:T(8,128)(2,1)} collective-permute-done((bf16[128,2560]{1,0:T(8,128)(2,1)}, bf16[128,2560]{1,0:T(8,128)(2,1)}, u32[]{:S(2)}, u32[]{:S(2)}) %collective-permute-start.5) | collective-permute-done | bytes 655392 | tf_op jit(solution)/shard_map/ppermute | solution.py:27
  91.9 11.5 %shard_map.103 = (bf16[8,4,2,16,2560]{4,3,2,1,0:T(8,128)(2,1)}, bf16[1024,2560]{1,0:T(8,128)(2,1)}) custom-call(s32[7]{0:T(128)} %concatenate.9.info, bf16[128,2560]{1,0:T(8,128)(2,1)} %copy-done.1, bf16[128,2560]{1,0:T(8,128)(2,1)} %copy-done.9, bf16[128,2560]{1,0:T(8,128)(2,1)} %collective-permute-done.1.refs_2_, ...), custom_call_target="tpu_custom_call" | custom-call | flops 1048576 | bytes 1048576 | tf_op jit(solution)/shard_map/pallas_call | solution.py:82
  103.4 4.7 %all-to-all-start.1 = ((bf16[8,128,768]{2,1,0:T(8,128)(2,1)}), bf16[8,128,768]{2,1,0:T(8,128)(2,1)S(1)}, u32[]{:S(2)}, u32[]{:S(2)}) async-start(bf16[8,128,768]{2,1,0:T(8,128)(2,1)} %maximum_bitcast_fusion), calls=%async_computation.2 | async-start | bytes 3145728 | tf_op jit(solution)/shard_map/all_to_all | solution.py:309
  108.1 7.4 %shard_map.105 = bf16[1024,512]{1,0:T(8,128)(2,1)} custom-call(s32[7]{0:T(128)} %concatenate.9.info, bf16[1024,2560]{1,0:T(8,128)(2,1)} %get-tuple-element.31.rows, bf16[8,4,2,16,2560]{4,3,2,1,0:T(8,128)(2,1)} %bitcast.47), custom_call_target="tpu_custom_call" | custom-call | flops 1048576 | bytes 1048576 | tf_op jit(solution)/shard_map/pallas_call | solution.py:136
  115.8 7.8 %shard_map.104.mine = f32[1024,512]{1,0:T(8,128)} custom-call(s32[7]{0:T(128)} %concatenate.9.info, bf16[1024,2560]{1,0:T(8,128)(2,1)} %get-tuple-element.31.rows, bf16[8,4,2,16,2560]{4,3,2,1,0:T(8,128)(2,1)} %bitcast.48), custom_call_target="tpu_custom_call" | custom-call | flops 1048576 | bytes 1048576 | tf_op jit(solution)/shard_map/pallas_call | solution.py:136
  123.5 5.2 %all-to-all-done.1 = bf16[8,128,768]{2,1,0:T(8,128)(2,1)S(1)} async-done(((bf16[8,128,768]{2,1,0:T(8,128)(2,1)}), bf16[8,128,768]{2,1,0:T(8,128)(2,1)S(1)}, u32[]{:S(2)}, u32[]{:S(2)}) %all-to-all-start.1) | async-done | bytes 1572896 | tf_op jit(solution)/shard_map/all_to_all | solution.py:309
  128.8 1.2 copy-done.2
  130.3 16.8 %shard_map.106 = (bf16[2,128,768]{2,1,0:T(8,128)(2,1)}, bf16[2,128,768]{2,1,0:T(8,128)(2,1)}, bf16[2,128,768]{2,1,0:T(8,128)(2,1)}, bf16[2,128,768]{2,1,0:T(8,128)(2,1)}) custom-call(s32[7]{0:T(128)} %concatenate.9.info, bf16[1024,768]{1,0:T(8,128)(2,1)} %bitcast.52, bf16[1024,768]{1,0:T(8,128)(2,1)} %bitcast.53, bf16[1024,768]{1,0:T(8,128)(2,1)} %bitcast.54, ...), custom_call_target="tpu_custom_call" | custom-call | flops 14000000000 | bytes 8388608 | tf_op jit(solution)/shard_map/pallas_call | solution.py:224
  147.4 1.7 collective-permute-start.14
  149.1 0.8 collective-permute-start.15
  149.9 0.9 slice.52
  150.8 8.1 %collective-permute-done.13.refs_1_ = bf16[2,128,768]{2,1,0:T(8,128)(2,1)S(1)} collective-permute-done((bf16[2,128,768]{2,1,0:T(8,128)(2,1)}, bf16[2,128,768]{2,1,0:T(8,128)(2,1)S(1)}, u32[]{:S(2)}, u32[]{:S(2)}) %collective-permute-start.13) | collective-permute-done | bytes 393248 | tf_op jit(solution)/shard_map/ppermute | solution.py:27
  159.0 7.1 %collective-permute-done.14.refs_2_ = bf16[2,128,768]{2,1,0:T(8,128)(2,1)S(1)} collective-permute-done((bf16[2,128,768]{2,1,0:T(8,128)(2,1)}, bf16[2,128,768]{2,1,0:T(8,128)(2,1)S(1)}, u32[]{:S(2)}, u32[]{:S(2)}) %collective-permute-start.14) | collective-permute-done | bytes 393248 | tf_op jit(solution)/shard_map/ppermute | solution.py:27
  166.1 1.2 collective-permute-done.15.refs_3_
  167.5 1.8 collective-permute-start.19
  169.3 1.2 slice_bitcast_fusion
  171.1 3.0 %collective-permute-start.17 = (bf16[2,16,2560]{2,1,0:T(8,128)(2,1)S(1)}, bf16[2,16,2560]{2,1,0:T(8,128)(2,1)S(1)}, u32[]{:S(2)}, u32[]{:S(2)}) collective-permute-start(bf16[2,16,2560]{2,1,0:T(8,128)(2,1)S(1)} %get-tuple-element.51), channel_id=1, source_target_pairs={{0,16},{8,24},{16,0},{24,8},{1,17},{9,25},{17,1},{25,9},{2,18},{10... | collective-permute-start | bytes 491528 | tf_op jit(solution)/shard_map/ppermute | solution.py:27
  174.7 0.9 copy-done.8
  175.6 2.8 %shard_map.107 = (bf16[128,4096]{1,0:T(8,128)(2,1)}, bf16[128,512]{1,0:T(8,128)(2,1)}, bf16[128,512]{1,0:T(8,128)(2,1)}) custom-call(s32[7]{0:T(128)} %concatenate.9.info, bf16[2,128,768]{2,1,0:T(8,128)(2,1)} %get-tuple-element.37.refs_0_, bf16[2,128,768]{2,1,0:T(8,128)(2,1)} %copy-done.5, bf16[2,128,768]{2,1,0:T(8,128)(2,1)} %copy-done.6, ...), custom_call_target="tpu_custom_call" | custom-call | tf_op jit(solution)/shard_map/pallas_call | solution.py:255
  178.4 2.5 %copy.19 = bf16[16,8,32,128]{3,2,1,0:T(8,128)(2,1)} copy(bf16[16,8,32,128]{3,1,2,0:T(8,128)(2,1)} %bitcast.59) | data formatting | bytes 2097152
  180.8 1.1 collective-permute-done.17
  182.0 0.9 collective-permute-start.20
  183.7 0.7 reshape.47
  184.4 0.7 pad_maximum_fusion.2
  (69 shorter events, 6.8 us)
Async XLA Ops:
  7.2 11.5 %copy-start.3 = (bf16[1,128,32,128]{3,2,1,0:T(8,128)(2,1)S(1)}, bf16[1,128,32,128]{3,2,1,0:T(8,128)(2,1)}, u32[]{:S(2)}) copy-start(bf16[1,128,32,128]{3,2,1,0:T(8,128)(2,1)} %param.10) | copy-start | bytes 3145732
  7.2 100.9 %all-gather.3.cloned.1.call-start = ((), (), s32[]{:S(2)}) async-start(), calls=%async_computation.4 | async-start | bytes 5898240 | tf_op jit(solution)/shard_map/all_gather | solution.py:292
  8.3 4.3 %collective-permute-start.8 = (bf16[16,2560]{1,0:T(8,128)(2,1)S(1)}, bf16[16,2560]{1,0:T(8,128)(2,1)S(1)}, u32[]{:S(2)}, u32[]{:S(2)}) collective-permute-start(bf16[16,2560]{1,0:T(8,128)(2,1)S(1)} %get-tuple-element.59), channel_id=1, source_target_pairs={{0,32},{32,0},{1,33},{33,1},{2,34},{34,2},{3,35},{35,3},{4,36},{36... | collective-permute-start | bytes 245768 | tf_op jit(solution)/shard_map/ppermute | solution.py:35
  13.2 7.3 %collective-permute-start.9 = (bf16[2,16,2560]{2,1,0:T(8,128)(2,1)}, bf16[2,16,2560]{2,1,0:T(8,128)(2,1)S(1)}, u32[]{:S(2)}, u32[]{:S(2)}) collective-permute-start(bf16[2,16,2560]{2,1,0:T(8,128)(2,1)} %get-tuple-element.57), channel_id=1, source_target_pairs={{0,8},{8,16},{16,24},{24,0},{1,9},{9,17},{17,25},{25,1},{2,10},{10... | collective-permute-start | bytes 491528 | tf_op jit(solution)/shard_map/ppermute | solution.py:27
  13.2 9.9 %collective-permute-start.10 = (bf16[2,16,2560]{2,1,0:T(8,128)(2,1)}, bf16[2,16,2560]{2,1,0:T(8,128)(2,1)S(1)}, u32[]{:S(2)}, u32[]{:S(2)}) collective-permute-start(bf16[2,16,2560]{2,1,0:T(8,128)(2,1)} %get-tuple-element.57), channel_id=1, source_target_pairs={{0,16},{8,24},{16,0},{24,8},{1,17},{9,25},{17,1},{25,9},{2,18},{10... | collective-permute-start | bytes 491528 | tf_op jit(solution)/shard_map/ppermute | solution.py:27
  15.4 8.5 %collective-permute-start.11 = (bf16[2,16,2560]{2,1,0:T(8,128)(2,1)}, bf16[2,16,2560]{2,1,0:T(8,128)(2,1)S(1)}, u32[]{:S(2)}, u32[]{:S(2)}) collective-permute-start(bf16[2,16,2560]{2,1,0:T(8,128)(2,1)} %get-tuple-element.57), channel_id=1, source_target_pairs={{0,24},{8,0},{16,8},{24,16},{1,25},{9,1},{17,9},{25,17},{2,26},{10... | collective-permute-start | bytes 491528 | tf_op jit(solution)/shard_map/ppermute | solution.py:27
  18.7 41.2 %copy-start.1 = (bf16[128,2560]{1,0:T(8,128)(2,1)}, bf16[128,2560]{1,0:T(8,128)(2,1)S(1)}, u32[]{:S(2)}) copy-start(bf16[128,2560]{1,0:T(8,128)(2,1)S(1)} %get-tuple-element.49.refs_0_) | copy-start | bytes 1966084
  24.9 6.5 %collective-permute-start = (bf16[128,2560]{1,0:T(8,128)(2,1)}, bf16[128,2560]{1,0:T(8,128)(2,1)S(1)}, u32[]{:S(2)}, u32[]{:S(2)}) collective-permute-start(bf16[128,2560]{1,0:T(8,128)(2,1)} %get-tuple-element.48), channel_id=1, source_target_pairs={{0,32},{32,0},{1,33},{33,1},{2,34},{34,2},{3,35},{35,3},{4,36},{36... | collective-permute-start | bytes 1966088 | tf_op jit(solution)/shard_map/ppermute | solution.py:35
  26.4 32.6 %all-to-all-start = ((bf16[4,128,1024]{2,1,0:T(8,128)(2,1)}), bf16[4,128,1024]{2,1,0:T(8,128)(2,1)S(1)}, u32[]{:S(2)}, u32[]{:S(2)}) async-start(bf16[4,128,1024]{2,1,0:T(8,128)(2,1)} %bitcast.46), calls=%async_computation | async-start | bytes 2097152 | tf_op jit(solution)/shard_map/all_to_all | solution.py:293
  29.9 4.9 %copy-start.10 = (bf16[1,128,4,128]{3,2,1,0:T(4,128)(2,1)S(1)}, bf16[1,128,4,128]{3,2,1,0:T(4,128)(2,1)}, u32[]{:S(2)}) copy-start(bf16[1,128,4,128]{3,2,1,0:T(4,128)(2,1)} %param.8) | copy-start | bytes 393220
  29.9 139.3 %reduce-scatter.2.cloned.1.call-start = ((), (), s32[]{:S(2)}) async-start(), calls=%async_computation.3 | async-start | bytes 5898240 | tf_op jit(solution)/shard_map/reduce_scatter | solution.py:316
  30.0 29.0 %collective-permute-start.1 = (bf16[128,2560]{1,0:T(8,128)(2,1)S(1)}, bf16[128,2560]{1,0:T(8,128)(2,1)}, u32[]{:S(2)}, u32[]{:S(2)}) collective-permute-start(bf16[128,2560]{1,0:T(8,128)(2,1)S(1)} %get-tuple-element.49.refs_0_), channel_id=1, source_target_pairs={{0,64},{64,128},{128,192},{192,0},{1,65},{65,129},{129,193},{193,1... | collective-permute-start | bytes 1966088 | tf_op jit(solution)/shard_map/ppermute | solution.py:27
  31.4 29.2 %copy-start.9 = (bf16[128,2560]{1,0:T(8,128)(2,1)}, bf16[128,2560]{1,0:T(8,128)(2,1)S(1)}, u32[]{:S(2)}) copy-start(bf16[128,2560]{1,0:T(8,128)(2,1)S(1)} %collective-permute-done.refs_1_) | copy-start | bytes 1966084
  31.4 27.6 %collective-permute-start.2 = (bf16[128,2560]{1,0:T(8,128)(2,1)S(1)}, bf16[128,2560]{1,0:T(8,128)(2,1)}, u32[]{:S(2)}, u32[]{:S(2)}) collective-permute-start(bf16[128,2560]{1,0:T(8,128)(2,1)S(1)} %collective-permute-done.refs_1_), channel_id=1, source_target_pairs={{0,192},{64,0},{128,64},{192,128},{1,193},{65,1},{129,65},{193,129... | collective-permute-start | bytes 1966088 | tf_op jit(solution)/shard_map/ppermute | solution.py:27
  34.5 0.9 copy-start.11
  35.4 28.7 %copy-start.14 = (s32[1,3]{1,0:T(1,128)S(1)}, s32[1,3]{1,0:T(1,128)}, u32[]{:S(2)}) copy-start(s32[1,3]{1,0:T(1,128)} %param.13) | copy-start | bytes 40
  59.0 5.6 %copy-start = (bf16[4,128,1024]{2,1,0:T(8,128)(2,1)}, bf16[4,128,1024]{2,1,0:T(8,128)(2,1)S(1)}, u32[]{:S(2)}) copy-start(bf16[4,128,1024]{2,1,0:T(8,128)(2,1)S(1)} %all-to-all-done) | copy-start | bytes 3145732
  59.0 5.6 %collective-permute-start.7 = (bf16[512,1024]{1,0:T(8,128)(2,1)S(1)}, bf16[512,1024]{1,0:T(8,128)(2,1)S(1)}, u32[]{:S(2)}, u32[]{:S(2)}) collective-permute-start(bf16[512,1024]{1,0:T(8,128)(2,1)S(1)} %bitcast.49), channel_id=1, source_target_pairs={{0,32},{32,0},{1,33},{33,1},{2,34},{34,2},{3,35},{35,3},{4,36},{36... | collective-permute-start | bytes 3145736 | tf_op jit(solution)/shard_map/ppermute | solution.py:35
  59.9 16.4 %collective-permute-start.4 = (bf16[128,2560]{1,0:T(8,128)(2,1)S(1)}, bf16[128,2560]{1,0:T(8,128)(2,1)}, u32[]{:S(2)}, u32[]{:S(2)}) collective-permute-start(bf16[128,2560]{1,0:T(8,128)(2,1)S(1)} %get-tuple-element.49.refs_0_), channel_id=1, source_target_pairs={{0,192},{64,0},{128,64},{192,128},{1,193},{65,1},{129,65},{193,129... | collective-permute-start | bytes 1966088 | tf_op jit(solution)/shard_map/ppermute | solution.py:27
  60.6 17.3 %collective-permute-start.3 = (bf16[128,2560]{1,0:T(8,128)(2,1)S(1)}, bf16[128,2560]{1,0:T(8,128)(2,1)}, u32[]{:S(2)}, u32[]{:S(2)}) collective-permute-start(bf16[128,2560]{1,0:T(8,128)(2,1)S(1)} %collective-permute-done.refs_1_), channel_id=1, source_target_pairs={{0,64},{64,128},{128,192},{192,0},{1,65},{65,129},{129,193},{193,1... | collective-permute-start | bytes 1966088 | tf_op jit(solution)/shard_map/ppermute | solution.py:27
  61.4 30.5 %collective-permute-start.5 = (bf16[128,2560]{1,0:T(8,128)(2,1)}, bf16[128,2560]{1,0:T(8,128)(2,1)}, u32[]{:S(2)}, u32[]{:S(2)}) collective-permute-start(bf16[128,2560]{1,0:T(8,128)(2,1)} %collective-permute-done.1.refs_2_), channel_id=1, source_target_pairs={{0,64},{64,128},{128,192},{192,0},{1,65},{65,129},{129,193},{193,1... | collective-permute-start | bytes 1966088 | tf_op jit(solution)/shard_map/ppermute | solution.py:27
  61.4 30.4 %collective-permute-start.6 = (bf16[128,2560]{1,0:T(8,128)(2,1)}, bf16[128,2560]{1,0:T(8,128)(2,1)}, u32[]{:S(2)}, u32[]{:S(2)}) collective-permute-start(bf16[128,2560]{1,0:T(8,128)(2,1)} %collective-permute-done.2.refs_5_), channel_id=1, source_target_pairs={{0,192},{64,0},{128,64},{192,128},{1,193},{65,1},{129,65},{193,129... | collective-permute-start | bytes 1966088 | tf_op jit(solution)/shard_map/ppermute | solution.py:27
  64.7 1.0 copy-start.4
  103.4 25.4 %all-to-all-start.1 = ((bf16[8,128,768]{2,1,0:T(8,128)(2,1)}), bf16[8,128,768]{2,1,0:T(8,128)(2,1)S(1)}, u32[]{:S(2)}, u32[]{:S(2)}) async-start(bf16[8,128,768]{2,1,0:T(8,128)(2,1)} %maximum_bitcast_fusion), calls=%async_computation.2 | async-start | bytes 3145728 | tf_op jit(solution)/shard_map/all_to_all | solution.py:309
  115.4 13.3 %collective-permute-start.12 = (bf16[1024,512]{1,0:T(8,128)(2,1)}, bf16[1024,512]{1,0:T(8,128)(2,1)S(1)}, u32[]{:S(2)}, u32[]{:S(2)}) collective-permute-start(bf16[1024,512]{1,0:T(8,128)(2,1)} %shard_map.105), channel_id=1, source_target_pairs={{0,32},{32,0},{1,33},{33,1},{2,34},{34,2},{3,35},{35,3},{4,36},{36... | collective-permute-start | bytes 3145736 | tf_op jit(solution)/shard_map/ppermute | solution.py:35
  128.8 1.2 copy-start.2
  128.8 1.5 copy-start.15
  147.1 11.9 %collective-permute-start.13 = (bf16[2,128,768]{2,1,0:T(8,128)(2,1)}, bf16[2,128,768]{2,1,0:T(8,128)(2,1)S(1)}, u32[]{:S(2)}, u32[]{:S(2)}) collective-permute-start(bf16[2,128,768]{2,1,0:T(8,128)(2,1)} %get-tuple-element.33), channel_id=1, source_target_pairs={{0,64},{64,128},{128,192},{192,0},{1,65},{65,129},{129,193},{193,1... | collective-permute-start | bytes 1179656 | tf_op jit(solution)/shard_map/ppermute | solution.py:27
  147.4 18.7 %collective-permute-start.14 = (bf16[2,128,768]{2,1,0:T(8,128)(2,1)}, bf16[2,128,768]{2,1,0:T(8,128)(2,1)S(1)}, u32[]{:S(2)}, u32[]{:S(2)}) collective-permute-start(bf16[2,128,768]{2,1,0:T(8,128)(2,1)} %get-tuple-element.34), channel_id=1, source_target_pairs={{0,128},{64,192},{128,0},{192,64},{1,129},{65,193},{129,1},{193,65... | collective-permute-start | bytes 1179656 | tf_op jit(solution)/shard_map/ppermute | solution.py:27
  149.1 18.2 %collective-permute-start.15 = (bf16[2,128,768]{2,1,0:T(8,128)(2,1)}, bf16[2,128,768]{2,1,0:T(8,128)(2,1)S(1)}, u32[]{:S(2)}, u32[]{:S(2)}) collective-permute-start(bf16[2,128,768]{2,1,0:T(8,128)(2,1)} %get-tuple-element.35), channel_id=1, source_target_pairs={{0,192},{64,0},{128,64},{192,128},{1,193},{65,1},{129,65},{193,129... | collective-permute-start | bytes 1179656 | tf_op jit(solution)/shard_map/ppermute | solution.py:27
  159.0 15.7 %copy-start.5 = (bf16[2,128,768]{2,1,0:T(8,128)(2,1)}, bf16[2,128,768]{2,1,0:T(8,128)(2,1)S(1)}, u32[]{:S(2)}) copy-start(bf16[2,128,768]{2,1,0:T(8,128)(2,1)S(1)} %collective-permute-done.13.refs_1_) | copy-start | bytes 1179652
  166.1 8.6 %copy-start.6 = (bf16[2,128,768]{2,1,0:T(8,128)(2,1)}, bf16[2,128,768]{2,1,0:T(8,128)(2,1)S(1)}, u32[]{:S(2)}) copy-start(bf16[2,128,768]{2,1,0:T(8,128)(2,1)S(1)} %collective-permute-done.14.refs_2_) | copy-start | bytes 1179652
  167.3 7.3 %copy-start.7 = (bf16[2,128,768]{2,1,0:T(8,128)(2,1)}, bf16[2,128,768]{2,1,0:T(8,128)(2,1)S(1)}, u32[]{:S(2)}) copy-start(bf16[2,128,768]{2,1,0:T(8,128)(2,1)S(1)} %collective-permute-done.15.refs_3_) | copy-start | bytes 1179652
  167.5 7.2 %collective-permute-start.19 = (bf16[4,128,768]{2,1,0:T(8,128)(2,1)S(1)}, bf16[4,128,768]{2,1,0:T(8,128)(2,1)S(1)}, u32[]{:S(2)}, u32[]{:S(2)}) collective-permute-start(bf16[4,128,768]{2,1,0:T(8,128)(2,1)S(1)} %pad_maximum_fusion), channel_id=1, source_target_pairs={{0,32},{32,0},{1,33},{33,1},{2,34},{34,2},{3,35},{35,3},{4,36},{36... | collective-permute-start | bytes 2359304 | tf_op jit(solution)/shard_map/ppermute | solution.py:35
  170.5 10.4 %collective-permute-start.16 = (bf16[2,16,2560]{2,1,0:T(8,128)(2,1)S(1)}, bf16[2,16,2560]{2,1,0:T(8,128)(2,1)S(1)}, u32[]{:S(2)}, u32[]{:S(2)}) collective-permute-start(bf16[2,16,2560]{2,1,0:T(8,128)(2,1)S(1)} %get-tuple-element.52), channel_id=1, source_target_pairs={{0,8},{8,16},{16,24},{24,0},{1,9},{9,17},{17,25},{25,1},{2,10},{10... | collective-permute-start | bytes 491528 | tf_op jit(solution)/shard_map/ppermute | solution.py:27
  171.1 10.8 %collective-permute-start.17 = (bf16[2,16,2560]{2,1,0:T(8,128)(2,1)S(1)}, bf16[2,16,2560]{2,1,0:T(8,128)(2,1)S(1)}, u32[]{:S(2)}, u32[]{:S(2)}) collective-permute-start(bf16[2,16,2560]{2,1,0:T(8,128)(2,1)S(1)} %get-tuple-element.51), channel_id=1, source_target_pairs={{0,16},{8,24},{16,0},{24,8},{1,17},{9,25},{17,1},{25,9},{2,18},{10... | collective-permute-start | bytes 491528 | tf_op jit(solution)/shard_map/ppermute | solution.py:27
  174.1 7.8 %collective-permute-start.18 = (bf16[2,16,2560]{2,1,0:T(8,128)(2,1)S(1)}, bf16[2,16,2560]{2,1,0:T(8,128)(2,1)S(1)}, u32[]{:S(2)}, u32[]{:S(2)}) collective-permute-start(bf16[2,16,2560]{2,1,0:T(8,128)(2,1)S(1)} %get-tuple-element.50), channel_id=1, source_target_pairs={{0,24},{8,0},{16,8},{24,16},{1,25},{9,1},{17,9},{25,17},{2,26},{10... | collective-permute-start | bytes 491528 | tf_op jit(solution)/shard_map/ppermute | solution.py:27
  174.7 0.9 copy-start.8
  178.4 4.6 %copy-start.13 = (bf16[128,512]{1,0:T(8,128)(2,1)S(1)}, bf16[128,512]{1,0:T(8,128)(2,1)}, u32[]{:S(2)}) copy-start(bf16[128,512]{1,0:T(8,128)(2,1)} %get-tuple-element.42) | copy-start | bytes 393220
  178.4 5.3 %copy-start.12 = (bf16[128,512]{1,0:T(8,128)(2,1)S(1)}, bf16[128,512]{1,0:T(8,128)(2,1)}, u32[]{:S(2)}) copy-start(bf16[128,512]{1,0:T(8,128)(2,1)} %get-tuple-element.43) | copy-start | bytes 393220
  182.0 2.3 %collective-permute-start.20 = (f32[16,2560]{1,0:T(8,128)S(1)}, f32[16,2560]{1,0:T(8,128)S(1)}, u32[]{:S(2)}, u32[]{:S(2)}) collective-permute-start(f32[16,2560]{1,0:T(8,128)S(1)} %select_bitcast_fusion), channel_id=1, source_target_pairs={{0,32},{32,0},{1,33},{33,1},{2,34},{34,2},{3,35},{35,3},{4,36},{36... | collective-permute-start | bytes 491528 | tf_op jit(solution)/shard_map/ppermute | solution.py:35
Sparse Core Ops, SparseCore 0:
  25.0 66.6 all-gather.2
  103.5 65.0 reduce-scatter.1

commit v6 on v5

--- a/solution.py
+++ b/solution.py
@@ -12,6 +12,7 @@
 TOK = 128
 QB = 256
 COLS = 512
+SPLIT = 4
 PCOLS = 1280
 F32 = jnp.float32
 BF16 = jnp.bfloat16
@@ -52,20 +53,37 @@
 
 
 def weight_kernel(factor, info, *refs):
-    *parts, turned, term, rows = refs
-    here, y = info[0], info[1]
-    for place, (chip, rc) in enumerate((step, rc) for step in (0, 3, 1, 2) for rc in range(2)):
+    *parts, turned, z_first, y0, y1, y2, y3, rows, product = refs
+    here, y, z = info[0], info[1], info[2]
+    step = pl.program_id(0)
+    for place, (chip, rc) in enumerate((hop, rc) for hop in (0, 3, 1, 2) for rc in range(2)):
         spot = rc * 512 + lax.rem(here + chip, 4) * TOK
         rows[pl.ds(pl.multiple_of(spot, TOK), TOK), :] = parts[place][...]
-    for part in range(4):
-        product = jnp.dot(
-            turned[part * 256 : part * 256 + 256, :], rows[...], preferred_element_type=F32
-        )
-        product = (product * factor).astype(BF16)
-        for at in range(16):
-            f = part % 2 * 16 + at
-            ry = lax.rem(f // 8 - y + 4, 4)
-            term[f % 8, ry, part // 2] = product[at * 16 : at * 16 + 16, :]
+
+    def term(part):
+        block = turned[part * 256 : part * 256 + 256, :]
+        value = jnp.dot(block, rows[...], preferred_element_type=F32)
+        return (value * factor).astype(BF16)
+
+    @pl.when(step < SPLIT)
+    def _():
+        for part in range(4):
+            value = term(part)
+            for at in range(16):
+                f = part % 2 * 16 + at
+                ry = lax.rem(f // 8 - y + 4, 4)
+                z_first[f % 8, ry, part // 2] = value[at * 16 : at * 16 + 16, :]
+
+    @pl.when(step >= SPLIT)
+    def _():
+        for part in range(4):
+            product[part * 256 : part * 256 + 256, :] = term(part)
+        for r, out in enumerate((y0, y1, y2, y3)):
+            for at in range(8):
+                f = lax.rem(y + r, 4) * 8 + lax.rem(z + at, 8)
+                for kk in range(2):
+                    row = pl.multiple_of(kk * 512 + f * 16, 16)
+                    out[at, kk] = product[pl.ds(row, 16), :]
 
 
 def weight_product(info, parts, turned, factor):
@@ -75,14 +93,19 @@
         in_specs=[pl.BlockSpec((p.shape[0], COLS), lambda n, info: (0, n)) for p in parts]
         + [pl.BlockSpec((1024, 1024), lambda n, info: (0, 0))],
         out_specs=(
-            pl.BlockSpec((8, 4, 2, 16, COLS), lambda n, info: (0, 0, 0, 0, n)),
+            pl.BlockSpec(
+                (8, 4, 2, 16, COLS), lambda n, info: (0, 0, 0, 0, jnp.minimum(n, SPLIT - 1))
+            ),
+            *[pl.BlockSpec((8, 2, 16, COLS), lambda n, info: (0, 0, 0, 0)) for _ in range(4)],
             pl.BlockSpec((1024, COLS), lambda n, info: (0, n)),
         ),
+        scratch_shapes=[pltpu.VMEM((1024, COLS), BF16)],
     )
     return pl.pallas_call(
         functools.partial(weight_kernel, factor),
         out_shape=(
-            jax.ShapeDtypeStruct((8, 4, 2, 16, 2560), BF16),
+            jax.ShapeDtypeStruct((8, 4, 2, 16, SPLIT * COLS), BF16),
+            *[jax.ShapeDtypeStruct((8, 2, 16, COLS), BF16) for _ in range(4)],
             jax.ShapeDtypeStruct((1024, 2560), BF16),
         ),
         grid_spec=grid_spec,
@@ -93,15 +116,14 @@
     )(info, *parts, turned)
 
 
-def project_kernel(info, rows, block, out, weight, total):
-    y, core = info[1], info[3]
+def project_kernel(info, rows, block, out, total):
+    core = info[3]
     step = pl.program_id(0)
-    for r in range(4):
-        for z in range(8):
-            row = (lax.rem(y - r + 4, 4) * 8 + z) * 16
-            weight[pl.ds(pl.multiple_of(row, 16), 16), :] = block[z, r]
     product = lax.dot_general(
-        rows[...], weight[...], (((1,), (1,)), ((), ())), preferred_element_type=F32
+        rows[...],
+        block[...].reshape(512, PCOLS),
+        (((1,), (1,)), ((), ())),
+        preferred_element_type=F32,
     )
 
     @pl.when(step == 0)
@@ -128,10 +150,10 @@
         grid=(2560 // PCOLS,),
         in_specs=[
             pl.BlockSpec((1024, PCOLS), lambda n, info: (0, n)),
-            pl.BlockSpec((8, 4, None, 16, PCOLS), lambda n, info: (0, 0, rc, 0, n)),
+            pl.BlockSpec((32, None, 16, PCOLS), lambda n, info: (0, rc, 0, n)),
         ],
         out_specs=pl.BlockSpec((1024, 512), lambda n, info: (0, 0)),
-        scratch_shapes=[pltpu.VMEM((512, PCOLS), BF16), pltpu.VMEM((1024, 512), F32)],
+        scratch_shapes=[pltpu.VMEM((1024, 512), F32)],
     )
     return pl.pallas_call(
         project_kernel,
@@ -284,12 +306,11 @@
 
     weight_mine, weight_theirs = halves(out_weight)
     weight_pair = jnp.stack([weight_mine, swap(weight_theirs)])
-    near = jnp.stack([weight_pair] + [shift(weight_pair, "y", r) for r in (1, 2, 3)])
+    weight = lax.all_gather(weight_pair, ("y", "z"), axis=0, tiled=False)
 
     o_split = jnp.transpose(attn_out.reshape(TOK, 4, 1024), (1, 0, 2))
     grad_mine, grad_theirs = halves(out_grad[0])
     own = (grad_mine, swap(grad_theirs))
-    weight = lax.all_gather(after(near, o_split, grad_mine), "z", axis=0, tiled=False)
     o_own = lax.all_to_all(o_split, "x", split_axis=0, concat_axis=0, tiled=True)
     o_own = o_own.reshape(512, 1024)
 
@@ -311,26 +332,30 @@
     o_sib = swap(o_own)
     far0, far1 = shift(prev0, "x", 1), shift(succ1, "x", -1)
     parts = (*own, prev0, prev1, succ0, succ1, far0, far1)
-    term, rows = weight_product(info, parts, turn(o_own, o_sib), factor)
-
-    summed = lax.psum_scatter(term, "z", scatter_dimension=0, tiled=True)[0]
+    z_first, *y_first, rows = weight_product(info, parts, turn(o_own, o_sib), factor)
+
+    z_first = lax.psum_scatter(z_first, "z", scatter_dimension=0, tiled=True)[0]
+    y_first = [y_first[0]] + [shift(y_first[r], "y", r) for r in (1, 2, 3)]
 
     theirs = swap(project(info, rows, weight, 1, BF16))
     mine = project(info, rows, weight, 0, F32)
     grads = attention(info, packed, mine, theirs, o_own, o_sib)
-
-    back = [grads[0]] + [shift(grads[r], "x", r) for r in (1, 2, 3)]
+    *y_first, g0, g1, g2, g3 = lax.optimization_barrier((*y_first, *grads))
+
+    back = [g0, shift(g1, "x", 1), shift(g2, "x", 2), shift(g3, "x", 3)]
     grad_queries, grad_keys, grad_values = merge(
         info, back, swap(jnp.stack([part[1] for part in back]))
     )
 
-    summed = after(summed, *back[1:])
-    summed = [summed[0]] + [shift(summed[r], "y", r) for r in (1, 2, 3)]
+    y_first = add(*y_first).astype(BF16)
+    z_first, y_first = after(z_first, *back[1:]), after(y_first, *back[1:])
+    z_first = [z_first[0]] + [shift(z_first[r], "y", r) for r in (1, 2, 3)]
+    y_first = [y_first[0]] + [shift(y_first[r], "z", r) for r in range(1, 8)]
     grad_queries = grad_queries.reshape(1, TOK, 32, 128)
-    *summed, grad_queries, grad_keys, grad_values = lax.optimization_barrier(
-        (*summed, grad_queries, grad_keys, grad_values)
-    )
-    summed = add(*summed)
+    *z_first, grad_queries, grad_keys, grad_values = lax.optimization_barrier(
+        (*z_first, grad_queries, grad_keys, grad_values)
+    )
+    summed = jnp.concatenate([add(*z_first), add(*y_first)], axis=-1)
     keep = jnp.where(core == 0, summed[0], summed[1])
     give = jnp.where(core == 0, summed[1], summed[0])
     come = swap(give)

time: 193 us -> 204 us (1.057)
  starting transfers between devices: 34.3 us -> 49.4 us
  waiting for transfers between devices: 72.3 us -> 66.4 us
    ppermute x15 -> x22, starting transfers between devices: 17.2 us -> 31.8 us  [shift(): lax.ppermute(value, axis, [(i, (i + by) % size) for i in range(size)])]
    all_to_all x1, waiting for transfers between devices: 5.23 us -> 1.75 us  [per_device(): lax.all_to_all(packed, ('x', 'core'), split_axis=0, concat_axis=0, tiled=...]
    ppermute x15 -> x22, waiting for transfers between devices: 66.1 us -> 63.6 us  [shift(): lax.ppermute(value, axis, [(i, (i + by) % size) for i in range(size)])]
    unnamed x33 -> x37, local copies, waits for them, and re-layouts: 6.42 us -> 6.58 us
  transfers between devices with their start and end apart: 25 -> 32, of which waited for: 13 -> 10; matrix products, arithmetic and copies ran while one was open for 7% -> 7% of each run, Pallas kernels for 26% -> 25%
where the time goes in v6:
time: 204 us; the launch traced here: 203 us
  waiting for transfers between devices  66.4 us (33%)
  Pallas kernels  51 us (25%)
  starting transfers between devices  49.4 us (24%)
  between operations  15.8 us (8%)
  local copies, waits for them, and re-layouts  15.1 us (7%)
  other arithmetic  5.55 us (3%)
    ppermute x22, waiting for transfers between devices, shift(): lax.ppermute(value, axis, [(i, (i + by) % size) for i in range(size)])  63.6 us
    ppermute x22, starting transfers between devices, shift(): lax.ppermute(value, axis, [(i, (i + by) % size) for i in range(size)])  31.8 us
    pallas_call x1, Pallas kernels, attention(): pl.pallas_call(attention_kernel, out_shape=[jax.ShapeDtypeStruct((2, TOK,...  16.9 us
    pallas_call x2, Pallas kernels, project(): pl.pallas_call(project_kernel, out_shape=jax.ShapeDtypeStruct((1024, 512)...  14.9 us
    pallas_call x1, Pallas kernels, weight_product(): pl.pallas_call(functools.partial(weight_kernel, factor), out_shape=(jax.S...  12.9 us
    ppermute x6, starting transfers between devices, swap(): return lax.ppermute(value, 'core', [(0, 1), (1, 0)])  9.21 us
    unnamed x37, local copies, waits for them, and re-layouts  6.58 us
    all_to_all x1, starting transfers between devices, per_device(): lax.all_to_all(packed, ('x', 'core'), split_axis=0, concat_axis=0, tiled=...  4.67 us
  transfers between devices with their start and end apart: 32, of which 10 were waited for; matrix products, arithmetic and copies ran while one was open for 7% of the time, Pallas kernels for 25%

profile of v6, /device:TPU:1, one launch (start us, length us, event | category | flops | bytes accessed | tf_op | source)
XLA Modules:
  0.0 203.2 jit_solution(16025841413093814560)
XLA Ops:
  8.1 1.0 select_bitcast_fusion.1
  9.1 3.3 %collective-permute-start.11 = (bf16[16,2560]{1,0:T(8,128)(2,1)S(1)}, bf16[16,2560]{1,0:T(8,128)(2,1)S(1)}, u32[]{:S(2)}, u32[]{:S(2)}) collective-permute-start(bf16[16,2560]{1,0:T(8,128)(2,1)S(1)} %get-tuple-element.88), channel_id=1, source_target_pairs={{0,32},{32,0},{1,33},{33,1},{2,34},{34,2},{3,35},{35,3},{4,36},{36... | collective-permute-start | bytes 245768 | tf_op jit(solution)/shard_map/ppermute | solution.py:36
  12.4 0.9 collective-permute-done.11
  14.0 1.4 broadcast_select_fusion
  16.2 1.3 copy.21
  17.4 3.6 %all-to-all-start = ((bf16[4,128,1024]{2,1,0:T(8,128)(2,1)}), bf16[4,128,1024]{2,1,0:T(8,128)(2,1)S(1)}, u32[]{:S(2)}, u32[]{:S(2)}) async-start(bf16[4,128,1024]{2,1,0:T(8,128)(2,1)} %bitcast.58), calls=%async_computation | async-start | bytes 2097152 | tf_op jit(solution)/shard_map/all_to_all | solution.py:314
  21.1 1.4 collective-permute-start.1
  22.5 1.4 collective-permute-start.2
  24.6 1.7 reshape.41
  27.3 1.3 maximum_bitcast_fusion
  28.6 21.4 %collective-permute-done.1.refs_2_ = bf16[128,2560]{1,0:T(8,128)(2,1)} collective-permute-done((bf16[128,2560]{1,0:T(8,128)(2,1)S(1)}, bf16[128,2560]{1,0:T(8,128)(2,1)}, u32[]{:S(2)}, u32[]{:S(2)}) %collective-permute-start.1) | collective-permute-done | bytes 655392 | tf_op jit(solution)/shard_map/ppermute | solution.py:28
  50.0 1.1 collective-permute-start.7
  51.7 0.8 collective-permute-start.3
  52.6 2.6 %collective-permute-start.6 = (bf16[128,2560]{1,0:T(8,128)(2,1)S(1)}, bf16[128,2560]{1,0:T(8,128)(2,1)}, u32[]{:S(2)}, u32[]{:S(2)}) collective-permute-start(bf16[128,2560]{1,0:T(8,128)(2,1)S(1)} %collective-permute-done.2.refs_5_), channel_id=1, source_target_pairs={{0,192},{64,0},{128,64},{192,128},{1,193},{65,1},{129,65},{193,129... | collective-permute-start | bytes 1966088 | tf_op jit(solution)/shard_map/ppermute | solution.py:28
  55.9 1.0 copy-done.4
  56.9 3.5 %shard_map.102.refs_8_ = bf16[1024,1024]{1,0:T(8,128)(2,1)} custom-call(bf16[512,1024]{1,0:T(8,128)(2,1)} %bitcast.62, bf16[512,1024]{1,0:T(8,128)(2,1)} %copy-done.4), custom_call_target="tpu_custom_call" | custom-call | tf_op jit(solution)/shard_map/pallas_call | solution.py:46
  60.4 7.1 %collective-permute-done.4.refs_4_ = bf16[128,2560]{1,0:T(8,128)(2,1)} collective-permute-done((bf16[128,2560]{1,0:T(8,128)(2,1)S(1)}, bf16[128,2560]{1,0:T(8,128)(2,1)}, u32[]{:S(2)}, u32[]{:S(2)}) %collective-permute-start.4) | collective-permute-done | bytes 655392 | tf_op jit(solution)/shard_map/ppermute | solution.py:28
  67.5 1.7 collective-permute-done.3.refs_3_
  69.2 14.0 %collective-permute-done.5.refs_6_ = bf16[128,2560]{1,0:T(8,128)(2,1)} collective-permute-done((bf16[128,2560]{1,0:T(8,128)(2,1)}, bf16[128,2560]{1,0:T(8,128)(2,1)}, u32[]{:S(2)}, u32[]{:S(2)}) %collective-permute-start.5) | collective-permute-done | bytes 655392 | tf_op jit(solution)/shard_map/ppermute | solution.py:28
  83.3 12.9 %shard_map.103 = (bf16[8,4,2,16,2048]{4,3,2,1,0:T(8,128)(2,1)}, bf16[8,2,16,512]{3,2,1,0:T(8,128)(2,1)}, bf16[8,2,16,512]{3,2,1,0:T(8,128)(2,1)}, bf16[8,2,16,51...) custom-call(s32[7]{0:T(128)} %concatenate.12.info, bf16[128,2560]{1,0:T(8,128)(2,1)} %copy-done.1, ...), custom_call_target="tpu_custom_call" | custom-call | flops 1048576 | bytes 1048576 | tf_op jit(solution)/shard_map/pallas_call | solution.py:104
  96.2 4.7 %all-to-all-start.1 = ((bf16[8,128,768]{2,1,0:T(8,128)(2,1)}), bf16[8,128,768]{2,1,0:T(8,128)(2,1)S(1)}, u32[]{:S(2)}, u32[]{:S(2)}) async-start(bf16[8,128,768]{2,1,0:T(8,128)(2,1)} %maximum_bitcast_fusion), calls=%async_computation.2 | async-start | bytes 3145728 | tf_op jit(solution)/shard_map/all_to_all | solution.py:330
  100.9 7.3 %shard_map.105 = bf16[1024,512]{1,0:T(8,128)(2,1)} custom-call(s32[7]{0:T(128)} %concatenate.12.info, bf16[1024,2560]{1,0:T(8,128)(2,1)} %get-tuple-element.47.rows, bf16[32,2,16,2560]{3,2,1,0:T(8,128)(2,1)} %bitcast.59), custom_call_target="tpu_custom_call" | custom-call | flops 1048576 | bytes 1048576 | tf_op jit(solution)/shard_map/pallas_call | solution.py:158
  108.5 2.6 %collective-permute-start.9 = (bf16[8,2,16,512]{3,2,1,0:T(8,128)(2,1)}, bf16[8,2,16,512]{3,2,1,0:T(8,128)(2,1)S(1)}, u32[]{:S(2)}, u32[]{:S(2)}) collective-permute-start(bf16[8,2,16,512]{3,2,1,0:T(8,128)(2,1)} %get-tuple-element.44), channel_id=1, source_target_pairs={{0,16},{8,24},{16,0},{24,8},{1,17},{9,25},{17,1},{25,9},{2,18},{10... | collective-permute-start | bytes 786440 | tf_op jit(solution)/shard_map/ppermute | solution.py:28
  111.1 1.0 collective-permute-start.10
  112.2 7.7 %shard_map.104.mine = f32[1024,512]{1,0:T(8,128)} custom-call(s32[7]{0:T(128)} %concatenate.12.info, bf16[1024,2560]{1,0:T(8,128)(2,1)} %get-tuple-element.47.rows, bf16[32,2,16,2560]{3,2,1,0:T(8,128)(2,1)} %bitcast.60), custom_call_target="tpu_custom_call" | custom-call | flops 1048576 | bytes 1048576 | tf_op jit(solution)/shard_map/pallas_call | solution.py:158
  119.8 1.8 all-to-all-done.1
  121.6 1.2 copy-done.2
  123.2 16.9 %shard_map.106 = (bf16[2,128,768]{2,1,0:T(8,128)(2,1)}, bf16[2,128,768]{2,1,0:T(8,128)(2,1)}, bf16[2,128,768]{2,1,0:T(8,128)(2,1)}, bf16[2,128,768]{2,1,0:T(8,128)(2,1)}) custom-call(s32[7]{0:T(128)} %concatenate.12.info, bf16[1024,768]{1,0:T(8,128)(2,1)} %bitcast.64, bf16[1024,768]{1,0:T(8,128)(2,1)} %bitcast.65, bf16[1024,768]{1,0:T(8,128)(2,1)} %bitcast.66, ...), custom_call_target="tpu_custom_call" | custom-call | flops 14000000000 | bytes 8388608 | tf_op jit(solution)/shard_map/pallas_call | solution.py:246
  140.1 1.0 collective-permute-start.15
  141.1 1.2 collective-permute-start.14
  142.3 0.9 slice.76
  143.5 6.8 %collective-permute-done.15.refs_3_ = bf16[2,128,768]{2,1,0:T(8,128)(2,1)S(1)} collective-permute-done((bf16[2,128,768]{2,1,0:T(8,128)(2,1)}, bf16[2,128,768]{2,1,0:T(8,128)(2,1)S(1)}, u32[]{:S(2)}, u32[]{:S(2)}) %collective-permute-start.15) | collective-permute-done | bytes 393248 | tf_op jit(solution)/shard_map/ppermute | solution.py:28
  150.3 1.9 collective-permute-done.14.refs_2_
  152.2 10.1 %collective-permute-done.13.refs_1_ = bf16[2,128,768]{2,1,0:T(8,128)(2,1)S(1)} collective-permute-done((bf16[2,128,768]{2,1,0:T(8,128)(2,1)}, bf16[2,128,768]{2,1,0:T(8,128)(2,1)S(1)}, u32[]{:S(2)}, u32[]{:S(2)}) %collective-permute-start.13) | collective-permute-done | bytes 393248 | tf_op jit(solution)/shard_map/ppermute | solution.py:28
  163.0 5.9 %collective-permute-start.26 = (bf16[2,16,512]{2,1,0:T(8,128)(2,1)S(1)}, bf16[2,16,512]{2,1,0:T(8,128)(2,1)S(1)}, u32[]{:S(2)}, u32[]{:S(2)}) collective-permute-start(bf16[2,16,512]{2,1,0:T(8,128)(2,1)S(1)} %get-tuple-element.81), channel_id=1, source_target_pairs={{0,7},{1,0},{2,1},{3,2},{4,3},{5,4},{6,5},{7,6},{8,15},{9,8},{10,9... | collective-permute-start | bytes 98312 | tf_op jit(solution)/shard_map/ppermute | solution.py:28
  168.9 1.2 collective-permute-start.25
  170.6 4.4 %collective-permute-start.23 = (bf16[2,16,512]{2,1,0:T(8,128)(2,1)S(1)}, bf16[2,16,512]{2,1,0:T(8,128)(2,1)S(1)}, u32[]{:S(2)}, u32[]{:S(2)}) collective-permute-start(bf16[2,16,512]{2,1,0:T(8,128)(2,1)S(1)} %get-tuple-element.84), channel_id=1, source_target_pairs={{0,4},{1,5},{2,6},{3,7},{4,0},{5,1},{6,2},{7,3},{8,12},{9,13},{10,... | collective-permute-start | bytes 98312 | tf_op jit(solution)/shard_map/ppermute | solution.py:28
  175.0 2.2 %collective-permute-start.21 = (bf16[2,16,512]{2,1,0:T(8,128)(2,1)S(1)}, bf16[2,16,512]{2,1,0:T(8,128)(2,1)S(1)}, u32[]{:S(2)}, u32[]{:S(2)}) collective-permute-start(bf16[2,16,512]{2,1,0:T(8,128)(2,1)S(1)} %get-tuple-element.86), channel_id=1, source_target_pairs={{0,2},{1,3},{2,4},{3,5},{4,6},{5,7},{6,0},{7,1},{8,10},{9,11},{10,... | collective-permute-start | bytes 98312 | tf_op jit(solution)/shard_map/ppermute | solution.py:28
  177.2 1.4 collective-permute-start.20
  178.6 1.1 slice_bitcast_fusion
  180.8 1.6 collective-permute-start.17
  182.4 1.3 collective-permute-start.18
  183.8 0.9 copy-done.8
  184.7 2.8 %shard_map.107 = (bf16[128,4096]{1,0:T(8,128)(2,1)}, bf16[128,512]{1,0:T(8,128)(2,1)}, bf16[128,512]{1,0:T(8,128)(2,1)}) custom-call(s32[7]{0:T(128)} %concatenate.12.info, bf16[2,128,768]{2,1,0:T(8,128)(2,1)} %get-tuple-element.56.refs_0_, bf16[2,128,768]{2,1,0:T(8,128)(2,1)} %copy-done.7, bf16[2,128,768]{2,1,0:T(8,128)(2,1)} %copy-done.6, ...), custom_call_target="tpu_custom_call" | custom-call | tf_op jit(solution)/shard_map/pallas_call | solution.py:277
  187.5 2.5 %copy.19 = bf16[16,8,32,128]{3,2,1,0:T(8,128)(2,1)} copy(bf16[16,8,32,128]{3,1,2,0:T(8,128)(2,1)} %bitcast.71) | data formatting | bytes 2097152
  190.0 3.5 %collective-permute-start.27 = (f32[16,2560]{1,0:T(8,128)S(1)}, f32[16,2560]{1,0:T(8,128)S(1)}, u32[]{:S(2)}, u32[]{:S(2)}) collective-permute-start(f32[16,2560]{1,0:T(8,128)S(1)} %select_bitcast_fusion), channel_id=1, source_target_pairs={{0,32},{32,0},{1,33},{33,1},{2,34},{34,2},{3,35},{35,3},{4,36},{36... | collective-permute-start | bytes 491528 | tf_op jit(solution)/shard_map/ppermute | solution.py:36
  193.5 0.7 reshape.48
  195.0 0.7 pad_maximum_fusion.1
  (89 shorter events, 8.6 us)
Async XLA Ops:
  8.0 7.9 %copy-start.3 = (bf16[1,128,32,128]{3,2,1,0:T(8,128)(2,1)S(1)}, bf16[1,128,32,128]{3,2,1,0:T(8,128)(2,1)}, u32[]{:S(2)}) copy-start(bf16[1,128,32,128]{3,2,1,0:T(8,128)(2,1)} %param.10) | copy-start | bytes 3145732
  8.0 92.8 %all-gather.3.cloned.1.call-start = ((), (), s32[]{:S(2)}) async-start(), calls=%async_computation.4 | async-start | bytes 5406720 | tf_op jit(solution)/shard_map/all_gather | solution.py:309
  9.1 4.3 %collective-permute-start.11 = (bf16[16,2560]{1,0:T(8,128)(2,1)S(1)}, bf16[16,2560]{1,0:T(8,128)(2,1)S(1)}, u32[]{:S(2)}, u32[]{:S(2)}) collective-permute-start(bf16[16,2560]{1,0:T(8,128)(2,1)S(1)} %get-tuple-element.88), channel_id=1, source_target_pairs={{0,32},{32,0},{1,33},{33,1},{2,34},{34,2},{3,35},{35,3},{4,36},{36... | collective-permute-start | bytes 245768 | tf_op jit(solution)/shard_map/ppermute | solution.py:36
  15.4 35.7 %copy-start.1 = (bf16[128,2560]{1,0:T(8,128)(2,1)}, bf16[128,2560]{1,0:T(8,128)(2,1)S(1)}, u32[]{:S(2)}) copy-start(bf16[128,2560]{1,0:T(8,128)(2,1)S(1)} %get-tuple-element.73.refs_0_) | copy-start | bytes 1966084
  15.4 7.1 %collective-permute-start = (bf16[128,2560]{1,0:T(8,128)(2,1)S(1)}, bf16[128,2560]{1,0:T(8,128)(2,1)}, u32[]{:S(2)}, u32[]{:S(2)}) collective-permute-start(bf16[128,2560]{1,0:T(8,128)(2,1)S(1)} %get-tuple-element.72), channel_id=1, source_target_pairs={{0,32},{32,0},{1,33},{33,1},{2,34},{34,2},{3,35},{35,3},{4,36},{36... | collective-permute-start | bytes 1966088 | tf_op jit(solution)/shard_map/ppermute | solution.py:36
  16.1 7.8 %copy-start.12 = (bf16[1,128,4,128]{3,2,1,0:T(4,128)(2,1)S(1)}, bf16[1,128,4,128]{3,2,1,0:T(4,128)(2,1)}, u32[]{:S(2)}) copy-start(bf16[1,128,4,128]{3,2,1,0:T(4,128)(2,1)} %param.9) | copy-start | bytes 393220
  17.4 7.1 %copy-start.13 = (bf16[1,128,4,128]{3,2,1,0:T(4,128)(2,1)S(1)}, bf16[1,128,4,128]{3,2,1,0:T(4,128)(2,1)}, u32[]{:S(2)}) copy-start(bf16[1,128,4,128]{3,2,1,0:T(4,128)(2,1)} %param.8) | copy-start | bytes 393220
  17.4 32.6 %all-to-all-start = ((bf16[4,128,1024]{2,1,0:T(8,128)(2,1)}), bf16[4,128,1024]{2,1,0:T(8,128)(2,1)S(1)}, u32[]{:S(2)}, u32[]{:S(2)}) async-start(bf16[4,128,1024]{2,1,0:T(8,128)(2,1)} %bitcast.58), calls=%async_computation | async-start | bytes 2097152 | tf_op jit(solution)/shard_map/all_to_all | solution.py:314
  21.1 149.5 %reduce-scatter.2.cloned.1.call-start = ((), (), s32[]{:S(2)}) async-start(), calls=%async_computation.3 | async-start | bytes 4718592 | tf_op jit(solution)/shard_map/reduce_scatter | solution.py:337
  21.1 28.9 %collective-permute-start.1 = (bf16[128,2560]{1,0:T(8,128)(2,1)S(1)}, bf16[128,2560]{1,0:T(8,128)(2,1)}, u32[]{:S(2)}, u32[]{:S(2)}) collective-permute-start(bf16[128,2560]{1,0:T(8,128)(2,1)S(1)} %get-tuple-element.73.refs_0_), channel_id=1, source_target_pairs={{0,64},{64,128},{128,192},{192,0},{1,65},{65,129},{129,193},{193,1... | collective-permute-start | bytes 1966088 | tf_op jit(solution)/shard_map/ppermute | solution.py:28
  22.5 27.5 %collective-permute-start.2 = (bf16[128,2560]{1,0:T(8,128)(2,1)}, bf16[128,2560]{1,0:T(8,128)(2,1)S(1)}, u32[]{:S(2)}, u32[]{:S(2)}) collective-permute-start(bf16[128,2560]{1,0:T(8,128)(2,1)} %collective-permute-done.refs_1_), channel_id=1, source_target_pairs={{0,192},{64,0},{128,64},{192,128},{1,193},{65,1},{129,65},{193,129... | collective-permute-start | bytes 1966088 | tf_op jit(solution)/shard_map/ppermute | solution.py:28
  27.2 28.0 %copy-start.16 = (s32[1,3]{1,0:T(1,128)S(1)}, s32[1,3]{1,0:T(1,128)}, u32[]{:S(2)}) copy-start(s32[1,3]{1,0:T(1,128)} %param.13) | copy-start | bytes 40
  50.0 5.9 %copy-start = (bf16[4,128,1024]{2,1,0:T(8,128)(2,1)}, bf16[4,128,1024]{2,1,0:T(8,128)(2,1)S(1)}, u32[]{:S(2)}) copy-start(bf16[4,128,1024]{2,1,0:T(8,128)(2,1)S(1)} %all-to-all-done) | copy-start | bytes 3145732
  50.0 33.2 %copy-start.9 = (bf16[128,2560]{1,0:T(8,128)(2,1)}, bf16[128,2560]{1,0:T(8,128)(2,1)S(1)}, u32[]{:S(2)}) copy-start(bf16[128,2560]{1,0:T(8,128)(2,1)S(1)} %collective-permute-done.2.refs_5_) | copy-start | bytes 1966084
  50.0 5.8 %collective-permute-start.7 = (bf16[512,1024]{1,0:T(8,128)(2,1)S(1)}, bf16[512,1024]{1,0:T(8,128)(2,1)S(1)}, u32[]{:S(2)}, u32[]{:S(2)}) collective-permute-start(bf16[512,1024]{1,0:T(8,128)(2,1)S(1)} %bitcast.61), channel_id=1, source_target_pairs={{0,32},{32,0},{1,33},{33,1},{2,34},{34,2},{3,35},{35,3},{4,36},{36... | collective-permute-start | bytes 3145736 | tf_op jit(solution)/shard_map/ppermute | solution.py:36
  51.1 16.4 %collective-permute-start.4 = (bf16[128,2560]{1,0:T(8,128)(2,1)S(1)}, bf16[128,2560]{1,0:T(8,128)(2,1)}, u32[]{:S(2)}, u32[]{:S(2)}) collective-permute-start(bf16[128,2560]{1,0:T(8,128)(2,1)S(1)} %get-tuple-element.73.refs_0_), channel_id=1, source_target_pairs={{0,192},{64,0},{128,64},{192,128},{1,193},{65,1},{129,65},{193,129... | collective-permute-start | bytes 1966088 | tf_op jit(solution)/shard_map/ppermute | solution.py:28
  51.7 17.5 %collective-permute-start.3 = (bf16[128,2560]{1,0:T(8,128)(2,1)}, bf16[128,2560]{1,0:T(8,128)(2,1)}, u32[]{:S(2)}, u32[]{:S(2)}) collective-permute-start(bf16[128,2560]{1,0:T(8,128)(2,1)} %collective-permute-done.refs_1_), channel_id=1, source_target_pairs={{0,64},{64,128},{128,192},{192,0},{1,65},{65,129},{129,193},{193,1... | collective-permute-start | bytes 1966088 | tf_op jit(solution)/shard_map/ppermute | solution.py:28
  52.6 30.7 %collective-permute-start.5 = (bf16[128,2560]{1,0:T(8,128)(2,1)}, bf16[128,2560]{1,0:T(8,128)(2,1)}, u32[]{:S(2)}, u32[]{:S(2)}) collective-permute-start(bf16[128,2560]{1,0:T(8,128)(2,1)} %collective-permute-done.1.refs_2_), channel_id=1, source_target_pairs={{0,64},{64,128},{128,192},{192,0},{1,65},{65,129},{129,193},{193,1... | collective-permute-start | bytes 1966088 | tf_op jit(solution)/shard_map/ppermute | solution.py:28
  52.6 30.7 %collective-permute-start.6 = (bf16[128,2560]{1,0:T(8,128)(2,1)S(1)}, bf16[128,2560]{1,0:T(8,128)(2,1)}, u32[]{:S(2)}, u32[]{:S(2)}) collective-permute-start(bf16[128,2560]{1,0:T(8,128)(2,1)S(1)} %collective-permute-done.2.refs_5_), channel_id=1, source_target_pairs={{0,192},{64,0},{128,64},{192,128},{1,193},{65,1},{129,65},{193,129... | collective-permute-start | bytes 1966088 | tf_op jit(solution)/shard_map/ppermute | solution.py:28
  55.9 1.0 copy-start.4
  96.2 25.4 %all-to-all-start.1 = ((bf16[8,128,768]{2,1,0:T(8,128)(2,1)}), bf16[8,128,768]{2,1,0:T(8,128)(2,1)S(1)}, u32[]{:S(2)}, u32[]{:S(2)}) async-start(bf16[8,128,768]{2,1,0:T(8,128)(2,1)} %maximum_bitcast_fusion), calls=%async_computation.2 | async-start | bytes 3145728 | tf_op jit(solution)/shard_map/all_to_all | solution.py:330
  108.1 13.5 %collective-permute-start.12 = (bf16[1024,512]{1,0:T(8,128)(2,1)}, bf16[1024,512]{1,0:T(8,128)(2,1)S(1)}, u32[]{:S(2)}, u32[]{:S(2)}) collective-permute-start(bf16[1024,512]{1,0:T(8,128)(2,1)} %shard_map.105), channel_id=1, source_target_pairs={{0,32},{32,0},{1,33},{33,1},{2,34},{34,2},{3,35},{35,3},{4,36},{36... | collective-permute-start | bytes 3145736 | tf_op jit(solution)/shard_map/ppermute | solution.py:36
  108.4 31.6 %collective-permute-start.8 = (bf16[8,2,16,512]{3,2,1,0:T(8,128)(2,1)}, bf16[8,2,16,512]{3,2,1,0:T(8,128)(2,1)S(1)}, u32[]{:S(2)}, u32[]{:S(2)}) collective-permute-start(bf16[8,2,16,512]{3,2,1,0:T(8,128)(2,1)} %get-tuple-element.43), channel_id=1, source_target_pairs={{0,8},{8,16},{16,24},{24,0},{1,9},{9,17},{17,25},{25,1},{2,10},{10... | collective-permute-start | bytes 786440 | tf_op jit(solution)/shard_map/ppermute | solution.py:28
  108.5 31.6 %collective-permute-start.9 = (bf16[8,2,16,512]{3,2,1,0:T(8,128)(2,1)}, bf16[8,2,16,512]{3,2,1,0:T(8,128)(2,1)S(1)}, u32[]{:S(2)}, u32[]{:S(2)}) collective-permute-start(bf16[8,2,16,512]{3,2,1,0:T(8,128)(2,1)} %get-tuple-element.44), channel_id=1, source_target_pairs={{0,16},{8,24},{16,0},{24,8},{1,17},{9,25},{17,1},{25,9},{2,18},{10... | collective-permute-start | bytes 786440 | tf_op jit(solution)/shard_map/ppermute | solution.py:28
  111.1 28.9 %collective-permute-start.10 = (bf16[8,2,16,512]{3,2,1,0:T(8,128)(2,1)}, bf16[8,2,16,512]{3,2,1,0:T(8,128)(2,1)S(1)}, u32[]{:S(2)}, u32[]{:S(2)}) collective-permute-start(bf16[8,2,16,512]{3,2,1,0:T(8,128)(2,1)} %get-tuple-element.45), channel_id=1, source_target_pairs={{0,24},{8,0},{16,8},{24,16},{1,25},{9,1},{17,9},{25,17},{2,26},{10... | collective-permute-start | bytes 786440 | tf_op jit(solution)/shard_map/ppermute | solution.py:28
  121.6 1.2 copy-start.2
  121.6 1.6 copy-start.17
  123.2 20.1 %copy-start.11 = (bf16[8,2,16,512]{3,2,1,0:T(8,128)(2,1)S(1)}, bf16[8,2,16,512]{3,2,1,0:T(8,128)(2,1)}, u32[]{:S(2)}) copy-start(bf16[8,2,16,512]{3,2,1,0:T(8,128)(2,1)} %get-tuple-element.67) | copy-start | bytes 786436
  140.1 10.1 %collective-permute-start.15 = (bf16[2,128,768]{2,1,0:T(8,128)(2,1)}, bf16[2,128,768]{2,1,0:T(8,128)(2,1)S(1)}, u32[]{:S(2)}, u32[]{:S(2)}) collective-permute-start(bf16[2,128,768]{2,1,0:T(8,128)(2,1)} %get-tuple-element.54), channel_id=1, source_target_pairs={{0,192},{64,0},{128,64},{192,128},{1,193},{65,1},{129,65},{193,129... | collective-permute-start | bytes 1179656 | tf_op jit(solution)/shard_map/ppermute | solution.py:28
  141.1 11.1 %collective-permute-start.14 = (bf16[2,128,768]{2,1,0:T(8,128)(2,1)}, bf16[2,128,768]{2,1,0:T(8,128)(2,1)S(1)}, u32[]{:S(2)}, u32[]{:S(2)}) collective-permute-start(bf16[2,128,768]{2,1,0:T(8,128)(2,1)} %get-tuple-element.53), channel_id=1, source_target_pairs={{0,128},{64,192},{128,0},{192,64},{1,129},{65,193},{129,1},{193,65... | collective-permute-start | bytes 1179656 | tf_op jit(solution)/shard_map/ppermute | solution.py:28
  142.3 19.9 %collective-permute-start.13 = (bf16[2,128,768]{2,1,0:T(8,128)(2,1)}, bf16[2,128,768]{2,1,0:T(8,128)(2,1)S(1)}, u32[]{:S(2)}, u32[]{:S(2)}) collective-permute-start(bf16[2,128,768]{2,1,0:T(8,128)(2,1)} %get-tuple-element.52), channel_id=1, source_target_pairs={{0,64},{64,128},{128,192},{192,0},{1,65},{65,129},{129,193},{193,1... | collective-permute-start | bytes 1179656 | tf_op jit(solution)/shard_map/ppermute | solution.py:28
  150.2 29.5 %copy-start.5 = (bf16[2,128,768]{2,1,0:T(8,128)(2,1)}, bf16[2,128,768]{2,1,0:T(8,128)(2,1)S(1)}, u32[]{:S(2)}) copy-start(bf16[2,128,768]{2,1,0:T(8,128)(2,1)S(1)} %collective-permute-done.15.refs_3_) | copy-start | bytes 1179652
  152.2 31.6 %copy-start.6 = (bf16[2,128,768]{2,1,0:T(8,128)(2,1)}, bf16[2,128,768]{2,1,0:T(8,128)(2,1)S(1)}, u32[]{:S(2)}) copy-start(bf16[2,128,768]{2,1,0:T(8,128)(2,1)S(1)} %collective-permute-done.14.refs_2_) | copy-start | bytes 1179652
  162.3 21.5 %copy-start.7 = (bf16[2,128,768]{2,1,0:T(8,128)(2,1)}, bf16[2,128,768]{2,1,0:T(8,128)(2,1)S(1)}, u32[]{:S(2)}) copy-start(bf16[2,128,768]{2,1,0:T(8,128)(2,1)S(1)} %collective-permute-done.13.refs_1_) | copy-start | bytes 1179652
  162.4 21.4 %collective-permute-start.19 = (bf16[4,128,768]{2,1,0:T(8,128)(2,1)S(1)}, bf16[4,128,768]{2,1,0:T(8,128)(2,1)S(1)}, u32[]{:S(2)}, u32[]{:S(2)}) collective-permute-start(bf16[4,128,768]{2,1,0:T(8,128)(2,1)S(1)} %pad_maximum_fusion), channel_id=1, source_target_pairs={{0,32},{32,0},{1,33},{33,1},{2,34},{34,2},{3,35},{35,3},{4,36},{36... | collective-permute-start | bytes 2359304 | tf_op jit(solution)/shard_map/ppermute | solution.py:36
  163.0 12.0 %collective-permute-start.26 = (bf16[2,16,512]{2,1,0:T(8,128)(2,1)S(1)}, bf16[2,16,512]{2,1,0:T(8,128)(2,1)S(1)}, u32[]{:S(2)}, u32[]{:S(2)}) collective-permute-start(bf16[2,16,512]{2,1,0:T(8,128)(2,1)S(1)} %get-tuple-element.81), channel_id=1, source_target_pairs={{0,7},{1,0},{2,1},{3,2},{4,3},{5,4},{6,5},{7,6},{8,15},{9,8},{10,9... | collective-permute-start | bytes 98312 | tf_op jit(solution)/shard_map/ppermute | solution.py:28
  168.9 6.1 %collective-permute-start.25 = (bf16[2,16,512]{2,1,0:T(8,128)(2,1)S(1)}, bf16[2,16,512]{2,1,0:T(8,128)(2,1)S(1)}, u32[]{:S(2)}, u32[]{:S(2)}) collective-permute-start(bf16[2,16,512]{2,1,0:T(8,128)(2,1)S(1)} %get-tuple-element.82), channel_id=1, source_target_pairs={{0,6},{1,7},{2,0},{3,1},{4,2},{5,3},{6,4},{7,5},{8,14},{9,15},{10,... | collective-permute-start | bytes 98312 | tf_op jit(solution)/shard_map/ppermute | solution.py:28
  170.1 7.1 %collective-permute-start.24 = (bf16[2,16,512]{2,1,0:T(8,128)(2,1)S(1)}, bf16[2,16,512]{2,1,0:T(8,128)(2,1)S(1)}, u32[]{:S(2)}, u32[]{:S(2)}) collective-permute-start(bf16[2,16,512]{2,1,0:T(8,128)(2,1)S(1)} %get-tuple-element.83), channel_id=1, source_target_pairs={{0,5},{1,6},{2,7},{3,0},{4,1},{5,2},{6,3},{7,4},{8,13},{9,14},{10,... | collective-permute-start | bytes 98312 | tf_op jit(solution)/shard_map/ppermute | solution.py:28
  170.6 9.2 %collective-permute-start.23 = (bf16[2,16,512]{2,1,0:T(8,128)(2,1)S(1)}, bf16[2,16,512]{2,1,0:T(8,128)(2,1)S(1)}, u32[]{:S(2)}, u32[]{:S(2)}) collective-permute-start(bf16[2,16,512]{2,1,0:T(8,128)(2,1)S(1)} %get-tuple-element.84), channel_id=1, source_target_pairs={{0,4},{1,5},{2,6},{3,7},{4,0},{5,1},{6,2},{7,3},{8,12},{9,13},{10,... | collective-permute-start | bytes 98312 | tf_op jit(solution)/shard_map/ppermute | solution.py:28
  175.0 5.8 %collective-permute-start.22 = (bf16[2,16,512]{2,1,0:T(8,128)(2,1)S(1)}, bf16[2,16,512]{2,1,0:T(8,128)(2,1)S(1)}, u32[]{:S(2)}, u32[]{:S(2)}) collective-permute-start(bf16[2,16,512]{2,1,0:T(8,128)(2,1)S(1)} %get-tuple-element.85), channel_id=1, source_target_pairs={{0,3},{1,4},{2,5},{3,6},{4,7},{5,0},{6,1},{7,2},{8,11},{9,12},{10,... | collective-permute-start | bytes 98312 | tf_op jit(solution)/shard_map/ppermute | solution.py:28
  175.0 7.4 %collective-permute-start.21 = (bf16[2,16,512]{2,1,0:T(8,128)(2,1)S(1)}, bf16[2,16,512]{2,1,0:T(8,128)(2,1)S(1)}, u32[]{:S(2)}, u32[]{:S(2)}) collective-permute-start(bf16[2,16,512]{2,1,0:T(8,128)(2,1)S(1)} %get-tuple-element.86), channel_id=1, source_target_pairs={{0,2},{1,3},{2,4},{3,5},{4,6},{5,7},{6,0},{7,1},{8,10},{9,11},{10,... | collective-permute-start | bytes 98312 | tf_op jit(solution)/shard_map/ppermute | solution.py:28
  177.2 6.5 %collective-permute-start.20 = (bf16[2,16,512]{2,1,0:T(8,128)(2,1)S(1)}, bf16[2,16,512]{2,1,0:T(8,128)(2,1)S(1)}, u32[]{:S(2)}, u32[]{:S(2)}) collective-permute-start(bf16[2,16,512]{2,1,0:T(8,128)(2,1)S(1)} %get-tuple-element.80), channel_id=1, source_target_pairs={{0,1},{1,2},{2,3},{3,4},{4,5},{5,6},{6,7},{7,0},{8,9},{9,10},{10,1... | collective-permute-start | bytes 98312 | tf_op jit(solution)/shard_map/ppermute | solution.py:28
  179.8 10.2 %collective-permute-start.16 = (bf16[2,16,2048]{2,1,0:T(8,128)(2,1)S(1)}, bf16[2,16,2048]{2,1,0:T(8,128)(2,1)S(1)}, u32[]{:S(2)}, u32[]{:S(2)}) collective-permute-start(bf16[2,16,2048]{2,1,0:T(8,128)(2,1)S(1)} %get-tuple-element.76), channel_id=1, source_target_pairs={{0,8},{8,16},{16,24},{24,0},{1,9},{9,17},{17,25},{25,1},{2,10},{10... | collective-permute-start | bytes 393224 | tf_op jit(solution)/shard_map/ppermute | solution.py:28
  180.8 9.1 %collective-permute-start.17 = (bf16[2,16,2048]{2,1,0:T(8,128)(2,1)S(1)}, bf16[2,16,2048]{2,1,0:T(8,128)(2,1)S(1)}, u32[]{:S(2)}, u32[]{:S(2)}) collective-permute-start(bf16[2,16,2048]{2,1,0:T(8,128)(2,1)S(1)} %get-tuple-element.75), channel_id=1, source_target_pairs={{0,16},{8,24},{16,0},{24,8},{1,17},{9,25},{17,1},{25,9},{2,18},{10... | collective-permute-start | bytes 393224 | tf_op jit(solution)/shard_map/ppermute | solution.py:28
  182.4 7.5 %collective-permute-start.18 = (bf16[2,16,2048]{2,1,0:T(8,128)(2,1)S(1)}, bf16[2,16,2048]{2,1,0:T(8,128)(2,1)S(1)}, u32[]{:S(2)}, u32[]{:S(2)}) collective-permute-start(bf16[2,16,2048]{2,1,0:T(8,128)(2,1)S(1)} %get-tuple-element.74), channel_id=1, source_target_pairs={{0,24},{8,0},{16,8},{24,16},{1,25},{9,1},{17,9},{25,17},{2,26},{10... | collective-permute-start | bytes 393224 | tf_op jit(solution)/shard_map/ppermute | solution.py:28
  187.5 6.1 %copy-start.15 = (bf16[128,512]{1,0:T(8,128)(2,1)S(1)}, bf16[128,512]{1,0:T(8,128)(2,1)}, u32[]{:S(2)}) copy-start(bf16[128,512]{1,0:T(8,128)(2,1)} %get-tuple-element.61) | copy-start | bytes 393220
  187.5 6.8 %copy-start.14 = (bf16[128,512]{1,0:T(8,128)(2,1)S(1)}, bf16[128,512]{1,0:T(8,128)(2,1)}, u32[]{:S(2)}) copy-start(bf16[128,512]{1,0:T(8,128)(2,1)} %get-tuple-element.62) | copy-start | bytes 393220
  190.0 4.9 %collective-permute-start.27 = (f32[16,2560]{1,0:T(8,128)S(1)}, f32[16,2560]{1,0:T(8,128)S(1)}, u32[]{:S(2)}, u32[]{:S(2)}) collective-permute-start(f32[16,2560]{1,0:T(8,128)S(1)} %select_bitcast_fusion), channel_id=1, source_target_pairs={{0,32},{32,0},{1,33},{33,1},{2,34},{34,2},{3,35},{35,3},{4,36},{36... | collective-permute-start | bytes 491528 | tf_op jit(solution)/shard_map/ppermute | solution.py:36
  (2 other events, 1.8 us)
Sparse Core Ops, SparseCore 0:
  14.1 83.8 all-gather.2
Sparse Core Ops, SparseCore 1:
  96.3 54.9 reduce-scatter.1

commit v7 on v5

--- a/solution.py
+++ b/solution.py
@@ -93,15 +93,14 @@
     )(info, *parts, turned)
 
 
-def project_kernel(info, rows, block, out, weight, total):
-    y, core = info[1], info[3]
+def project_kernel(info, rows, block, out, total):
+    core = info[3]
     step = pl.program_id(0)
-    for r in range(4):
-        for z in range(8):
-            row = (lax.rem(y - r + 4, 4) * 8 + z) * 16
-            weight[pl.ds(pl.multiple_of(row, 16), 16), :] = block[z, r]
     product = lax.dot_general(
-        rows[...], weight[...], (((1,), (1,)), ((), ())), preferred_element_type=F32
+        rows[...],
+        block[...].reshape(512, PCOLS),
+        (((1,), (1,)), ((), ())),
+        preferred_element_type=F32,
     )
 
     @pl.when(step == 0)
@@ -128,10 +127,10 @@
         grid=(2560 // PCOLS,),
         in_specs=[
             pl.BlockSpec((1024, PCOLS), lambda n, info: (0, n)),
-            pl.BlockSpec((8, 4, None, 16, PCOLS), lambda n, info: (0, 0, rc, 0, n)),
+            pl.BlockSpec((32, None, 16, PCOLS), lambda n, info: (0, rc, 0, n)),
         ],
         out_specs=pl.BlockSpec((1024, 512), lambda n, info: (0, 0)),
-        scratch_shapes=[pltpu.VMEM((512, PCOLS), BF16), pltpu.VMEM((1024, 512), F32)],
+        scratch_shapes=[pltpu.VMEM((1024, 512), F32)],
     )
     return pl.pallas_call(
         project_kernel,
@@ -284,12 +283,11 @@
 
     weight_mine, weight_theirs = halves(out_weight)
     weight_pair = jnp.stack([weight_mine, swap(weight_theirs)])
-    near = jnp.stack([weight_pair] + [shift(weight_pair, "y", r) for r in (1, 2, 3)])
+    weight = lax.all_gather(weight_pair, ("y", "z"), axis=0, tiled=False)
 
     o_split = jnp.transpose(attn_out.reshape(TOK, 4, 1024), (1, 0, 2))
     grad_mine, grad_theirs = halves(out_grad[0])
     own = (grad_mine, swap(grad_theirs))
-    weight = lax.all_gather(after(near, o_split, grad_mine), "z", axis=0, tiled=False)
     o_own = lax.all_to_all(o_split, "x", split_axis=0, concat_axis=0, tiled=True)
     o_own = o_own.reshape(512, 1024)
 

time: 193 us -> 185 us (0.959)
  starting transfers between devices: 34.3 us -> 30 us
  waiting for transfers between devices: 72.3 us -> 68.8 us
    ppermute x15 -> x12, starting transfers between devices: 17.2 us -> 12.7 us  [shift(): lax.ppermute(value, axis, [(i, (i + by) % size) for i in range(size)])]
    ppermute x15 -> x12, waiting for transfers between devices: 66.1 us -> 64.2 us  [shift(): lax.ppermute(value, axis, [(i, (i + by) % size) for i in range(size)])]
    unnamed x33 -> x35, local copies, waits for them, and re-layouts: 6.42 us -> 6.5 us
  transfers between devices with their start and end apart: 25 -> 22, of which waited for: 13 -> 11; matrix products, arithmetic and copies ran while one was open for 7% -> 7% of each run, Pallas kernels for 26% -> 27%
where the time goes in v7:
time: 185 us; the launch traced here: 184 us
  waiting for transfers between devices  68.8 us (37%)
  Pallas kernels  49.7 us (27%)
  starting transfers between devices  30 us (16%)
  between operations  15.7 us (8%)
  local copies, waits for them, and re-layouts  15 us (8%)
  other arithmetic  5.33 us (3%)
    ppermute x12, waiting for transfers between devices, shift(): lax.ppermute(value, axis, [(i, (i + by) % size) for i in range(size)])  64.2 us
    pallas_call x1, Pallas kernels, attention(): pl.pallas_call(attention_kernel, out_shape=[jax.ShapeDtypeStruct((2, TOK,...  16.8 us
    pallas_call x2, Pallas kernels, project(): pl.pallas_call(project_kernel, out_shape=jax.ShapeDtypeStruct((1024, 512)...  15 us
    ppermute x12, starting transfers between devices, shift(): lax.ppermute(value, axis, [(i, (i + by) % size) for i in range(size)])  12.7 us
    pallas_call x1, Pallas kernels, weight_product(): pl.pallas_call(functools.partial(weight_kernel, factor), out_shape=(jax.S...  11.6 us
    ppermute x6, starting transfers between devices, swap(): return lax.ppermute(value, 'core', [(0, 1), (1, 0)])  8.71 us
    unnamed x35, local copies, waits for them, and re-layouts  6.5 us
    all_to_all x1, starting transfers between devices, per_device(): lax.all_to_all(packed, ('x', 'core'), split_axis=0, concat_axis=0, tiled=...  4.77 us
  transfers between devices with their start and end apart: 22, of which 11 were waited for; matrix products, arithmetic and copies ran while one was open for 7% of the time, Pallas kernels for 27%

profile of v7, /device:TPU:1, one launch (start us, length us, event | category | flops | bytes accessed | tf_op | source)
XLA Modules:
  0.0 184.5 jit_solution(6169123999295413387)
XLA Ops:
  8.1 1.0 select_bitcast_fusion.1
  9.1 3.3 %collective-permute-start.8 = (bf16[16,2560]{1,0:T(8,128)(2,1)S(1)}, bf16[16,2560]{1,0:T(8,128)(2,1)S(1)}, u32[]{:S(2)}, u32[]{:S(2)}) collective-permute-start(bf16[16,2560]{1,0:T(8,128)(2,1)S(1)} %get-tuple-element.55), channel_id=1, source_target_pairs={{0,32},{32,0},{1,33},{33,1},{2,34},{34,2},{3,35},{35,3},{4,36},{36... | collective-permute-start | bytes 245768 | tf_op jit(solution)/shard_map/ppermute | solution.py:35
  12.4 0.9 collective-permute-done.8
  13.3 0.7 pad_maximum_fusion.2
  14.0 1.4 broadcast_select_fusion
  16.2 1.3 copy.21
  17.5 3.6 %all-to-all-start = ((bf16[4,128,1024]{2,1,0:T(8,128)(2,1)}), bf16[4,128,1024]{2,1,0:T(8,128)(2,1)S(1)}, u32[]{:S(2)}, u32[]{:S(2)}) async-start(bf16[4,128,1024]{2,1,0:T(8,128)(2,1)} %bitcast.41), calls=%async_computation | async-start | bytes 2097152 | tf_op jit(solution)/shard_map/all_to_all | solution.py:291
  21.2 1.4 collective-permute-start.1
  22.5 1.4 collective-permute-start.2
  23.9 0.7 copy.16
  24.6 1.7 reshape.39
  27.3 1.3 maximum_bitcast_fusion
  28.6 21.4 %collective-permute-done.1.refs_2_ = bf16[128,2560]{1,0:T(8,128)(2,1)} collective-permute-done((bf16[128,2560]{1,0:T(8,128)(2,1)S(1)}, bf16[128,2560]{1,0:T(8,128)(2,1)}, u32[]{:S(2)}, u32[]{:S(2)}) %collective-permute-start.1) | collective-permute-done | bytes 655392 | tf_op jit(solution)/shard_map/ppermute | solution.py:27
  50.0 1.1 collective-permute-start.7
  51.1 0.6 collective-permute-start.4
  51.7 0.8 collective-permute-start.3
  52.6 2.6 %collective-permute-start.6 = (bf16[128,2560]{1,0:T(8,128)(2,1)S(1)}, bf16[128,2560]{1,0:T(8,128)(2,1)}, u32[]{:S(2)}, u32[]{:S(2)}) collective-permute-start(bf16[128,2560]{1,0:T(8,128)(2,1)S(1)} %collective-permute-done.2.refs_5_), channel_id=1, source_target_pairs={{0,192},{64,0},{128,64},{192,128},{1,193},{65,1},{129,65},{193,129... | collective-permute-start | bytes 1966088 | tf_op jit(solution)/shard_map/ppermute | solution.py:27
  55.3 0.6 concatenate.9.info
  55.9 1.0 copy-done.4
  56.9 3.5 %shard_map.102.refs_8_ = bf16[1024,1024]{1,0:T(8,128)(2,1)} custom-call(bf16[512,1024]{1,0:T(8,128)(2,1)} %bitcast.45, bf16[512,1024]{1,0:T(8,128)(2,1)} %copy-done.4), custom_call_target="tpu_custom_call" | custom-call | tf_op jit(solution)/shard_map/pallas_call | solution.py:45
  60.4 7.0 %collective-permute-done.4.refs_4_ = bf16[128,2560]{1,0:T(8,128)(2,1)} collective-permute-done((bf16[128,2560]{1,0:T(8,128)(2,1)S(1)}, bf16[128,2560]{1,0:T(8,128)(2,1)}, u32[]{:S(2)}, u32[]{:S(2)}) %collective-permute-start.4) | collective-permute-done | bytes 655392 | tf_op jit(solution)/shard_map/ppermute | solution.py:27
  67.5 1.7 collective-permute-done.3.refs_3_
  69.2 14.0 %collective-permute-done.5.refs_6_ = bf16[128,2560]{1,0:T(8,128)(2,1)} collective-permute-done((bf16[128,2560]{1,0:T(8,128)(2,1)}, bf16[128,2560]{1,0:T(8,128)(2,1)}, u32[]{:S(2)}, u32[]{:S(2)}) %collective-permute-start.5) | collective-permute-done | bytes 655392 | tf_op jit(solution)/shard_map/ppermute | solution.py:27
  83.3 11.6 %shard_map.103 = (bf16[8,4,2,16,2560]{4,3,2,1,0:T(8,128)(2,1)}, bf16[1024,2560]{1,0:T(8,128)(2,1)}) custom-call(s32[7]{0:T(128)} %concatenate.9.info, bf16[128,2560]{1,0:T(8,128)(2,1)} %copy-done.1, bf16[128,2560]{1,0:T(8,128)(2,1)} %collective-permute-done.refs_1_, bf16[128,2560]{1,0:T(8,128)(2,1)} %collective-permute-done.1.refs_2_, ...), custom_call_target="tpu_custom_call" | custom-call | flops 1048576 | bytes 1048576 | tf_op jit(solution)/shard_map/pallas_call | solution.py:82
  94.9 4.8 %all-to-all-start.1 = ((bf16[8,128,768]{2,1,0:T(8,128)(2,1)}), bf16[8,128,768]{2,1,0:T(8,128)(2,1)S(1)}, u32[]{:S(2)}, u32[]{:S(2)}) async-start(bf16[8,128,768]{2,1,0:T(8,128)(2,1)} %maximum_bitcast_fusion), calls=%async_computation.2 | async-start | bytes 3145728 | tf_op jit(solution)/shard_map/all_to_all | solution.py:307
  99.7 7.3 %shard_map.105 = bf16[1024,512]{1,0:T(8,128)(2,1)} custom-call(s32[7]{0:T(128)} %concatenate.9.info, bf16[1024,2560]{1,0:T(8,128)(2,1)} %get-tuple-element.30.rows, bf16[32,2,16,2560]{3,2,1,0:T(8,128)(2,1)} %bitcast.42), custom_call_target="tpu_custom_call" | custom-call | flops 1048576 | bytes 1048576 | tf_op jit(solution)/shard_map/pallas_call | solution.py:135
  107.0 2.1 %collective-permute-start.9 = (bf16[1024,512]{1,0:T(8,128)(2,1)}, bf16[1024,512]{1,0:T(8,128)(2,1)S(1)}, u32[]{:S(2)}, u32[]{:S(2)}) collective-permute-start(bf16[1024,512]{1,0:T(8,128)(2,1)} %shard_map.105), channel_id=1, source_target_pairs={{0,32},{32,0},{1,33},{33,1},{2,34},{34,2},{3,35},{35,3},{4,36},{36... | collective-permute-start | bytes 3145736 | tf_op jit(solution)/shard_map/ppermute | solution.py:35
  109.0 7.7 %shard_map.104.mine = f32[1024,512]{1,0:T(8,128)} custom-call(s32[7]{0:T(128)} %concatenate.9.info, bf16[1024,2560]{1,0:T(8,128)(2,1)} %get-tuple-element.30.rows, bf16[32,2,16,2560]{3,2,1,0:T(8,128)(2,1)} %bitcast.43), custom_call_target="tpu_custom_call" | custom-call | flops 1048576 | bytes 1048576 | tf_op jit(solution)/shard_map/pallas_call | solution.py:135
  116.7 3.7 %all-to-all-done.1 = bf16[8,128,768]{2,1,0:T(8,128)(2,1)S(1)} async-done(((bf16[8,128,768]{2,1,0:T(8,128)(2,1)}), bf16[8,128,768]{2,1,0:T(8,128)(2,1)S(1)}, u32[]{:S(2)}, u32[]{:S(2)}) %all-to-all-start.1) | async-done | bytes 1572896 | tf_op jit(solution)/shard_map/all_to_all | solution.py:307
  120.4 1.2 copy-done.2
  121.9 16.8 %shard_map.106 = (bf16[2,128,768]{2,1,0:T(8,128)(2,1)}, bf16[2,128,768]{2,1,0:T(8,128)(2,1)}, bf16[2,128,768]{2,1,0:T(8,128)(2,1)}, bf16[2,128,768]{2,1,0:T(8,128)(2,1)}) custom-call(s32[7]{0:T(128)} %concatenate.9.info, bf16[1024,768]{1,0:T(8,128)(2,1)} %bitcast.47, bf16[1024,768]{1,0:T(8,128)(2,1)} %bitcast.48, bf16[1024,768]{1,0:T(8,128)(2,1)} %bitcast.49, ...), custom_call_target="tpu_custom_call" | custom-call | flops 14000000000 | bytes 8388608 | tf_op jit(solution)/shard_map/pallas_call | solution.py:223
  138.7 0.8 collective-permute-start.12
  139.5 1.3 collective-permute-start.11
  140.8 0.9 slice.52
  141.8 7.0 %collective-permute-done.12.refs_3_ = bf16[2,128,768]{2,1,0:T(8,128)(2,1)S(1)} collective-permute-done((bf16[2,128,768]{2,1,0:T(8,128)(2,1)}, bf16[2,128,768]{2,1,0:T(8,128)(2,1)S(1)}, u32[]{:S(2)}, u32[]{:S(2)}) %collective-permute-start.12) | collective-permute-done | bytes 393248 | tf_op jit(solution)/shard_map/ppermute | solution.py:27
  148.8 2.0 %collective-permute-done.11.refs_2_ = bf16[2,128,768]{2,1,0:T(8,128)(2,1)S(1)} collective-permute-done((bf16[2,128,768]{2,1,0:T(8,128)(2,1)}, bf16[2,128,768]{2,1,0:T(8,128)(2,1)S(1)}, u32[]{:S(2)}, u32[]{:S(2)}) %collective-permute-start.11) | collective-permute-done | bytes 393248 | tf_op jit(solution)/shard_map/ppermute | solution.py:27
  150.8 10.0 %collective-permute-done.10.refs_1_ = bf16[2,128,768]{2,1,0:T(8,128)(2,1)S(1)} collective-permute-done((bf16[2,128,768]{2,1,0:T(8,128)(2,1)}, bf16[2,128,768]{2,1,0:T(8,128)(2,1)S(1)}, u32[]{:S(2)}, u32[]{:S(2)}) %collective-permute-start.10) | collective-permute-done | bytes 393248 | tf_op jit(solution)/shard_map/ppermute | solution.py:27
  161.4 1.2 slice_bitcast_fusion
  162.7 2.5 %collective-permute-start.14 = (bf16[2,16,2560]{2,1,0:T(8,128)(2,1)S(1)}, bf16[2,16,2560]{2,1,0:T(8,128)(2,1)S(1)}, u32[]{:S(2)}, u32[]{:S(2)}) collective-permute-start(bf16[2,16,2560]{2,1,0:T(8,128)(2,1)S(1)} %get-tuple-element.49), channel_id=1, source_target_pairs={{0,16},{8,24},{16,0},{24,8},{1,17},{9,25},{17,1},{25,9},{2,18},{10... | collective-permute-start | bytes 491528 | tf_op jit(solution)/shard_map/ppermute | solution.py:27
  165.3 1.1 collective-permute-start.15
  166.4 0.9 copy-done.8
  167.2 2.8 %shard_map.107 = (bf16[128,4096]{1,0:T(8,128)(2,1)}, bf16[128,512]{1,0:T(8,128)(2,1)}, bf16[128,512]{1,0:T(8,128)(2,1)}) custom-call(s32[7]{0:T(128)} %concatenate.9.info, bf16[2,128,768]{2,1,0:T(8,128)(2,1)} %get-tuple-element.35.refs_0_, bf16[2,128,768]{2,1,0:T(8,128)(2,1)} %copy-done.7, bf16[2,128,768]{2,1,0:T(8,128)(2,1)} %copy-done.6, ...), custom_call_target="tpu_custom_call" | custom-call | tf_op jit(solution)/shard_map/pallas_call | solution.py:254
  170.0 2.5 %copy.19 = bf16[16,8,32,128]{3,2,1,0:T(8,128)(2,1)} copy(bf16[16,8,32,128]{3,1,2,0:T(8,128)(2,1)} %bitcast.54) | data formatting | bytes 2097152
  172.9 0.6 collective-permute-done.15
  173.6 1.2 collective-permute-start.17
  174.9 0.7 reshape.46
  175.6 0.7 reshape.47
  176.3 0.7 pad_maximum_fusion.1
  (64 shorter events, 3.6 us)
Async XLA Ops:
  8.0 7.9 %copy-start.3 = (bf16[1,128,32,128]{3,2,1,0:T(8,128)(2,1)S(1)}, bf16[1,128,32,128]{3,2,1,0:T(8,128)(2,1)}, u32[]{:S(2)}) copy-start(bf16[1,128,32,128]{3,2,1,0:T(8,128)(2,1)} %param.10) | copy-start | bytes 3145732
  8.0 91.7 %all-gather.3.cloned.1.call-start = ((), (), s32[]{:S(2)}) async-start(), calls=%async_computation.4 | async-start | bytes 5406720 | tf_op jit(solution)/shard_map/all_gather | solution.py:286
  9.1 4.3 %collective-permute-start.8 = (bf16[16,2560]{1,0:T(8,128)(2,1)S(1)}, bf16[16,2560]{1,0:T(8,128)(2,1)S(1)}, u32[]{:S(2)}, u32[]{:S(2)}) collective-permute-start(bf16[16,2560]{1,0:T(8,128)(2,1)S(1)} %get-tuple-element.55), channel_id=1, source_target_pairs={{0,32},{32,0},{1,33},{33,1},{2,34},{34,2},{3,35},{35,3},{4,36},{36... | collective-permute-start | bytes 245768 | tf_op jit(solution)/shard_map/ppermute | solution.py:35
  15.4 35.7 %copy-start.1 = (bf16[128,2560]{1,0:T(8,128)(2,1)}, bf16[128,2560]{1,0:T(8,128)(2,1)S(1)}, u32[]{:S(2)}) copy-start(bf16[128,2560]{1,0:T(8,128)(2,1)S(1)} %get-tuple-element.47.refs_0_) | copy-start | bytes 1966084
  15.4 7.1 %collective-permute-start = (bf16[128,2560]{1,0:T(8,128)(2,1)S(1)}, bf16[128,2560]{1,0:T(8,128)(2,1)}, u32[]{:S(2)}, u32[]{:S(2)}) collective-permute-start(bf16[128,2560]{1,0:T(8,128)(2,1)S(1)} %get-tuple-element.46), channel_id=1, source_target_pairs={{0,32},{32,0},{1,33},{33,1},{2,34},{34,2},{3,35},{35,3},{4,36},{36... | collective-permute-start | bytes 1966088 | tf_op jit(solution)/shard_map/ppermute | solution.py:35
  16.2 7.8 %copy-start.11 = (bf16[1,128,4,128]{3,2,1,0:T(4,128)(2,1)S(1)}, bf16[1,128,4,128]{3,2,1,0:T(4,128)(2,1)}, u32[]{:S(2)}) copy-start(bf16[1,128,4,128]{3,2,1,0:T(4,128)(2,1)} %param.9) | copy-start | bytes 393220
  17.5 7.1 %copy-start.12 = (bf16[1,128,4,128]{3,2,1,0:T(4,128)(2,1)S(1)}, bf16[1,128,4,128]{3,2,1,0:T(4,128)(2,1)}, u32[]{:S(2)}) copy-start(bf16[1,128,4,128]{3,2,1,0:T(4,128)(2,1)} %param.8) | copy-start | bytes 393220
  17.5 32.6 %all-to-all-start = ((bf16[4,128,1024]{2,1,0:T(8,128)(2,1)}), bf16[4,128,1024]{2,1,0:T(8,128)(2,1)S(1)}, u32[]{:S(2)}, u32[]{:S(2)}) async-start(bf16[4,128,1024]{2,1,0:T(8,128)(2,1)} %bitcast.41), calls=%async_computation | async-start | bytes 2097152 | tf_op jit(solution)/shard_map/all_to_all | solution.py:291
  21.1 140.3 %reduce-scatter.2.cloned.1.call-start = ((), (), s32[]{:S(2)}) async-start(), calls=%async_computation.3 | async-start | bytes 5898240 | tf_op jit(solution)/shard_map/reduce_scatter | solution.py:314
  21.2 28.9 %collective-permute-start.1 = (bf16[128,2560]{1,0:T(8,128)(2,1)S(1)}, bf16[128,2560]{1,0:T(8,128)(2,1)}, u32[]{:S(2)}, u32[]{:S(2)}) collective-permute-start(bf16[128,2560]{1,0:T(8,128)(2,1)S(1)} %get-tuple-element.47.refs_0_), channel_id=1, source_target_pairs={{0,64},{64,128},{128,192},{192,0},{1,65},{65,129},{129,193},{193,1... | collective-permute-start | bytes 1966088 | tf_op jit(solution)/shard_map/ppermute | solution.py:27
  22.5 27.5 %collective-permute-start.2 = (bf16[128,2560]{1,0:T(8,128)(2,1)}, bf16[128,2560]{1,0:T(8,128)(2,1)S(1)}, u32[]{:S(2)}, u32[]{:S(2)}) collective-permute-start(bf16[128,2560]{1,0:T(8,128)(2,1)} %collective-permute-done.refs_1_), channel_id=1, source_target_pairs={{0,192},{64,0},{128,64},{192,128},{1,193},{65,1},{129,65},{193,129... | collective-permute-start | bytes 1966088 | tf_op jit(solution)/shard_map/ppermute | solution.py:27
  26.3 0.9 copy-start.10
  27.2 28.0 %copy-start.15 = (s32[1,3]{1,0:T(1,128)S(1)}, s32[1,3]{1,0:T(1,128)}, u32[]{:S(2)}) copy-start(s32[1,3]{1,0:T(1,128)} %param.13) | copy-start | bytes 40
  50.0 5.9 %copy-start = (bf16[4,128,1024]{2,1,0:T(8,128)(2,1)}, bf16[4,128,1024]{2,1,0:T(8,128)(2,1)S(1)}, u32[]{:S(2)}) copy-start(bf16[4,128,1024]{2,1,0:T(8,128)(2,1)S(1)} %all-to-all-done) | copy-start | bytes 3145732
  50.0 33.2 %copy-start.9 = (bf16[128,2560]{1,0:T(8,128)(2,1)}, bf16[128,2560]{1,0:T(8,128)(2,1)S(1)}, u32[]{:S(2)}) copy-start(bf16[128,2560]{1,0:T(8,128)(2,1)S(1)} %collective-permute-done.2.refs_5_) | copy-start | bytes 1966084
  50.0 5.8 %collective-permute-start.7 = (bf16[512,1024]{1,0:T(8,128)(2,1)S(1)}, bf16[512,1024]{1,0:T(8,128)(2,1)S(1)}, u32[]{:S(2)}, u32[]{:S(2)}) collective-permute-start(bf16[512,1024]{1,0:T(8,128)(2,1)S(1)} %bitcast.44), channel_id=1, source_target_pairs={{0,32},{32,0},{1,33},{33,1},{2,34},{34,2},{3,35},{35,3},{4,36},{36... | collective-permute-start | bytes 3145736 | tf_op jit(solution)/shard_map/ppermute | solution.py:35
  51.1 16.4 %collective-permute-start.4 = (bf16[128,2560]{1,0:T(8,128)(2,1)S(1)}, bf16[128,2560]{1,0:T(8,128)(2,1)}, u32[]{:S(2)}, u32[]{:S(2)}) collective-permute-start(bf16[128,2560]{1,0:T(8,128)(2,1)S(1)} %get-tuple-element.47.refs_0_), channel_id=1, source_target_pairs={{0,192},{64,0},{128,64},{192,128},{1,193},{65,1},{129,65},{193,129... | collective-permute-start | bytes 1966088 | tf_op jit(solution)/shard_map/ppermute | solution.py:27
  51.7 17.5 %collective-permute-start.3 = (bf16[128,2560]{1,0:T(8,128)(2,1)}, bf16[128,2560]{1,0:T(8,128)(2,1)}, u32[]{:S(2)}, u32[]{:S(2)}) collective-permute-start(bf16[128,2560]{1,0:T(8,128)(2,1)} %collective-permute-done.refs_1_), channel_id=1, source_target_pairs={{0,64},{64,128},{128,192},{192,0},{1,65},{65,129},{129,193},{193,1... | collective-permute-start | bytes 1966088 | tf_op jit(solution)/shard_map/ppermute | solution.py:27
  52.6 30.7 %collective-permute-start.5 = (bf16[128,2560]{1,0:T(8,128)(2,1)}, bf16[128,2560]{1,0:T(8,128)(2,1)}, u32[]{:S(2)}, u32[]{:S(2)}) collective-permute-start(bf16[128,2560]{1,0:T(8,128)(2,1)} %collective-permute-done.1.refs_2_), channel_id=1, source_target_pairs={{0,64},{64,128},{128,192},{192,0},{1,65},{65,129},{129,193},{193,1... | collective-permute-start | bytes 1966088 | tf_op jit(solution)/shard_map/ppermute | solution.py:27
  52.6 30.7 %collective-permute-start.6 = (bf16[128,2560]{1,0:T(8,128)(2,1)S(1)}, bf16[128,2560]{1,0:T(8,128)(2,1)}, u32[]{:S(2)}, u32[]{:S(2)}) collective-permute-start(bf16[128,2560]{1,0:T(8,128)(2,1)S(1)} %collective-permute-done.2.refs_5_), channel_id=1, source_target_pairs={{0,192},{64,0},{128,64},{192,128},{1,193},{65,1},{129,65},{193,129... | collective-permute-start | bytes 1966088 | tf_op jit(solution)/shard_map/ppermute | solution.py:27
  55.9 1.0 copy-start.4
  94.9 25.5 %all-to-all-start.1 = ((bf16[8,128,768]{2,1,0:T(8,128)(2,1)}), bf16[8,128,768]{2,1,0:T(8,128)(2,1)S(1)}, u32[]{:S(2)}, u32[]{:S(2)}) async-start(bf16[8,128,768]{2,1,0:T(8,128)(2,1)} %maximum_bitcast_fusion), calls=%async_computation.2 | async-start | bytes 3145728 | tf_op jit(solution)/shard_map/all_to_all | solution.py:307
  107.0 13.5 %collective-permute-start.9 = (bf16[1024,512]{1,0:T(8,128)(2,1)}, bf16[1024,512]{1,0:T(8,128)(2,1)S(1)}, u32[]{:S(2)}, u32[]{:S(2)}) collective-permute-start(bf16[1024,512]{1,0:T(8,128)(2,1)} %shard_map.105), channel_id=1, source_target_pairs={{0,32},{32,0},{1,33},{33,1},{2,34},{34,2},{3,35},{35,3},{4,36},{36... | collective-permute-start | bytes 3145736 | tf_op jit(solution)/shard_map/ppermute | solution.py:35
  120.4 1.2 copy-start.2
  120.4 1.5 copy-start.16
  138.7 10.1 %collective-permute-start.12 = (bf16[2,128,768]{2,1,0:T(8,128)(2,1)}, bf16[2,128,768]{2,1,0:T(8,128)(2,1)S(1)}, u32[]{:S(2)}, u32[]{:S(2)}) collective-permute-start(bf16[2,128,768]{2,1,0:T(8,128)(2,1)} %get-tuple-element.33), channel_id=1, source_target_pairs={{0,192},{64,0},{128,64},{192,128},{1,193},{65,1},{129,65},{193,129... | collective-permute-start | bytes 1179656 | tf_op jit(solution)/shard_map/ppermute | solution.py:27
  139.5 11.2 %collective-permute-start.11 = (bf16[2,128,768]{2,1,0:T(8,128)(2,1)}, bf16[2,128,768]{2,1,0:T(8,128)(2,1)S(1)}, u32[]{:S(2)}, u32[]{:S(2)}) collective-permute-start(bf16[2,128,768]{2,1,0:T(8,128)(2,1)} %get-tuple-element.32), channel_id=1, source_target_pairs={{0,128},{64,192},{128,0},{192,64},{1,129},{65,193},{129,1},{193,65... | collective-permute-start | bytes 1179656 | tf_op jit(solution)/shard_map/ppermute | solution.py:27
  140.8 19.9 %collective-permute-start.10 = (bf16[2,128,768]{2,1,0:T(8,128)(2,1)}, bf16[2,128,768]{2,1,0:T(8,128)(2,1)S(1)}, u32[]{:S(2)}, u32[]{:S(2)}) collective-permute-start(bf16[2,128,768]{2,1,0:T(8,128)(2,1)} %get-tuple-element.31), channel_id=1, source_target_pairs={{0,64},{64,128},{128,192},{192,0},{1,65},{65,129},{129,193},{193,1... | collective-permute-start | bytes 1179656 | tf_op jit(solution)/shard_map/ppermute | solution.py:27
  148.8 17.6 %copy-start.5 = (bf16[2,128,768]{2,1,0:T(8,128)(2,1)}, bf16[2,128,768]{2,1,0:T(8,128)(2,1)S(1)}, u32[]{:S(2)}) copy-start(bf16[2,128,768]{2,1,0:T(8,128)(2,1)S(1)} %collective-permute-done.12.refs_3_) | copy-start | bytes 1179652
  150.8 15.6 %copy-start.6 = (bf16[2,128,768]{2,1,0:T(8,128)(2,1)}, bf16[2,128,768]{2,1,0:T(8,128)(2,1)S(1)}, u32[]{:S(2)}) copy-start(bf16[2,128,768]{2,1,0:T(8,128)(2,1)S(1)} %collective-permute-done.11.refs_2_) | copy-start | bytes 1179652
  160.7 5.6 %copy-start.7 = (bf16[2,128,768]{2,1,0:T(8,128)(2,1)}, bf16[2,128,768]{2,1,0:T(8,128)(2,1)S(1)}, u32[]{:S(2)}) copy-start(bf16[2,128,768]{2,1,0:T(8,128)(2,1)S(1)} %collective-permute-done.10.refs_1_) | copy-start | bytes 1179652
  160.9 5.5 %collective-permute-start.16 = (bf16[4,128,768]{2,1,0:T(8,128)(2,1)S(1)}, bf16[4,128,768]{2,1,0:T(8,128)(2,1)S(1)}, u32[]{:S(2)}, u32[]{:S(2)}) collective-permute-start(bf16[4,128,768]{2,1,0:T(8,128)(2,1)S(1)} %pad_maximum_fusion), channel_id=1, source_target_pairs={{0,32},{32,0},{1,33},{33,1},{2,34},{34,2},{3,35},{35,3},{4,36},{36... | collective-permute-start | bytes 2359304 | tf_op jit(solution)/shard_map/ppermute | solution.py:35
  162.6 9.9 %collective-permute-start.13 = (bf16[2,16,2560]{2,1,0:T(8,128)(2,1)S(1)}, bf16[2,16,2560]{2,1,0:T(8,128)(2,1)S(1)}, u32[]{:S(2)}, u32[]{:S(2)}) collective-permute-start(bf16[2,16,2560]{2,1,0:T(8,128)(2,1)S(1)} %get-tuple-element.50), channel_id=1, source_target_pairs={{0,8},{8,16},{16,24},{24,0},{1,9},{9,17},{17,25},{25,1},{2,10},{10... | collective-permute-start | bytes 491528 | tf_op jit(solution)/shard_map/ppermute | solution.py:27
  162.7 10.1 %collective-permute-start.14 = (bf16[2,16,2560]{2,1,0:T(8,128)(2,1)S(1)}, bf16[2,16,2560]{2,1,0:T(8,128)(2,1)S(1)}, u32[]{:S(2)}, u32[]{:S(2)}) collective-permute-start(bf16[2,16,2560]{2,1,0:T(8,128)(2,1)S(1)} %get-tuple-element.49), channel_id=1, source_target_pairs={{0,16},{8,24},{16,0},{24,8},{1,17},{9,25},{17,1},{25,9},{2,18},{10... | collective-permute-start | bytes 491528 | tf_op jit(solution)/shard_map/ppermute | solution.py:27
  165.3 8.3 %collective-permute-start.15 = (bf16[2,16,2560]{2,1,0:T(8,128)(2,1)S(1)}, bf16[2,16,2560]{2,1,0:T(8,128)(2,1)S(1)}, u32[]{:S(2)}, u32[]{:S(2)}) collective-permute-start(bf16[2,16,2560]{2,1,0:T(8,128)(2,1)S(1)} %get-tuple-element.48), channel_id=1, source_target_pairs={{0,24},{8,0},{16,8},{24,16},{1,25},{9,1},{17,9},{25,17},{2,26},{10... | collective-permute-start | bytes 491528 | tf_op jit(solution)/shard_map/ppermute | solution.py:27
  166.4 0.9 copy-start.8
  170.0 4.8 %copy-start.14 = (bf16[128,512]{1,0:T(8,128)(2,1)S(1)}, bf16[128,512]{1,0:T(8,128)(2,1)}, u32[]{:S(2)}) copy-start(bf16[128,512]{1,0:T(8,128)(2,1)} %get-tuple-element.40) | copy-start | bytes 393220
  170.0 5.5 %copy-start.13 = (bf16[128,512]{1,0:T(8,128)(2,1)S(1)}, bf16[128,512]{1,0:T(8,128)(2,1)}, u32[]{:S(2)}) copy-start(bf16[128,512]{1,0:T(8,128)(2,1)} %get-tuple-element.41) | copy-start | bytes 393220
  173.6 2.6 %collective-permute-start.17 = (f32[16,2560]{1,0:T(8,128)S(1)}, f32[16,2560]{1,0:T(8,128)S(1)}, u32[]{:S(2)}, u32[]{:S(2)}) collective-permute-start(f32[16,2560]{1,0:T(8,128)S(1)} %select_bitcast_fusion), channel_id=1, source_target_pairs={{0,32},{32,0},{1,33},{33,1},{2,34},{34,2},{3,35},{35,3},{4,36},{36... | collective-permute-start | bytes 491528 | tf_op jit(solution)/shard_map/ppermute | solution.py:35
Sparse Core Ops, SparseCore 0:
  14.2 84.4 all-gather.2
Sparse Core Ops, SparseCore 1:
  95.0 64.9 reduce-scatter.1

commit v8 on v5

--- a/solution.py
+++ b/solution.py
@@ -305,7 +305,8 @@
 
     prev0, prev1 = (shift(part, "x", 1) for part in own)
     succ0, succ1 = (shift(part, "x", -1) for part in own)
-    prev0, succ1, packed, o_own = lax.optimization_barrier((prev0, succ1, packed, o_own))
+    prev0, succ1, o_own = lax.optimization_barrier((prev0, succ1, o_own))
+    packed = after(packed, prev0, succ1)
     packed = lax.all_to_all(packed, ("x", "core"), split_axis=0, concat_axis=0, tiled=True)
     packed = packed.reshape(1024, 768)
     o_sib = swap(o_own)

time: 193 us -> 198 us (1.026)
  waiting for transfers between devices: 72.3 us -> 82 us
  starting transfers between devices: 34.3 us -> 29.8 us
    ppermute x15, waiting for transfers between devices: 66.1 us -> 76.2 us  [shift(): lax.ppermute(value, axis, [(i, (i + by) % size) for i in range(size)])]
    ppermute x15, starting transfers between devices: 17.2 us -> 13.9 us  [shift(): lax.ppermute(value, axis, [(i, (i + by) % size) for i in range(size)])]
    unnamed x33 -> x35, local copies, waits for them, and re-layouts: 6.42 us -> 7.16 us
where the time goes in v8:
time: 198 us
  waiting for transfers between devices  82 us (41%)
  Pallas kernels  50.4 us (25%)
  starting transfers between devices  29.8 us (15%)
  between operations  14.3 us (7%)
  local copies, waits for them, and re-layouts  13.9 us (7%)
  other arithmetic  7.15 us (4%)
    ppermute x15, waiting for transfers between devices, shift(): lax.ppermute(value, axis, [(i, (i + by) % size) for i in range(size)])  76.2 us
    pallas_call x1, Pallas kernels, attention(): pl.pallas_call(attention_kernel, out_shape=[jax.ShapeDtypeStruct((2, TOK,...  16.8 us
    pallas_call x2, Pallas kernels, project(): pl.pallas_call(project_kernel, out_shape=jax.ShapeDtypeStruct((1024, 512)...  15.7 us
    ppermute x15, starting transfers between devices, shift(): lax.ppermute(value, axis, [(i, (i + by) % size) for i in range(size)])  13.9 us
    pallas_call x1, Pallas kernels, weight_product(): pl.pallas_call(functools.partial(weight_kernel, factor), out_shape=(jax.S...  11.5 us
    ppermute x6, starting transfers between devices, swap(): return lax.ppermute(value, 'core', [(0, 1), (1, 0)])  7.2 us
    unnamed x35, local copies, waits for them, and re-layouts  7.16 us
    all_to_all x1, waiting for transfers between devices, per_device(): lax.all_to_all(packed, ('x', 'core'), split_axis=0, concat_axis=0, tiled=...  4.78 us
  transfers between devices with their start and end apart: 25, of which 13 were waited for; matrix products, arithmetic and copies ran while one was open for 7% of the time, Pallas kernels for 26%

profile of v8, /device:TPU:1, one launch (start us, length us, event | category | flops | bytes accessed | tf_op | source)
XLA Modules:
  0.0 197.5 jit_solution(1248247146936056192)
XLA Ops:
  7.2 1.0 select_bitcast_fusion.1
  8.3 3.3 %collective-permute-start.8 = (bf16[16,2560]{1,0:T(8,128)(2,1)S(1)}, bf16[16,2560]{1,0:T(8,128)(2,1)S(1)}, u32[]{:S(2)}, u32[]{:S(2)}) collective-permute-start(bf16[16,2560]{1,0:T(8,128)(2,1)S(1)} %get-tuple-element.59), channel_id=1, source_target_pairs={{0,32},{32,0},{1,33},{33,1},{2,34},{34,2},{3,35},{35,3},{4,36},{36... | collective-permute-start | bytes 245768 | tf_op jit(solution)/shard_map/ppermute | solution.py:35
  11.6 0.9 collective-permute-done.8
  13.2 1.0 collective-permute-start.11
  14.5 0.7 collective-permute-start.9
  15.2 2.2 %broadcast_select_fusion = (bf16[128,2560]{1,0:T(8,128)(2,1)}, bf16[128,2560]{1,0:T(8,128)(2,1)S(1)}) fusion(pred[]{:T(512)S(6)} %eq.2, bf16[128,5120]{1,0:T(8,128)(2,1)} %bitcast.55), kind=kLoop, calls=%fused_computation.4 | loop fusion | flops 655360 | bytes 2621441 | tf_op jit(solution)/shard_map/jit(_where)/select_n | solution.py:283
  17.7 1.3 copy.21
  19.0 2.0 %collective-permute-done.10 = bf16[2,16,2560]{2,1,0:T(8,128)(2,1)S(1)} collective-permute-done((bf16[2,16,2560]{2,1,0:T(8,128)(2,1)}, bf16[2,16,2560]{2,1,0:T(8,128)(2,1)S(1)}, u32[]{:S(2)}, u32[]{:S(2)}) %collective-permute-start.10) | collective-permute-done | bytes 163872 | tf_op jit(solution)/shard_map/ppermute | solution.py:27
  21.1 4.5 %collective-permute-done.9 = bf16[2,16,2560]{2,1,0:T(8,128)(2,1)S(1)} collective-permute-done((bf16[2,16,2560]{2,1,0:T(8,128)(2,1)}, bf16[2,16,2560]{2,1,0:T(8,128)(2,1)S(1)}, u32[]{:S(2)}, u32[]{:S(2)}) %collective-permute-start.9) | collective-permute-done | bytes 163872 | tf_op jit(solution)/shard_map/ppermute | solution.py:27
  25.5 1.0 pad_maximum_fusion.1
  27.1 4.0 %all-to-all-start = ((bf16[4,128,1024]{2,1,0:T(8,128)(2,1)}), bf16[4,128,1024]{2,1,0:T(8,128)(2,1)S(1)}, u32[]{:S(2)}, u32[]{:S(2)}) async-start(bf16[4,128,1024]{2,1,0:T(8,128)(2,1)} %bitcast.46), calls=%async_computation | async-start | bytes 2097152 | tf_op jit(solution)/shard_map/all_to_all | solution.py:293
  31.1 1.5 collective-permute-start.1
  32.6 1.3 collective-permute-start.2
  33.9 26.0 %collective-permute-done.1.refs_2_ = bf16[128,2560]{1,0:T(8,128)(2,1)} collective-permute-done((bf16[128,2560]{1,0:T(8,128)(2,1)S(1)}, bf16[128,2560]{1,0:T(8,128)(2,1)}, u32[]{:S(2)}, u32[]{:S(2)}) %collective-permute-start.1) | collective-permute-done | bytes 655392 | tf_op jit(solution)/shard_map/ppermute | solution.py:27
  59.9 1.2 collective-permute-start.7
  61.8 0.8 collective-permute-start.3
  62.6 2.6 %collective-permute-start.6 = (bf16[128,2560]{1,0:T(8,128)(2,1)}, bf16[128,2560]{1,0:T(8,128)(2,1)}, u32[]{:S(2)}, u32[]{:S(2)}) collective-permute-start(bf16[128,2560]{1,0:T(8,128)(2,1)} %collective-permute-done.2.refs_5_), channel_id=1, source_target_pairs={{0,192},{64,0},{128,64},{192,128},{1,193},{65,1},{129,65},{193,129... | collective-permute-start | bytes 1966088 | tf_op jit(solution)/shard_map/ppermute | solution.py:27
  65.9 1.0 copy-done.5
  66.9 3.6 %shard_map.102.refs_8_ = bf16[1024,1024]{1,0:T(8,128)(2,1)} custom-call(bf16[512,1024]{1,0:T(8,128)(2,1)} %bitcast.50, bf16[512,1024]{1,0:T(8,128)(2,1)} %copy-done.5), custom_call_target="tpu_custom_call" | custom-call | tf_op jit(solution)/shard_map/pallas_call | solution.py:45
  70.5 7.1 %collective-permute-done.4.refs_4_ = bf16[128,2560]{1,0:T(8,128)(2,1)} collective-permute-done((bf16[128,2560]{1,0:T(8,128)(2,1)S(1)}, bf16[128,2560]{1,0:T(8,128)(2,1)}, u32[]{:S(2)}, u32[]{:S(2)}) %collective-permute-start.4) | collective-permute-done | bytes 655392 | tf_op jit(solution)/shard_map/ppermute | solution.py:27
  77.5 1.7 collective-permute-done.3.refs_3_
  79.3 14.0 %collective-permute-done.5.refs_6_ = bf16[128,2560]{1,0:T(8,128)(2,1)} collective-permute-done((bf16[128,2560]{1,0:T(8,128)(2,1)}, bf16[128,2560]{1,0:T(8,128)(2,1)}, u32[]{:S(2)}, u32[]{:S(2)}) %collective-permute-start.5) | collective-permute-done | bytes 655392 | tf_op jit(solution)/shard_map/ppermute | solution.py:27
  93.3 11.5 %shard_map.103 = (bf16[8,4,2,16,2560]{4,3,2,1,0:T(8,128)(2,1)}, bf16[1024,2560]{1,0:T(8,128)(2,1)}) custom-call(s32[7]{0:T(128)} %concatenate.9.info, bf16[128,2560]{1,0:T(8,128)(2,1)} %copy-done.1, bf16[128,2560]{1,0:T(8,128)(2,1)} %collective-permute-done.refs_1_, bf16[128,2560]{1,0:T(8,128)(2,1)} %collective-permute-done.1.refs_2_, ...), custom_call_target="tpu_custom_call" | custom-call | flops 1048576 | bytes 1048576 | tf_op jit(solution)/shard_map/pallas_call | solution.py:82
  104.9 0.8 copy-done.11
  107.3 1.3 maximum_bitcast_fusion
  108.6 4.7 %all-to-all-start.1 = ((bf16[8,128,768]{2,1,0:T(8,128)(2,1)}), bf16[8,128,768]{2,1,0:T(8,128)(2,1)S(1)}, u32[]{:S(2)}, u32[]{:S(2)}) async-start(bf16[8,128,768]{2,1,0:T(8,128)(2,1)} %maximum_bitcast_fusion), calls=%async_computation.2 | async-start | bytes 3145728 | tf_op jit(solution)/shard_map/all_to_all | solution.py:310
  113.3 7.9 %shard_map.105 = bf16[1024,512]{1,0:T(8,128)(2,1)} custom-call(s32[7]{0:T(128)} %concatenate.9.info, bf16[1024,2560]{1,0:T(8,128)(2,1)} %get-tuple-element.31.rows, bf16[8,4,2,16,2560]{4,3,2,1,0:T(8,128)(2,1)} %bitcast.47), custom_call_target="tpu_custom_call" | custom-call | flops 1048576 | bytes 1048576 | tf_op jit(solution)/shard_map/pallas_call | solution.py:136
  121.4 7.8 %shard_map.104.mine = f32[1024,512]{1,0:T(8,128)} custom-call(s32[7]{0:T(128)} %concatenate.9.info, bf16[1024,2560]{1,0:T(8,128)(2,1)} %get-tuple-element.31.rows, bf16[8,4,2,16,2560]{4,3,2,1,0:T(8,128)(2,1)} %bitcast.48), custom_call_target="tpu_custom_call" | custom-call | flops 1048576 | bytes 1048576 | tf_op jit(solution)/shard_map/pallas_call | solution.py:136
  129.2 4.8 %all-to-all-done.1 = bf16[8,128,768]{2,1,0:T(8,128)(2,1)S(1)} async-done(((bf16[8,128,768]{2,1,0:T(8,128)(2,1)}), bf16[8,128,768]{2,1,0:T(8,128)(2,1)S(1)}, u32[]{:S(2)}, u32[]{:S(2)}) %all-to-all-start.1) | async-done | bytes 1572896 | tf_op jit(solution)/shard_map/all_to_all | solution.py:310
  134.0 1.1 copy-done.2
  135.5 16.8 %shard_map.106 = (bf16[2,128,768]{2,1,0:T(8,128)(2,1)}, bf16[2,128,768]{2,1,0:T(8,128)(2,1)}, bf16[2,128,768]{2,1,0:T(8,128)(2,1)}, bf16[2,128,768]{2,1,0:T(8,128)(2,1)}) custom-call(s32[7]{0:T(128)} %concatenate.9.info, bf16[1024,768]{1,0:T(8,128)(2,1)} %bitcast.52, bf16[1024,768]{1,0:T(8,128)(2,1)} %bitcast.53, bf16[1024,768]{1,0:T(8,128)(2,1)} %bitcast.54, ...), custom_call_target="tpu_custom_call" | custom-call | flops 14000000000 | bytes 8388608 | tf_op jit(solution)/shard_map/pallas_call | solution.py:224
  152.3 0.9 collective-permute-start.15
  153.2 1.3 collective-permute-start.14
  154.5 0.9 slice.52
  155.4 7.0 %collective-permute-done.15.refs_3_ = bf16[2,128,768]{2,1,0:T(8,128)(2,1)S(1)} collective-permute-done((bf16[2,128,768]{2,1,0:T(8,128)(2,1)}, bf16[2,128,768]{2,1,0:T(8,128)(2,1)S(1)}, u32[]{:S(2)}, u32[]{:S(2)}) %collective-permute-start.15) | collective-permute-done | bytes 393248 | tf_op jit(solution)/shard_map/ppermute | solution.py:27
  162.4 2.0 %collective-permute-done.14.refs_2_ = bf16[2,128,768]{2,1,0:T(8,128)(2,1)S(1)} collective-permute-done((bf16[2,128,768]{2,1,0:T(8,128)(2,1)}, bf16[2,128,768]{2,1,0:T(8,128)(2,1)S(1)}, u32[]{:S(2)}, u32[]{:S(2)}) %collective-permute-start.14) | collective-permute-done | bytes 393248 | tf_op jit(solution)/shard_map/ppermute | solution.py:27
  164.5 9.9 %collective-permute-done.13.refs_1_ = bf16[2,128,768]{2,1,0:T(8,128)(2,1)S(1)} collective-permute-done((bf16[2,128,768]{2,1,0:T(8,128)(2,1)}, bf16[2,128,768]{2,1,0:T(8,128)(2,1)S(1)}, u32[]{:S(2)}, u32[]{:S(2)}) %collective-permute-start.13) | collective-permute-done | bytes 393248 | tf_op jit(solution)/shard_map/ppermute | solution.py:27
  175.1 1.2 slice_bitcast_fusion
  176.4 1.5 collective-permute-start.17
  177.9 1.2 collective-permute-start.18
  179.1 0.9 copy-done.9
  180.0 2.8 %shard_map.107 = (bf16[128,4096]{1,0:T(8,128)(2,1)}, bf16[128,512]{1,0:T(8,128)(2,1)}, bf16[128,512]{1,0:T(8,128)(2,1)}) custom-call(s32[7]{0:T(128)} %concatenate.9.info, bf16[2,128,768]{2,1,0:T(8,128)(2,1)} %get-tuple-element.37.refs_0_, bf16[2,128,768]{2,1,0:T(8,128)(2,1)} %copy-done.8, bf16[2,128,768]{2,1,0:T(8,128)(2,1)} %copy-done.7, ...), custom_call_target="tpu_custom_call" | custom-call | tf_op jit(solution)/shard_map/pallas_call | solution.py:255
  182.8 2.5 %copy.19 = bf16[16,8,32,128]{3,2,1,0:T(8,128)(2,1)} copy(bf16[16,8,32,128]{3,1,2,0:T(8,128)(2,1)} %bitcast.59) | data formatting | bytes 2097152
  185.2 1.7 collective-permute-done.16
  187.3 1.2 collective-permute-start.20
  188.5 0.7 reshape.46
  189.2 0.7 reshape.47
  190.0 0.7 pad_maximum_fusion.2
  (71 shorter events, 6.7 us)
Async XLA Ops:
  7.2 10.3 %copy-start.3 = (bf16[1,128,32,128]{3,2,1,0:T(8,128)(2,1)S(1)}, bf16[1,128,32,128]{3,2,1,0:T(8,128)(2,1)}, u32[]{:S(2)}) copy-start(bf16[1,128,32,128]{3,2,1,0:T(8,128)(2,1)} %param.10) | copy-start | bytes 3145732
  7.2 106.1 %all-gather.3.cloned.1.call-start = ((), (), s32[]{:S(2)}) async-start(), calls=%async_computation.4 | async-start | bytes 5898240 | tf_op jit(solution)/shard_map/all_gather | solution.py:292
  8.3 4.3 %collective-permute-start.8 = (bf16[16,2560]{1,0:T(8,128)(2,1)S(1)}, bf16[16,2560]{1,0:T(8,128)(2,1)S(1)}, u32[]{:S(2)}, u32[]{:S(2)}) collective-permute-start(bf16[16,2560]{1,0:T(8,128)(2,1)S(1)} %get-tuple-element.59), channel_id=1, source_target_pairs={{0,32},{32,0},{1,33},{33,1},{2,34},{34,2},{3,35},{35,3},{4,36},{36... | collective-permute-start | bytes 245768 | tf_op jit(solution)/shard_map/ppermute | solution.py:35
  13.2 5.8 %collective-permute-start.11 = (bf16[2,16,2560]{2,1,0:T(8,128)(2,1)}, bf16[2,16,2560]{2,1,0:T(8,128)(2,1)S(1)}, u32[]{:S(2)}, u32[]{:S(2)}) collective-permute-start(bf16[2,16,2560]{2,1,0:T(8,128)(2,1)} %get-tuple-element.57), channel_id=1, source_target_pairs={{0,24},{8,0},{16,8},{24,16},{1,25},{9,1},{17,9},{25,17},{2,26},{10... | collective-permute-start | bytes 491528 | tf_op jit(solution)/shard_map/ppermute | solution.py:27
  14.2 6.9 %collective-permute-start.10 = (bf16[2,16,2560]{2,1,0:T(8,128)(2,1)}, bf16[2,16,2560]{2,1,0:T(8,128)(2,1)S(1)}, u32[]{:S(2)}, u32[]{:S(2)}) collective-permute-start(bf16[2,16,2560]{2,1,0:T(8,128)(2,1)} %get-tuple-element.57), channel_id=1, source_target_pairs={{0,16},{8,24},{16,0},{24,8},{1,17},{9,25},{17,1},{25,9},{2,18},{10... | collective-permute-start | bytes 491528 | tf_op jit(solution)/shard_map/ppermute | solution.py:27
  14.5 11.0 %collective-permute-start.9 = (bf16[2,16,2560]{2,1,0:T(8,128)(2,1)}, bf16[2,16,2560]{2,1,0:T(8,128)(2,1)S(1)}, u32[]{:S(2)}, u32[]{:S(2)}) collective-permute-start(bf16[2,16,2560]{2,1,0:T(8,128)(2,1)} %get-tuple-element.57), channel_id=1, source_target_pairs={{0,8},{8,16},{16,24},{24,0},{1,9},{9,17},{17,25},{25,1},{2,10},{10... | collective-permute-start | bytes 491528 | tf_op jit(solution)/shard_map/ppermute | solution.py:27
  17.4 43.7 %copy-start.1 = (bf16[128,2560]{1,0:T(8,128)(2,1)}, bf16[128,2560]{1,0:T(8,128)(2,1)S(1)}, u32[]{:S(2)}) copy-start(bf16[128,2560]{1,0:T(8,128)(2,1)S(1)} %get-tuple-element.49.refs_0_) | copy-start | bytes 1966084
  17.7 8.8 %copy-start.10 = (bf16[128,2560]{1,0:T(8,128)(2,1)S(1)}, bf16[128,2560]{1,0:T(8,128)(2,1)}, u32[]{:S(2)}) copy-start(bf16[128,2560]{1,0:T(8,128)(2,1)} %get-tuple-element.48) | copy-start | bytes 1966084
  19.0 46.3 %copy-start.15 = (s32[1,3]{1,0:T(1,128)S(1)}, s32[1,3]{1,0:T(1,128)}, u32[]{:S(2)}) copy-start(s32[1,3]{1,0:T(1,128)} %param.13) | copy-start | bytes 40
  26.5 6.1 %collective-permute-start = (bf16[128,2560]{1,0:T(8,128)(2,1)S(1)}, bf16[128,2560]{1,0:T(8,128)(2,1)}, u32[]{:S(2)}, u32[]{:S(2)}) collective-permute-start(bf16[128,2560]{1,0:T(8,128)(2,1)S(1)} %copy-done.10), channel_id=1, source_target_pairs={{0,32},{32,0},{1,33},{33,1},{2,34},{34,2},{3,35},{35,3},{4,36},{36... | collective-permute-start | bytes 1966088 | tf_op jit(solution)/shard_map/ppermute | solution.py:35
  27.1 32.8 %all-to-all-start = ((bf16[4,128,1024]{2,1,0:T(8,128)(2,1)}), bf16[4,128,1024]{2,1,0:T(8,128)(2,1)S(1)}, u32[]{:S(2)}, u32[]{:S(2)}) async-start(bf16[4,128,1024]{2,1,0:T(8,128)(2,1)} %bitcast.46), calls=%async_computation | async-start | bytes 2097152 | tf_op jit(solution)/shard_map/all_to_all | solution.py:293
  31.1 144.0 %reduce-scatter.2.cloned.1.call-start = ((), (), s32[]{:S(2)}) async-start(), calls=%async_computation.3 | async-start | bytes 5898240 | tf_op jit(solution)/shard_map/reduce_scatter | solution.py:317
  31.1 28.8 %collective-permute-start.1 = (bf16[128,2560]{1,0:T(8,128)(2,1)S(1)}, bf16[128,2560]{1,0:T(8,128)(2,1)}, u32[]{:S(2)}, u32[]{:S(2)}) collective-permute-start(bf16[128,2560]{1,0:T(8,128)(2,1)S(1)} %get-tuple-element.49.refs_0_), channel_id=1, source_target_pairs={{0,64},{64,128},{128,192},{192,0},{1,65},{65,129},{129,193},{193,1... | collective-permute-start | bytes 1966088 | tf_op jit(solution)/shard_map/ppermute | solution.py:27
  32.6 27.3 %collective-permute-start.2 = (bf16[128,2560]{1,0:T(8,128)(2,1)}, bf16[128,2560]{1,0:T(8,128)(2,1)}, u32[]{:S(2)}, u32[]{:S(2)}) collective-permute-start(bf16[128,2560]{1,0:T(8,128)(2,1)} %collective-permute-done.refs_1_), channel_id=1, source_target_pairs={{0,192},{64,0},{128,64},{192,128},{1,193},{65,1},{129,65},{193,129... | collective-permute-start | bytes 1966088 | tf_op jit(solution)/shard_map/ppermute | solution.py:27
  59.9 6.0 %copy-start = (bf16[4,128,1024]{2,1,0:T(8,128)(2,1)}, bf16[4,128,1024]{2,1,0:T(8,128)(2,1)S(1)}, u32[]{:S(2)}) copy-start(bf16[4,128,1024]{2,1,0:T(8,128)(2,1)S(1)} %all-to-all-done) | copy-start | bytes 3145732
  59.9 6.0 %collective-permute-start.7 = (bf16[512,1024]{1,0:T(8,128)(2,1)S(1)}, bf16[512,1024]{1,0:T(8,128)(2,1)S(1)}, u32[]{:S(2)}, u32[]{:S(2)}) collective-permute-start(bf16[512,1024]{1,0:T(8,128)(2,1)S(1)} %bitcast.49), channel_id=1, source_target_pairs={{0,32},{32,0},{1,33},{33,1},{2,34},{34,2},{3,35},{35,3},{4,36},{36... | collective-permute-start | bytes 3145736 | tf_op jit(solution)/shard_map/ppermute | solution.py:35
  61.1 16.4 %collective-permute-start.4 = (bf16[128,2560]{1,0:T(8,128)(2,1)S(1)}, bf16[128,2560]{1,0:T(8,128)(2,1)}, u32[]{:S(2)}, u32[]{:S(2)}) collective-permute-start(bf16[128,2560]{1,0:T(8,128)(2,1)S(1)} %get-tuple-element.49.refs_0_), channel_id=1, source_target_pairs={{0,192},{64,0},{128,64},{192,128},{1,193},{65,1},{129,65},{193,129... | collective-permute-start | bytes 1966088 | tf_op jit(solution)/shard_map/ppermute | solution.py:27
  61.8 17.5 %collective-permute-start.3 = (bf16[128,2560]{1,0:T(8,128)(2,1)}, bf16[128,2560]{1,0:T(8,128)(2,1)}, u32[]{:S(2)}, u32[]{:S(2)}) collective-permute-start(bf16[128,2560]{1,0:T(8,128)(2,1)} %collective-permute-done.refs_1_), channel_id=1, source_target_pairs={{0,64},{64,128},{128,192},{192,0},{1,65},{65,129},{129,193},{193,1... | collective-permute-start | bytes 1966088 | tf_op jit(solution)/shard_map/ppermute | solution.py:27
  62.6 30.7 %collective-permute-start.5 = (bf16[128,2560]{1,0:T(8,128)(2,1)}, bf16[128,2560]{1,0:T(8,128)(2,1)}, u32[]{:S(2)}, u32[]{:S(2)}) collective-permute-start(bf16[128,2560]{1,0:T(8,128)(2,1)} %collective-permute-done.1.refs_2_), channel_id=1, source_target_pairs={{0,64},{64,128},{128,192},{192,0},{1,65},{65,129},{129,193},{193,1... | collective-permute-start | bytes 1966088 | tf_op jit(solution)/shard_map/ppermute | solution.py:27
  62.6 30.7 %collective-permute-start.6 = (bf16[128,2560]{1,0:T(8,128)(2,1)}, bf16[128,2560]{1,0:T(8,128)(2,1)}, u32[]{:S(2)}, u32[]{:S(2)}) collective-permute-start(bf16[128,2560]{1,0:T(8,128)(2,1)} %collective-permute-done.2.refs_5_), channel_id=1, source_target_pairs={{0,192},{64,0},{128,64},{192,128},{1,193},{65,1},{129,65},{193,129... | collective-permute-start | bytes 1966088 | tf_op jit(solution)/shard_map/ppermute | solution.py:27
  65.9 1.0 copy-start.5
  104.8 0.9 copy-start.11
  104.8 1.0 copy-start.12
  104.8 1.4 copy-start.4
  108.6 25.4 %all-to-all-start.1 = ((bf16[8,128,768]{2,1,0:T(8,128)(2,1)}), bf16[8,128,768]{2,1,0:T(8,128)(2,1)S(1)}, u32[]{:S(2)}, u32[]{:S(2)}) async-start(bf16[8,128,768]{2,1,0:T(8,128)(2,1)} %maximum_bitcast_fusion), calls=%async_computation.2 | async-start | bytes 3145728 | tf_op jit(solution)/shard_map/all_to_all | solution.py:310
  121.1 12.9 %collective-permute-start.12 = (bf16[1024,512]{1,0:T(8,128)(2,1)}, bf16[1024,512]{1,0:T(8,128)(2,1)S(1)}, u32[]{:S(2)}, u32[]{:S(2)}) collective-permute-start(bf16[1024,512]{1,0:T(8,128)(2,1)} %shard_map.105), channel_id=1, source_target_pairs={{0,32},{32,0},{1,33},{33,1},{2,34},{34,2},{3,35},{35,3},{4,36},{36... | collective-permute-start | bytes 3145736 | tf_op jit(solution)/shard_map/ppermute | solution.py:35
  134.0 1.2 copy-start.2
  134.0 1.5 copy-start.16
  152.3 10.1 %collective-permute-start.15 = (bf16[2,128,768]{2,1,0:T(8,128)(2,1)}, bf16[2,128,768]{2,1,0:T(8,128)(2,1)S(1)}, u32[]{:S(2)}, u32[]{:S(2)}) collective-permute-start(bf16[2,128,768]{2,1,0:T(8,128)(2,1)} %get-tuple-element.35), channel_id=1, source_target_pairs={{0,192},{64,0},{128,64},{192,128},{1,193},{65,1},{129,65},{193,129... | collective-permute-start | bytes 1179656 | tf_op jit(solution)/shard_map/ppermute | solution.py:27
  153.2 11.2 %collective-permute-start.14 = (bf16[2,128,768]{2,1,0:T(8,128)(2,1)}, bf16[2,128,768]{2,1,0:T(8,128)(2,1)S(1)}, u32[]{:S(2)}, u32[]{:S(2)}) collective-permute-start(bf16[2,128,768]{2,1,0:T(8,128)(2,1)} %get-tuple-element.34), channel_id=1, source_target_pairs={{0,128},{64,192},{128,0},{192,64},{1,129},{65,193},{129,1},{193,65... | collective-permute-start | bytes 1179656 | tf_op jit(solution)/shard_map/ppermute | solution.py:27
  154.5 19.9 %collective-permute-start.13 = (bf16[2,128,768]{2,1,0:T(8,128)(2,1)}, bf16[2,128,768]{2,1,0:T(8,128)(2,1)S(1)}, u32[]{:S(2)}, u32[]{:S(2)}) collective-permute-start(bf16[2,128,768]{2,1,0:T(8,128)(2,1)} %get-tuple-element.33), channel_id=1, source_target_pairs={{0,64},{64,128},{128,192},{192,0},{1,65},{65,129},{129,193},{193,1... | collective-permute-start | bytes 1179656 | tf_op jit(solution)/shard_map/ppermute | solution.py:27
  162.4 16.7 %copy-start.6 = (bf16[2,128,768]{2,1,0:T(8,128)(2,1)}, bf16[2,128,768]{2,1,0:T(8,128)(2,1)S(1)}, u32[]{:S(2)}) copy-start(bf16[2,128,768]{2,1,0:T(8,128)(2,1)S(1)} %collective-permute-done.15.refs_3_) | copy-start | bytes 1179652
  164.4 14.6 %copy-start.7 = (bf16[2,128,768]{2,1,0:T(8,128)(2,1)}, bf16[2,128,768]{2,1,0:T(8,128)(2,1)S(1)}, u32[]{:S(2)}) copy-start(bf16[2,128,768]{2,1,0:T(8,128)(2,1)S(1)} %collective-permute-done.14.refs_2_) | copy-start | bytes 1179652
  174.4 4.7 %copy-start.8 = (bf16[2,128,768]{2,1,0:T(8,128)(2,1)}, bf16[2,128,768]{2,1,0:T(8,128)(2,1)S(1)}, u32[]{:S(2)}) copy-start(bf16[2,128,768]{2,1,0:T(8,128)(2,1)S(1)} %collective-permute-done.13.refs_1_) | copy-start | bytes 1179652
  174.5 4.5 %collective-permute-start.19 = (bf16[4,128,768]{2,1,0:T(8,128)(2,1)S(1)}, bf16[4,128,768]{2,1,0:T(8,128)(2,1)S(1)}, u32[]{:S(2)}, u32[]{:S(2)}) collective-permute-start(bf16[4,128,768]{2,1,0:T(8,128)(2,1)S(1)} %pad_maximum_fusion), channel_id=1, source_target_pairs={{0,32},{32,0},{1,33},{33,1},{2,34},{34,2},{3,35},{35,3},{4,36},{36... | collective-permute-start | bytes 2359304 | tf_op jit(solution)/shard_map/ppermute | solution.py:35
  176.3 10.6 %collective-permute-start.16 = (bf16[2,16,2560]{2,1,0:T(8,128)(2,1)S(1)}, bf16[2,16,2560]{2,1,0:T(8,128)(2,1)S(1)}, u32[]{:S(2)}, u32[]{:S(2)}) collective-permute-start(bf16[2,16,2560]{2,1,0:T(8,128)(2,1)S(1)} %get-tuple-element.52), channel_id=1, source_target_pairs={{0,8},{8,16},{16,24},{24,0},{1,9},{9,17},{17,25},{25,1},{2,10},{10... | collective-permute-start | bytes 491528 | tf_op jit(solution)/shard_map/ppermute | solution.py:27
  176.4 10.5 %collective-permute-start.17 = (bf16[2,16,2560]{2,1,0:T(8,128)(2,1)S(1)}, bf16[2,16,2560]{2,1,0:T(8,128)(2,1)S(1)}, u32[]{:S(2)}, u32[]{:S(2)}) collective-permute-start(bf16[2,16,2560]{2,1,0:T(8,128)(2,1)S(1)} %get-tuple-element.51), channel_id=1, source_target_pairs={{0,16},{8,24},{16,0},{24,8},{1,17},{9,25},{17,1},{25,9},{2,18},{10... | collective-permute-start | bytes 491528 | tf_op jit(solution)/shard_map/ppermute | solution.py:27
  177.9 9.3 %collective-permute-start.18 = (bf16[2,16,2560]{2,1,0:T(8,128)(2,1)S(1)}, bf16[2,16,2560]{2,1,0:T(8,128)(2,1)S(1)}, u32[]{:S(2)}, u32[]{:S(2)}) collective-permute-start(bf16[2,16,2560]{2,1,0:T(8,128)(2,1)S(1)} %get-tuple-element.50), channel_id=1, source_target_pairs={{0,24},{8,0},{16,8},{24,16},{1,25},{9,1},{17,9},{25,17},{2,26},{10... | collective-permute-start | bytes 491528 | tf_op jit(solution)/shard_map/ppermute | solution.py:27
  179.1 0.9 copy-start.9
  182.7 5.8 %copy-start.14 = (bf16[128,512]{1,0:T(8,128)(2,1)S(1)}, bf16[128,512]{1,0:T(8,128)(2,1)}, u32[]{:S(2)}) copy-start(bf16[128,512]{1,0:T(8,128)(2,1)} %get-tuple-element.42) | copy-start | bytes 393220
  182.7 6.5 %copy-start.13 = (bf16[128,512]{1,0:T(8,128)(2,1)S(1)}, bf16[128,512]{1,0:T(8,128)(2,1)}, u32[]{:S(2)}) copy-start(bf16[128,512]{1,0:T(8,128)(2,1)} %get-tuple-element.43) | copy-start | bytes 393220
  187.3 2.6 %collective-permute-start.20 = (f32[16,2560]{1,0:T(8,128)S(1)}, f32[16,2560]{1,0:T(8,128)S(1)}, u32[]{:S(2)}, u32[]{:S(2)}) collective-permute-start(f32[16,2560]{1,0:T(8,128)S(1)} %select_bitcast_fusion), channel_id=1, source_target_pairs={{0,32},{32,0},{1,33},{33,1},{2,34},{34,2},{3,35},{35,3},{4,36},{36... | collective-permute-start | bytes 491528 | tf_op jit(solution)/shard_map/ppermute | solution.py:35
Sparse Core Ops, SparseCore 0:
  26.6 64.8 all-gather.2
  105.0 63.7 reduce-scatter.1
